TPU v7x, 32 devices: a whole 2x2x4 slice. The times are simulated.
32 devices in a mesh: bucket: 8 (over y, x, core), seq: 4 (over z).
Axes of the slice: x: 2, y: 2, z: 4, core: 2. Of those that a mesh axis runs over, the one named last changes fastest.
Arguments:
- tokens: bfloat16 [8192, 1536], P(('bucket', 'seq')), may hold values from -6 to 6
- condition: float32 [32, 1536], P('bucket'), may hold values from -6 to 6
- captions: bfloat16 [32, 256, 4096], P('bucket', 'seq'), may hold values from -6 to 6
- caption_lengths: int32 [32], P('bucket'), may hold values from 1 to 256, as said below
- null_flags: int32 [32], P('bucket'), may hold values 0 or 1
- slot_buckets: int32 [8], P('bucket'), may hold values from 0 to 2, as said below
- null_caption: bfloat16 [256, 4096], replicated, may hold values from -6 to 6
- modulation: bfloat16 [1536, 6144], P('bucket'), may hold values from -0.15625 to 0.15625
- projection: bfloat16 [1536, 4608], P('bucket'), may hold values from -0.15625 to 0.15625
- text_weight: bfloat16 [4096, 3072], P('bucket'), may hold values from -0.09375 to 0.09375
- output_weight: bfloat16 [1536, 1536], P('bucket'), may hold values from -0.15625 to 0.15625
- gate_up: bfloat16 [1536, 8192], P('bucket'), may hold values from -0.15625 to 0.15625
- down_weight: bfloat16 [4096, 1536], P('bucket'), may hold values from -0.09375 to 0.09375
- norm_gains: float32 [4, 1536], replicated, may hold values from 0.25 to 1.75
- head_gains: float32 [3, 1536], replicated, may hold values from 0.25 to 1.75
- cross_gates: float32 [24], replicated, may hold values from -1.5 to 1.5
- cotangent: bfloat16 [8192, 1536], P(('bucket', 'seq')), may hold values from -6 to 6
Outputs:
- mixed: bfloat16 [8192, 1536], P(('bucket', 'seq'))
- grad_tokens: float32 [8192, 1536], P(('bucket', 'seq'))
- grad_captions: float32 [32, 256, 4096], P('bucket', 'seq')
- grad_null: float32 [256, 4096], P(('bucket', 'seq'))
- grad_modulation: float32 [1536, 6144], P(('bucket', 'seq'))
- grad_projection: float32 [1536, 4608], P(('bucket', 'seq'))
- grad_text_weight: float32 [4096, 3072], P(('bucket', 'seq'))
- grad_output_weight: float32 [1536, 1536], P(('bucket', 'seq'))
- grad_gate_up: float32 [1536, 8192], P(('bucket', 'seq'))
- grad_down_weight: float32 [4096, 1536], P(('bucket', 'seq'))
- grad_norm_gains: float32 [4, 1536], P(None, ('bucket', 'seq'))
- grad_head_gains: float32 [3, 1536], P(None, ('bucket', 'seq'))
- grad_cross_gates: float32 [24], replicated
Inputs may be any that keep to these rules, and one draw needn't show every extreme that they name: `slot_buckets`: A slot of bucket u holds 4 / 2**u clips; about four sevenths of the slots are of bucket 2, two sevenths of bucket 1, the rest of bucket 0, and every bucket has a slot. `caption_lengths`: only the first 4 / 2**u clip places of a slot of bucket u are read. In every draw the first clip place of some slot has length 256.
All inputs are finite; a program needn't handle non-finite values. No bound on the sum of `null_flags` on one device may be relied on, other than what follows from the above.
Results may differ from a plain program's by a relative error of at most 0.017.
Values may be sent and summed in bfloat16 or wider, within the bound.
A program may use at most 576 MiB of HBM per device.

v0:
```python
from functools import partial

import jax
import jax.numpy as jnp
from jax import lax
from jax.sharding import PartitionSpec as P

EPSILON = 1e-06
NEGATIVE = -1e30
HIGHEST = lax.Precision.HIGHEST


def rms_norm(values, norm_gain):
    return (
        values * lax.rsqrt(jnp.mean(values * values, axis=-1, keepdims=True) + EPSILON) * norm_gain
    )


def rotate(values, angles):
    count = values.shape[0]
    half = angles.shape[1]
    shaped = values.reshape(count, -1, 2 * half)
    first_half = shaped[..., :half]
    second_half = shaped[..., half:]
    cosine = jnp.cos(angles)[:, None, :]
    sine = jnp.sin(angles)[:, None, :]
    turned = jnp.concatenate(
        [first_half * cosine - second_half * sine, first_half * sine + second_half * cosine],
        axis=-1,
    )
    return turned.reshape(count, -1)


def dense(leading, trailing):
    return jnp.dot(leading, trailing, preferred_element_type=jnp.float32)


def contract_rows(leading, trailing):
    return lax.dot_general(
        leading, trailing, (((0,), (0,)), ((), ())), preferred_element_type=jnp.float32
    )


def contract_cols(leading, trailing):
    return lax.dot_general(
        leading, trailing, (((1,), (1,)), ((), ())), preferred_element_type=jnp.float32
    )


def forward_product(leading, weight_shard):
    return dense(leading, lax.all_gather(weight_shard, "bucket", axis=0, tiled=True))


def backward_product(upstream, weight_shard):
    return contract_cols(upstream, lax.all_gather(weight_shard, "bucket", axis=0, tiled=True))


def pre_attention(tokens_in, modulated, norm_gains):
    model_width = tokens_in.shape[1]
    return rms_norm(tokens_in, norm_gains[0]) * (1.0 + modulated[:, :model_width])


def project_heads(projected, head_gains, angles):
    model_width = projected.shape[1] // 3
    query_norm = rms_norm(projected[:, :model_width], head_gains[0])
    key_norm = rms_norm(projected[:, model_width : 2 * model_width], head_gains[1])
    return (
        rotate(query_norm, angles),
        rotate(key_norm, angles),
        projected[:, 2 * model_width :],
        query_norm,
    )


def text_heads(text_pairs, head_gains):
    model_width = text_pairs.shape[1] // 2
    return (rms_norm(text_pairs[:, :model_width], head_gains[2]), text_pairs[:, model_width:])


def post_attention(attended, tokens_in, modulated, norm_gains):
    model_width = tokens_in.shape[1]
    middle = tokens_in + jnp.tanh(modulated[:, model_width : 2 * model_width]) * rms_norm(
        attended, norm_gains[1]
    )
    normed_ffn = rms_norm(middle, norm_gains[2]) * (
        1.0 + modulated[:, 2 * model_width : 3 * model_width]
    )
    return (middle, normed_ffn)


def swiglu(gate_values):
    hidden_width = gate_values.shape[1] // 2
    return jax.nn.silu(gate_values[:, :hidden_width]) * gate_values[:, hidden_width:]


def finish(lowered, middle, modulated, norm_gains):
    model_width = middle.shape[1]
    return middle + jnp.tanh(modulated[:, 3 * model_width :]) * rms_norm(lowered, norm_gains[3])


def split_heads(values, head_count):
    count = values.shape[0]
    head_size = values.shape[1] // head_count
    group = 4
    return values.reshape(count, head_count // group, group, head_size).transpose(1, 2, 0, 3)


def join_heads(values):
    blocks, group, count, head_size = values.shape
    return values.transpose(2, 0, 1, 3).reshape(count, blocks * group * head_size)


def attend(queries, keys, values, allowed, head_count):
    scaling = (queries.shape[1] // head_count) ** (-0.5)

    def group_step(operands):
        query_group, key_group, value_group = operands
        scores = (
            jnp.einsum("hqd,hkd->hqk", query_group, key_group, preferred_element_type=jnp.float32)
            * scaling
        )
        scores = jnp.where(allowed[None], scores, NEGATIVE)
        row_max = jnp.max(scores, axis=-1, keepdims=True)
        log_total = row_max + jnp.log(jnp.sum(jnp.exp(scores - row_max), axis=-1, keepdims=True))
        shares = jnp.exp(scores - log_total).astype(jnp.bfloat16)
        return (
            jnp.einsum("hqk,hkd->hqd", shares, value_group, preferred_element_type=jnp.float32),
            log_total,
        )

    result, log_total = lax.map(
        group_step,
        (
            split_heads(queries, head_count),
            split_heads(keys, head_count),
            split_heads(values, head_count),
        ),
    )
    return (join_heads(result), log_total)


def attend_back(queries, keys, values, allowed, log_total, upstream, head_count):
    scaling = (queries.shape[1] // head_count) ** (-0.5)

    def group_step(operands):
        query_group, key_group, value_group, total_group, upstream_group = operands
        scores = (
            jnp.einsum("hqd,hkd->hqk", query_group, key_group, preferred_element_type=jnp.float32)
            * scaling
        )
        scores = jnp.where(allowed[None], scores, NEGATIVE)
        shares = jnp.exp(scores - total_group)
        grad_value = jnp.einsum(
            "hqk,hqd->hkd",
            shares.astype(jnp.bfloat16),
            upstream_group,
            preferred_element_type=jnp.float32,
        )
        grad_shares = jnp.einsum(
            "hqd,hkd->hqk", upstream_group, value_group, preferred_element_type=jnp.float32
        )
        grad_scores = (
            shares * (grad_shares - jnp.sum(grad_shares * shares, axis=-1, keepdims=True))
        ).astype(jnp.bfloat16)
        grad_query = (
            jnp.einsum("hqk,hkd->hqd", grad_scores, key_group, preferred_element_type=jnp.float32)
            * scaling
        )
        grad_key = (
            jnp.einsum("hqk,hqd->hkd", grad_scores, query_group, preferred_element_type=jnp.float32)
            * scaling
        )
        return (grad_query, grad_key, grad_value)

    grad_query, grad_key, grad_value = lax.map(
        group_step,
        (
            split_heads(queries, head_count),
            split_heads(keys, head_count),
            split_heads(values, head_count),
            log_total,
            split_heads(upstream, head_count),
        ),
    )
    return (join_heads(grad_query), join_heads(grad_key), join_heads(grad_value))


def per_device(
    tokens,
    condition,
    captions,
    caption_lengths,
    null_flags,
    slot_buckets,
    null_caption,
    modulation,
    projection,
    text_weight,
    output_weight,
    gate_up,
    down_weight,
    norm_gains,
    head_gains,
    cross_gates,
    cotangent,
):
    wide = jnp.float32
    narrow = jnp.bfloat16
    local_rows, model_width = tokens.shape
    head_count = cross_gates.shape[0]
    head_size = model_width // head_count
    seq_count = lax.axis_size("seq")
    seq_index = lax.axis_index("seq")
    slot_rows = local_rows * seq_count
    clip_count, caption_rows, text_width = captions.shape
    caption_total = caption_rows * seq_count
    bucket = slot_buckets[0]
    clip_length = jnp.where(
        bucket == 0, slot_rows // 4, jnp.where(bucket == 1, slot_rows // 2, slot_rows)
    ).astype(jnp.int32)
    positions = seq_index * local_rows + jnp.arange(local_rows, dtype=jnp.int32)
    clip = positions // clip_length
    inside = positions - clip * clip_length
    key_clip = jnp.arange(slot_rows, dtype=jnp.int32) // clip_length
    half = head_size // 2
    frequency = 10000.0 ** (-jnp.arange(half, dtype=wide) / half)
    angles = inside.astype(wide)[:, None] * frequency[None, :]
    choose = (clip[:, None] == jnp.arange(clip_count, dtype=jnp.int32)[None, :]).astype(wide)
    caption_index = jnp.arange(clip_count * caption_total, dtype=jnp.int32)
    caption_clip = caption_index // caption_total
    caption_live = caption_index - caption_clip * caption_total < jnp.repeat(
        caption_lengths, caption_total
    )
    self_allowed = clip[:, None] == key_clip[None, :]
    cross_allowed = (clip[:, None] == caption_clip[None, :]) & caption_live[None, :]
    tokens_in = tokens.astype(wide)
    silu_cond = jax.nn.silu(condition).astype(narrow)
    modulated = jnp.dot(choose, forward_product(silu_cond, modulation), precision=HIGHEST)
    normed_full, pre_pull = jax.vjp(pre_attention, tokens_in, modulated, norm_gains)
    normed = normed_full.astype(narrow)
    projected = forward_product(normed, projection)
    head_outs, head_pull = jax.vjp(partial(project_heads, angles=angles), projected, head_gains)
    query_rot = head_outs[0].astype(narrow)
    query_cross = head_outs[3].astype(narrow)
    local_pairs = jnp.concatenate(
        [head_outs[1].astype(narrow), head_outs[2].astype(narrow)], axis=1
    )
    slot_pairs = lax.all_gather(local_pairs, "seq", axis=0, tiled=True)
    slot_keys = slot_pairs[:, :model_width]
    slot_values = slot_pairs[:, model_width:]
    null_rows = lax.dynamic_slice_in_dim(null_caption, seq_index * caption_rows, caption_rows, 0)
    is_null = null_flags[:, None, None] == 1
    words = jnp.where(is_null, null_rows[None], captions).reshape(
        clip_count * caption_rows, text_width
    )
    text_pairs = forward_product(words, text_weight)
    text_outs, text_pull = jax.vjp(text_heads, text_pairs, head_gains)
    local_text = jnp.concatenate(
        [text_outs[0].astype(narrow), text_outs[1].astype(narrow)], axis=1
    ).reshape(clip_count, caption_rows, 2 * model_width)
    slot_text = lax.all_gather(local_text, "seq", axis=1, tiled=True).reshape(
        clip_count * caption_total, 2 * model_width
    )
    text_keys = slot_text[:, :model_width]
    text_values = slot_text[:, model_width:]
    self_out, self_total = attend(query_rot, slot_keys, slot_values, self_allowed, head_count)
    cross_out, cross_total = attend(query_cross, text_keys, text_values, cross_allowed, head_count)
    tanh_gates = jnp.tanh(cross_gates)
    gate_columns = jnp.repeat(tanh_gates, head_size)
    combined = (self_out + gate_columns * cross_out).astype(narrow)
    attended = forward_product(combined, output_weight)
    (middle, ffn_full), post_pull = jax.vjp(
        post_attention, attended, tokens_in, modulated, norm_gains
    )
    normed_ffn = ffn_full.astype(narrow)
    gate_values = forward_product(normed_ffn, gate_up)
    hidden_full, swiglu_pull = jax.vjp(swiglu, gate_values)
    hidden = hidden_full.astype(narrow)
    lowered = forward_product(hidden, down_weight)
    mixed, finish_pull = jax.vjp(finish, lowered, middle, modulated, norm_gains)
    grad_lowered, grad_middle, grad_modulated_last, grad_norm_last = finish_pull(
        cotangent.astype(wide)
    )
    grad_lowered_low = grad_lowered.astype(narrow)
    grad_down_local = contract_rows(hidden, grad_lowered_low)
    grad_hidden = backward_product(grad_lowered_low, down_weight)
    (grad_gate_values,) = swiglu_pull(grad_hidden)
    grad_gate_low = grad_gate_values.astype(narrow)
    grad_gate_local = contract_rows(normed_ffn, grad_gate_low)
    grad_normed_ffn = backward_product(grad_gate_low, gate_up)
    gate_share, down_share = (
        lax.psum_scatter(grad_gate_local, ("bucket", "seq"), scatter_dimension=0, tiled=True),
        lax.psum_scatter(grad_down_local, ("bucket", "seq"), scatter_dimension=0, tiled=True),
    )
    grad_attended, grad_tokens_post, grad_modulated_post, grad_norm_post = post_pull(
        (grad_middle, grad_normed_ffn)
    )
    grad_attended_low = grad_attended.astype(narrow)
    grad_output_local = contract_rows(combined, grad_attended_low)
    grad_combined = backward_product(grad_attended_low, output_weight)
    grad_gates_local = jnp.sum(
        (grad_combined * cross_out).reshape(local_rows, head_count, head_size), axis=(0, 2)
    ) * (1.0 - tanh_gates * tanh_gates)
    grad_query_self, grad_keys_slot, grad_values_slot = attend_back(
        query_rot,
        slot_keys,
        slot_values,
        self_allowed,
        self_total,
        grad_combined.astype(narrow),
        head_count,
    )
    grad_query_cross, grad_keys_text, grad_values_text = attend_back(
        query_cross,
        text_keys,
        text_values,
        cross_allowed,
        cross_total,
        (gate_columns * grad_combined).astype(narrow),
        head_count,
    )
    grad_pairs = lax.psum_scatter(
        jnp.concatenate([grad_keys_slot, grad_values_slot], axis=1).astype(jnp.bfloat16),
        "seq",
        scatter_dimension=0,
        tiled=True,
    ).astype(jnp.float32)
    grad_text_pairs = (
        lax.psum_scatter(
            jnp.concatenate([grad_keys_text, grad_values_text], axis=1)
            .reshape(clip_count, caption_total, 2 * model_width)
            .astype(jnp.bfloat16),
            "seq",
            scatter_dimension=1,
            tiled=True,
        )
        .astype(jnp.float32)
        .reshape(clip_count * caption_rows, 2 * model_width)
    )
    grad_text_full, grad_head_text = text_pull(
        (grad_text_pairs[:, :model_width], grad_text_pairs[:, model_width:])
    )
    grad_text_low = grad_text_full.astype(narrow)
    grad_text_local = contract_rows(words, grad_text_low)
    grad_words = backward_product(grad_text_low, text_weight).reshape(
        clip_count, caption_rows, text_width
    )
    grad_captions = jnp.where(is_null, 0.0, grad_words)
    null_local = jnp.sum(jnp.where(is_null, grad_words, 0.0), axis=0)
    grad_null_local = lax.dynamic_update_slice_in_dim(
        jnp.zeros(null_caption.shape, wide), null_local, seq_index * caption_rows, 0
    )
    grad_projected, grad_head_proj = head_pull(
        (
            grad_query_self,
            grad_pairs[:, :model_width],
            grad_pairs[:, model_width:],
            grad_query_cross,
        )
    )
    grad_projected_low = grad_projected.astype(narrow)
    grad_projection_local = contract_rows(normed, grad_projected_low)
    grad_normed = backward_product(grad_projected_low, projection)
    grad_tokens_pre, grad_modulated_pre, grad_norm_pre = pre_pull(grad_normed)
    grad_modulated = grad_modulated_pre + grad_modulated_post + grad_modulated_last
    grad_clip_rows = jnp.dot(choose.T, grad_modulated, precision=HIGHEST)
    grad_modulation_local = jnp.dot(silu_cond.astype(wide).T, grad_clip_rows, precision=HIGHEST)
    grad_tokens = grad_tokens_pre + grad_tokens_post
    grad_norm_local = grad_norm_pre + grad_norm_post + grad_norm_last
    grad_head_local = grad_head_proj + grad_head_text
    mod_share, proj_share, text_share, output_share, null_share, norm_share, head_share = (
        lax.psum_scatter(grad_modulation_local, ("bucket", "seq"), scatter_dimension=0, tiled=True),
        lax.psum_scatter(grad_projection_local, ("bucket", "seq"), scatter_dimension=0, tiled=True),
        lax.psum_scatter(grad_text_local, ("bucket", "seq"), scatter_dimension=0, tiled=True),
        lax.psum_scatter(grad_output_local, ("bucket", "seq"), scatter_dimension=0, tiled=True),
        lax.psum_scatter(grad_null_local, ("bucket", "seq"), scatter_dimension=0, tiled=True),
        lax.psum_scatter(grad_norm_local.T, ("bucket", "seq"), scatter_dimension=0, tiled=True),
        lax.psum_scatter(grad_head_local.T, ("bucket", "seq"), scatter_dimension=0, tiled=True),
    )
    grad_cross_gates = lax.psum(grad_gates_local, ("bucket", "seq"))
    return (
        mixed.astype(narrow),
        grad_tokens,
        grad_captions,
        null_share,
        mod_share,
        proj_share,
        text_share,
        output_share,
        gate_share,
        down_share,
        norm_share.T,
        head_share.T,
        grad_cross_gates,
    )


def solution(mesh):
    return jax.shard_map(
        per_device,
        mesh=mesh,
        in_specs=(
            P(("bucket", "seq"), None),
            P("bucket", None),
            P("bucket", "seq", None),
            P("bucket"),
            P("bucket"),
            P("bucket"),
            P(),
            P("bucket", None),
            P("bucket", None),
            P("bucket", None),
            P("bucket", None),
            P("bucket", None),
            P("bucket", None),
            P(),
            P(),
            P(),
            P(("bucket", "seq"), None),
        ),
        out_specs=(
            P(("bucket", "seq"), None),
            P(("bucket", "seq"), None),
            P("bucket", "seq", None),
            P(("bucket", "seq"), None),
            P(("bucket", "seq"), None),
            P(("bucket", "seq"), None),
            P(("bucket", "seq"), None),
            P(("bucket", "seq"), None),
            P(("bucket", "seq"), None),
            P(("bucket", "seq"), None),
            P(None, ("bucket", "seq")),
            P(None, ("bucket", "seq")),
            P(),
        ),
        check_vma=False,
    )
```

profile of v0, /device:TPU:4, one launch (start us, length us, event | category | flops | bytes accessed | tf_op | source)
XLA Modules:
  0.0 3480.0 jit_solution(11265823724546249781)
XLA Ops:
  13.7 95.3 %all-gather.9.cloned.1.call-done = bf16[1536,6144]{1,0:T(8,128)(2,1)} async-done(((bf16[192,6144]{1,0:T(8,128)(2,1)}), bf16[1536,6144]{1,0:T(8,128)(2,1)}) %all-gather.9.cloned.1.call-update) | async-done | bytes 18874384 | tf_op jit(solution)/shard_map/all_gather | solution.py:51
  124.7 65.3 %all-gather.11.cloned.1.call-done = bf16[1536,4608]{1,0:T(8,128)(2,1)} async-done(((bf16[192,4608]{1,0:T(8,128)(2,1)}), bf16[1536,4608]{1,0:T(8,128)(2,1)}) %all-gather.11.cloned.1.call-update) | async-done | bytes 14155792 | tf_op jit(solution)/shard_map/all_gather | solution.py:51
  199.9 116.8 %all-gather.15.cloned.1.call-done = bf16[4096,3072]{1,0:T(8,128)(2,1)} async-done(((bf16[512,3072]{1,0:T(8,128)(2,1)}), bf16[4096,3072]{1,0:T(8,128)(2,1)}) %all-gather.15.cloned.1.call-update) | async-done | bytes 25165840 | tf_op jit(solution)/shard_map/all_gather | solution.py:51
  349.6 109.8 %all-gather.13.cloned.1.call-done = bf16[1024,3072]{1,0:T(8,128)(2,1)} async-done(((bf16[256,3072]{1,0:T(8,128)(2,1)}), bf16[1024,3072]{1,0:T(8,128)(2,1)}) %all-gather.13.cloned.1.call-update) | async-done | bytes 6291472 | tf_op jit(solution)/shard_map/all_gather | solution.py:248
  476.7 38.2 %while.56 = (s32[]{:T(128)}, f32[6,4,256,64]{2,3,1,0:T(8,128)}, f32[6,4,256,1]{2,1,3,0:T(4,128)S(1)}, bf16[6,4,256,64]{2,3,1,0:T(8,128)(2,1)S(1)}, bf16[6,4,1024...) while((s32[]{:T(128)}, f32[6,4,256,64]{2,3,1,0:T(8,128)}, ...), condition=%wide.region_6.7_spmd.clone, body=%wide.region_3.6_spmd.clone.sunk | while | flops 280230912 | bytes 15113321 | solution.py:131
  518.2 56.8 %all-gather.17.cloned.1.call-done = bf16[4,256,3072]{2,1,0:T(8,128)(2,1)} async-done(((bf16[4,64,3072]{2,1,0:T(8,128)(2,1)}), bf16[4,256,3072]{2,1,0:T(8,128)(2,1)}) %all-gather.17.cloned.1.call-update) | async-done | bytes 6291472 | tf_op jit(solution)/shard_map/all_gather | solution.py:261
  591.8 38.5 %while.57 = (s32[]{:T(128)}, f32[6,4,256,64]{2,3,1,0:T(8,128)}, f32[6,4,256,1]{2,1,3,0:T(4,128)S(1)}, bf16[6,4,256,64]{2,3,1,0:T(8,128)(2,1)S(1)}, bf16[6,4,1024...) while((s32[]{:T(128)}, f32[6,4,256,64]{2,3,1,0:T(8,128)}, ...), condition=%wide.region_11.12_spmd.clone, body=%wide.region_8.11_spmd.clone.sunk | while | flops 280493056 | bytes 15114353 | solution.py:131
  644.6 95.3 %all-gather.21.cloned.1.call-done = bf16[1536,8192]{1,0:T(8,128)(2,1)} async-done(((bf16[192,8192]{1,0:T(8,128)(2,1)}), bf16[1536,8192]{1,0:T(8,128)(2,1)}) %all-gather.21.cloned.1.call-update) | async-done | bytes 25165840 | tf_op jit(solution)/shard_map/all_gather | solution.py:51
  757.7 56.9 %all-gather.23.cloned.1.call-done = bf16[4096,1536]{1,0:T(8,128)(2,1)} async-done(((bf16[512,1536]{1,0:T(8,128)(2,1)}), bf16[4096,1536]{1,0:T(8,128)(2,1)}) %all-gather.23.cloned.1.call-update) | async-done | bytes 12582928 | tf_op jit(solution)/shard_map/all_gather | solution.py:51
  844.3 16.3 multiply_reduce_fusion.8
  882.7 79.3 %while.58 = (s32[]{:T(128)}, f32[6,4,256,64]{2,3,1,0:T(8,128)S(1)}, bf16[6,4,1024,64]{2,3,1,0:T(8,128)(2,1)}, bf16[6,4,1024,64]{2,3,1,0:T(8,128)(2,1)}, bf16[6,4...) while((s32[]{:T(128)}, f32[6,4,256,64]{2,3,1,0:T(8,128)S(1)}, ...), condition=%wide.region_20.21_spmd.clone, body=%wide.region_18.20_spmd.clone.sunk | while | flops 687406080 | bytes 37001344 | solution.py:175
  984.2 79.6 %while.59 = (s32[]{:T(128)}, f32[6,4,256,64]{2,3,1,0:T(8,128)S(1)}, bf16[6,4,1024,64]{2,3,1,0:T(8,128)(2,1)}, bf16[6,4,1024,64]{2,3,1,0:T(8,128)(2,1)}, bf16[6,4...) while((s32[]{:T(128)}, f32[6,4,256,64]{2,3,1,0:T(8,128)S(1)}, ...), condition=%wide.region_25.26_spmd.clone, body=%wide.region_23.25_spmd.clone.sunk | while | flops 687668224 | bytes 37002376 | solution.py:175
  1120.4 85.9 %reduce-scatter.18.cloned.1.call-done = bf16[4,64,3072]{2,1,0:T(8,128)(2,1)} async-done(((bf16[4,256,3072]{2,1,0:T(8,128)(2,1)}), bf16[4,64,3072]{2,1,0:T(8,128)(2,1)}) %reduce-scatter.18.cloned.1.call-update) | async-done | bytes 1572880 | tf_op jit(solution)/shard_map/reduce_scatter | solution.py:329
  1298.3 19.3 fusion.166
  1318.7 21.7 fusion.140
  1342.0 21.7 fusion.143
  1364.6 41.9 %psum.7 = f32[24]{0:T(128)} all-reduce(f32[24]{0:T(128)S(1)} %subtract_multiply_fusion.1), channel_id=1, replica_groups=mesh['bucket'=8,'seq'=4] {'bucket','seq'}, use_global_device_ids=true, to_apply=%region_49.50 | all-reduce | flops 24 | bytes 192 | tf_op jit(solution)/shard_map/psum | solution.py:380
  1428.6 139.8 %reduce-scatter.28.cloned.1.call-done = f32[48,1536]{1,0:T(8,128)} async-done(((f32[1536,1536]{1,0:T(8,128)}), f32[48,1536]{1,0:T(8,128)}) %reduce-scatter.28.cloned.1.call-update) | async-done | bytes 294928 | tf_op jit(solution)/shard_map/reduce_scatter | solution.py:375
  1568.4 149.4 %reduce-scatter.20.cloned.1.call-done = f32[8,4096]{1,0:T(8,128)} async-done(((f32[256,4096]{1,0:T(8,128)}), f32[8,4096]{1,0:T(8,128)}) %reduce-scatter.20.cloned.1.call-update) | async-done | bytes 131088 | tf_op jit(solution)/shard_map/reduce_scatter | solution.py:376
  1717.8 252.4 %reduce-scatter.32.cloned.1.call-done = f32[128,1536]{1,0:T(8,128)} async-done(((f32[4096,1536]{1,0:T(8,128)}), f32[128,1536]{1,0:T(8,128)}) %reduce-scatter.32.cloned.1.call-update) | async-done | bytes 786448 | tf_op jit(solution)/shard_map/reduce_scatter | solution.py:293
  1970.2 270.3 %reduce-scatter.24.cloned.1.call-done = f32[48,4608]{1,0:T(8,128)} async-done(((f32[1536,4608]{1,0:T(8,128)}), f32[48,4608]{1,0:T(8,128)}) %reduce-scatter.24.cloned.1.call-update) | async-done | bytes 884752 | tf_op jit(solution)/shard_map/reduce_scatter | solution.py:373
  2240.5 355.2 %reduce-scatter.22.cloned.1.call-done = f32[48,6144]{1,0:T(8,128)} async-done(((f32[1536,6144]{1,0:T(8,128)}), f32[48,6144]{1,0:T(8,128)}) %reduce-scatter.22.cloned.1.call-update) | async-done | bytes 1179664 | tf_op jit(solution)/shard_map/reduce_scatter | solution.py:372
  2595.6 438.7 %reduce-scatter.30.cloned.1.call-done = f32[48,8192]{1,0:T(8,128)} async-done(((f32[1536,8192]{1,0:T(8,128)}), f32[48,8192]{1,0:T(8,128)}) %reduce-scatter.30.cloned.1.call-update) | async-done | bytes 1572880 | tf_op jit(solution)/shard_map/reduce_scatter | solution.py:292
  3034.3 438.7 %reduce-scatter.26.cloned.1.call-done = f32[128,3072]{1,0:T(8,128)} async-done(((f32[4096,3072]{1,0:T(8,128)}), f32[128,3072]{1,0:T(8,128)}) %reduce-scatter.26.cloned.1.call-update) | async-done | bytes 1572880 | tf_op jit(solution)/shard_map/reduce_scatter | solution.py:374
  (499 shorter events, 616.0 us)
Async XLA Ops:
  7.2 101.9 %all-gather.9.cloned.1.call-start = ((), (), s32[]{:S(2)}) async-start(), calls=%async_computation.11 | async-start | bytes 21233664 | tf_op jit(solution)/shard_map/all_gather | solution.py:51
  8.0 182.0 %all-gather.11.cloned.1.call-start = ((), (), s32[]{:S(2)}) async-start(), calls=%async_computation.12 | async-start | bytes 15925248 | tf_op jit(solution)/shard_map/all_gather | solution.py:51
  8.7 308.0 %all-gather.15.cloned.1.call-start = ((), (), s32[]{:S(2)}) async-start(), calls=%async_computation.14 | async-start | bytes 28311552 | tf_op jit(solution)/shard_map/all_gather | solution.py:51
  9.5 449.9 %all-gather.13.cloned.1.call-start = ((), (), s32[]{:S(2)}) async-start(), calls=%async_computation.13 | async-start | bytes 7864320 | tf_op jit(solution)/shard_map/all_gather | solution.py:248
  10.5 318.2 %copy-start.45 = (f32[1536]{0:T(1024)}, f32[1536]{0:T(1024)S(1)}, u32[]{:S(2)}) copy-start(f32[1536]{0:T(1024)S(1)} %get-tuple-element.327) | copy-start | bytes 18436
  10.5 318.2 %copy-start.47 = (f32[1536]{0:T(1024)}, f32[1536]{0:T(1024)S(1)}, u32[]{:S(2)}) copy-start(f32[1536]{0:T(1024)S(1)} %get-tuple-element.328) | copy-start | bytes 18436
  11.7 324.1 %copy-start.39 = (f32[256,32]{0,1:T(8,128)}, f32[256,32]{0,1:T(8,128)S(1)}, u32[]{:S(2)}) copy-start(f32[256,32]{0,1:T(8,128)S(1)} %get-tuple-element.460) | copy-start | bytes 98308
  11.7 324.1 %copy-start.41 = (f32[256,32]{0,1:T(8,128)}, f32[256,32]{0,1:T(8,128)S(1)}, u32[]{:S(2)}) copy-start(f32[256,32]{0,1:T(8,128)S(1)} %get-tuple-element.461) | copy-start | bytes 98308
  342.7 232.3 %all-gather.17.cloned.1.call-start = ((), (), s32[]{:S(2)}) async-start(), calls=%async_computation.15 | async-start | bytes 7864320 | tf_op jit(solution)/shard_map/all_gather | solution.py:261
  345.7 290.6 %all-gather.19.cloned.1.call-start = ((), (), s32[]{:S(2)}) async-start(), calls=%async_computation.16 | async-start | bytes 5308416 | tf_op jit(solution)/shard_map/all_gather | solution.py:51
  346.3 393.7 %all-gather.21.cloned.1.call-start = ((), (), s32[]{:S(2)}) async-start(), calls=%async_computation.17 | async-start | bytes 28311552 | tf_op jit(solution)/shard_map/all_gather | solution.py:51
  347.0 467.6 %all-gather.23.cloned.1.call-start = ((), (), s32[]{:S(2)}) async-start(), calls=%async_computation.18 | async-start | bytes 14155776 | tf_op jit(solution)/shard_map/all_gather | solution.py:51
  347.8 749.3 %reduce-scatter.16.cloned.1.call-start = ((), (), s32[]{:S(2)}) async-start(), calls=%async_computation.19 | async-start | bytes 7864320 | tf_op jit(solution)/shard_map/reduce_scatter | solution.py:322
  978.5 227.8 %reduce-scatter.18.cloned.1.call-start = ((), (), s32[]{:S(2)}) async-start(), calls=%async_computation.20 | async-start | bytes 7864320 | tf_op jit(solution)/shard_map/reduce_scatter | solution.py:329
  1094.9 315.8 %reduce-scatter.36.cloned.1.call-start = ((), (), s32[]{:S(2)}) async-start(), calls=%async_computation.29 | async-start | bytes 811008
  1231.5 195.7 %reduce-scatter.34.cloned.1.call-start = ((), (), s32[]{:S(2)}) async-start(), calls=%async_computation.28 | async-start | bytes 811008
  1232.8 335.6 %reduce-scatter.28.cloned.1.call-start = ((), (), s32[]{:S(2)}) async-start(), calls=%async_computation.25 | async-start | bytes 9732096 | tf_op jit(solution)/shard_map/reduce_scatter | solution.py:375
  1237.8 480.0 %reduce-scatter.20.cloned.1.call-start = ((), (), s32[]{:S(2)}) async-start(), calls=%async_computation.21 | async-start | bytes 4325376 | tf_op jit(solution)/shard_map/reduce_scatter | solution.py:376
  1266.1 704.1 %reduce-scatter.32.cloned.1.call-start = ((), (), s32[]{:S(2)}) async-start(), calls=%async_computation.27 | async-start | bytes 25952256 | tf_op jit(solution)/shard_map/reduce_scatter | solution.py:293
  1277.9 962.5 %reduce-scatter.24.cloned.1.call-start = ((), (), s32[]{:S(2)}) async-start(), calls=%async_computation.23 | async-start | bytes 29196288 | tf_op jit(solution)/shard_map/reduce_scatter | solution.py:373
  1292.9 1302.8 %reduce-scatter.22.cloned.1.call-start = ((), (), s32[]{:S(2)}) async-start(), calls=%async_computation.22 | async-start | bytes 38928384 | tf_op jit(solution)/shard_map/reduce_scatter | solution.py:372
  1317.6 1716.7 %reduce-scatter.30.cloned.1.call-start = ((), (), s32[]{:S(2)}) async-start(), calls=%async_computation.26 | async-start | bytes 51904512 | tf_op jit(solution)/shard_map/reduce_scatter | solution.py:292
  1340.5 2132.5 %reduce-scatter.26.cloned.1.call-start = ((), (), s32[]{:S(2)}) async-start(), calls=%async_computation.24 | async-start | bytes 51904512 | tf_op jit(solution)/shard_map/reduce_scatter | solution.py:374
  1406.5 2066.5 %copy-start.1 = (bf16[256,4096]{1,0:T(8,128)(2,1)S(1)}, bf16[256,4096]{1,0:T(8,128)(2,1)}, u32[]{:S(2)}) copy-start(bf16[256,4096]{1,0:T(8,128)(2,1)} %param.31) | copy-start | bytes 6291460
  (79 other events, 2277.0 us)
Sparse Core Ops, SparseCore 0:
  9.9 99.0 all-gather.8
  110.9 78.9 all-gather.10
  191.9 124.8 all-gather.14
  342.8 116.5 all-gather.12
  461.3 113.5 all-gather.16
  576.7 36.9 all-gather.18
  615.5 124.3 all-gather.20
  741.9 72.6 all-gather.22
  978.6 111.2 reduce-scatter.15
  1095.0 111.3 reduce-scatter.17
  1231.6 95.9 reduce-scatter.35
  1332.5 94.5 reduce-scatter.33
  1433.7 134.6 reduce-scatter.27
  1571.2 146.5 reduce-scatter.19
  1725.8 244.3 reduce-scatter.31
  1977.1 263.3 reduce-scatter.23
  2247.3 348.2 reduce-scatter.21
  2603.6 430.6 reduce-scatter.29
  3042.5 430.5 reduce-scatter.25
where the time goes:
time: 3490 us; the launch traced here: 3480 us
  waiting for transfers between devices  2750 us (79%)
  matrix products  412 us (12%)
  local copies, waits for them, and re-layouts  139 us (4%)
  other arithmetic  123 us (4%)
  blocking collectives  41.9 us (1%)
    reduce_scatter x1, waiting for transfers between devices, per_device(): lax.psum_scatter(grad_text_local, ('bucket', 'seq'), scatter_dimension=0,...  439 us
    reduce_scatter x1, waiting for transfers between devices, per_device(): lax.psum_scatter(grad_gate_local, ('bucket', 'seq'), scatter_dimension=0,...  439 us
    all_gather x6, waiting for transfers between devices, forward_product(): lax.all_gather(weight_shard, 'bucket', axis=0, tiled=True)  430 us
    reduce_scatter x1, waiting for transfers between devices, per_device(): lax.psum_scatter(grad_modulation_local, ('bucket', 'seq'), scatter_dimens...  355 us
    reduce_scatter x1, waiting for transfers between devices, per_device(): lax.psum_scatter(grad_projection_local, ('bucket', 'seq'), scatter_dimens...  270 us
    reduce_scatter x1, waiting for transfers between devices, per_device(): lax.psum_scatter(grad_down_local, ('bucket', 'seq'), scatter_dimension=0,...  252 us
    reduce_scatter x1, waiting for transfers between devices, per_device(): lax.psum_scatter(grad_null_local, ('bucket', 'seq'), scatter_dimension=0,...  149 us
    reduce_scatter x1, waiting for transfers between devices, per_device(): lax.psum_scatter(grad_output_local, ('bucket', 'seq'), scatter_dimension=...  140 us
  transfers between devices with their start and end apart: 19, of which 16 were waited for; matrix products, arithmetic and copies ran while one was open for 13% of the time, Pallas kernels for 0%

commit v1 on v0

v1 whole, which is shorter than its diff:
```python
from functools import partial

import jax
import jax.numpy as jnp
from jax import lax
from jax.experimental import pallas as pl
from jax.experimental.pallas import tpu as pltpu
from jax.sharding import PartitionSpec as P

EPSILON = 1e-06
NEGATIVE = -1e30
HIGHEST = lax.Precision.HIGHEST
wide = jnp.float32
narrow = jnp.bfloat16
VMEM_LIMIT = 50 * 2**20


def rms_norm(values, norm_gain):
    return (
        values * lax.rsqrt(jnp.mean(values * values, axis=-1, keepdims=True) + EPSILON) * norm_gain
    )


def dense(leading, trailing):
    return jnp.dot(leading, trailing, preferred_element_type=wide)


def contract_rows(leading, trailing):
    return lax.dot_general(
        leading, trailing, (((0,), (0,)), ((), ())), preferred_element_type=wide
    )


def contract_cols(leading, trailing):
    return lax.dot_general(
        leading, trailing, (((1,), (1,)), ((), ())), preferred_element_type=wide
    )


def pre_attention(tokens_in, modulated, norm_gains):
    model_width = tokens_in.shape[1]
    return rms_norm(tokens_in, norm_gains[0]) * (1.0 + modulated[:, :model_width])


def text_heads(text_pairs, gain):
    model_width = text_pairs.shape[1] // 2
    return (rms_norm(text_pairs[:, :model_width], gain), text_pairs[:, model_width:])


def post_attention(attended, tokens_in, modulated, norm_gains):
    model_width = tokens_in.shape[1]
    middle = tokens_in + jnp.tanh(modulated[:, model_width : 2 * model_width]) * rms_norm(
        attended, norm_gains[1]
    )
    normed_ffn = rms_norm(middle, norm_gains[2]) * (
        1.0 + modulated[:, 2 * model_width : 3 * model_width]
    )
    return (middle, normed_ffn)


def swiglu(gate_values):
    hidden_width = gate_values.shape[1] // 2
    return jax.nn.silu(gate_values[:, :hidden_width]) * gate_values[:, hidden_width:]


def finish(lowered, middle, modulated, norm_gains):
    model_width = middle.shape[1]
    return middle + jnp.tanh(modulated[:, 3 * model_width :]) * rms_norm(lowered, norm_gains[3])


def flip(values, bits):
    count = lax.axis_size("bucket")
    return lax.ppermute(values, "bucket", [(i, i ^ bits) for i in range(count)])


def plane_orders():
    count = lax.axis_size("bucket")
    outer = [1 << i for i in range(1, count.bit_length() - 1)]
    return outer + [1], outer[::-1] + [1]


def plane_gather(values, order):
    blocks = [values]
    for bit in order:
        blocks = blocks + [flip(block, bit) for block in blocks]
    return jnp.concatenate(blocks, axis=0)


def plane_scatter(values, order):
    total = values
    for bit in order[::-1]:
        half = total.shape[0] // 2
        arrived = flip(total[half:].astype(narrow), bit)
        total = total[:half].astype(wide) + arrived.astype(wide)
    return total


def ring_gather(values):
    count = lax.axis_size("seq")
    index = lax.axis_index("seq")
    out = jnp.zeros((count,) + values.shape, values.dtype)
    block = values
    for step in range(count):
        if step > 0:
            block = lax.ppermute(block, "seq", [(i, (i + 1) % count) for i in range(count)])
        out = lax.dynamic_update_index_in_dim(out, block, lax.rem(index - step + count, count), 0)
    return out


def ring_scatter(values):
    count = lax.axis_size("seq")
    index = lax.axis_index("seq")

    def part(step):
        return lax.dynamic_index_in_dim(
            values, lax.rem(index - 1 - step + 2 * count, count), 0, keepdims=False
        ).astype(wide)

    total = part(0)
    for step in range(1, count):
        moved = lax.ppermute(
            total.astype(narrow), "seq", [(i, (i + 1) % count) for i in range(count)]
        )
        total = part(step) + moved.astype(wide)
    return total


def clip_span(bucket, slot_rows, block, block_rows):
    length = jnp.where(
        bucket == 0, slot_rows // 4, jnp.where(bucket == 1, slot_rows // 2, slot_rows)
    )
    clip = lax.div(jnp.int32(block * block_rows), length)
    return clip, clip * length, length


def dot_nt(leading, trailing):
    return contract_cols(leading, trailing)


def attend_kernel(
    blocks, bucket, lengths, gates, q, k, vt, qc, tk, tvt, out, total, cross_total
):
    head = pl.program_id(0)
    rows = q.shape[1]
    block_rows = rows // blocks
    key_index = lax.broadcasted_iota(jnp.int32, (rows, block_rows), 0)
    cap_index = lax.broadcasted_iota(jnp.int32, (tk.shape[2], block_rows), 0)
    for block in range(blocks):
        clip, first, length = clip_span(bucket[0], rows, block, block_rows)
        here = slice(block * block_rows, (block + 1) * block_rows)
        scores = dot_nt(k[0], q[0, here])
        scores = jnp.where(
            (key_index >= first) & (key_index < first + length), scores, NEGATIVE
        )
        peak = jnp.max(scores, axis=0, keepdims=True)
        shares = jnp.exp(scores - peak)
        mass = jnp.sum(shares, axis=0, keepdims=True)
        self_out = dense(vt[0], shares.astype(narrow)) / mass
        total[0, :, here] = peak + jnp.log(mass)
        scores = dot_nt(tk[0, clip], qc[0, here])
        scores = jnp.where(cap_index < lengths[clip], scores, NEGATIVE)
        peak = jnp.max(scores, axis=0, keepdims=True)
        shares = jnp.exp(scores - peak)
        mass = jnp.sum(shares, axis=0, keepdims=True)
        cross_out = dense(tvt[0, clip], shares.astype(narrow)) / mass
        cross_total[0, :, here] = peak + jnp.log(mass)
        out[0, :, here] = (self_out + gates[head] * cross_out).astype(narrow)


def attend_back_kernel(
    blocks, scaling, bucket, lengths, gates, q, k, kt, v, qc, tk, tkt, tv, go, total, cross_total,
    dq, dqc, dk, dv, dtk, dtv, dgate,
):
    head = pl.program_id(0)
    rows = q.shape[1]
    block_rows = rows // blocks
    gate = gates[head]
    key_index = lax.broadcasted_iota(jnp.int32, (rows, block_rows), 0)
    cap_index = lax.broadcasted_iota(jnp.int32, (tk.shape[2], block_rows), 0)
    dk[...] = jnp.zeros_like(dk)
    dv[...] = jnp.zeros_like(dv)
    dtk[...] = jnp.zeros_like(dtk)
    dtv[...] = jnp.zeros_like(dtv)
    for block in range(blocks):
        clip, first, length = clip_span(bucket[0], rows, block, block_rows)
        here = slice(block * block_rows, (block + 1) * block_rows)
        grad = go[0, here]
        scores = dot_nt(k[0], q[0, here])
        scores = jnp.where(
            (key_index >= first) & (key_index < first + length), scores, NEGATIVE
        )
        shares = jnp.exp(scores - total[0, :, here])
        grad_shares = dot_nt(v[0], grad)
        row = jnp.sum(grad_shares * shares, axis=0, keepdims=True)
        grad_scores = (shares * (grad_shares - row)).astype(narrow)
        dv[0] += dense(shares.astype(narrow), grad)
        dk[0] += dense(grad_scores, q[0, here])
        dq[0, :, here] = dense(kt[0], grad_scores) * scaling
        scores = dot_nt(tk[0, clip], qc[0, here])
        scores = jnp.where(cap_index < lengths[clip], scores, NEGATIVE)
        shares = jnp.exp(scores - cross_total[0, :, here])
        grad_shares = dot_nt(tv[0, clip], grad)
        row = jnp.sum(grad_shares * shares, axis=0, keepdims=True)
        grad_scores = (gate * (shares * (grad_shares - row))).astype(narrow)
        dtv[0, clip] += gate * dense(shares.astype(narrow), grad)
        dtk[0, clip] += dense(grad_scores, qc[0, here])
        dqc[0, :, here] = dense(tkt[0, clip], grad_scores) * scaling
        dgate[0, :, here] = row


def head_spec(shape):
    rest = len(shape) - 1
    return pl.BlockSpec((1,) + tuple(shape[1:]), lambda h: (h,) + (0,) * rest)


def call_heads(kernel, scalars, arrays, outs, flops, name):
    heads = arrays[0].shape[0]
    return pl.pallas_call(
        kernel,
        grid=(heads,),
        in_specs=[pl.BlockSpec(memory_space=pltpu.SMEM)] * len(scalars)
        + [head_spec(a.shape) for a in arrays],
        out_specs=[head_spec(o.shape) for o in outs],
        out_shape=outs,
        compiler_params=pltpu.CompilerParams(vmem_limit_bytes=VMEM_LIMIT),
        cost_estimate=pl.CostEstimate(flops=flops, bytes_accessed=16 * 2**20, transcendentals=0),
        name=name,
    )(*scalars, *arrays)


def turn(values, cosine, sine):
    half = cosine.shape[-1]
    first, second = values[..., :half], values[..., half:]
    return jnp.concatenate(
        [first * cosine - second * sine, first * sine + second * cosine], axis=-1
    )


def per_device(
    tokens,
    condition,
    captions,
    caption_lengths,
    null_flags,
    slot_buckets,
    null_caption,
    modulation,
    projection,
    text_weight,
    output_weight,
    gate_up,
    down_weight,
    norm_gains,
    head_gains,
    cross_gates,
    cotangent,
):
    count_s, count_b = lax.axis_size("seq"), lax.axis_size("bucket")
    s, b = lax.axis_index("seq"), lax.axis_index("bucket")
    assert count_s % 4 == 0
    local, width = tokens.shape
    heads = cross_gates.shape[0]
    size = width // heads
    own_heads = heads // count_s
    own = width // count_s
    rows = local * count_s
    places, cap_local, text_width = captions.shape
    cap_rows = places * cap_local
    hidden_width = down_weight.shape[0]
    scaling = size ** (-0.5)
    bucket = slot_buckets[0]
    clip_length = jnp.where(
        bucket == 0, rows // 4, jnp.where(bucket == 1, rows // 2, rows)
    ).astype(jnp.int32)
    order_a, order_b = plane_orders()
    halves = ((slice(0, local // 2), order_a), (slice(local // 2, local), order_b))

    own_projection = lax.dynamic_index_in_dim(
        projection.reshape(-1, 3, count_s, own), s, 2, keepdims=False
    ).reshape(-1, 3 * own)
    own_projection = lax.all_gather(own_projection, "bucket", axis=0, tiled=True)
    full_output = lax.all_gather(output_weight, "bucket", axis=0, tiled=True)

    silu_cond = jax.nn.silu(condition).astype(narrow)
    cond_columns = lax.all_to_all(silu_cond, "bucket", 1, 0, tiled=True)
    mod_width = modulation.shape[1] // count_s
    mod_part = dense(cond_columns, lax.dynamic_slice_in_dim(modulation, s * mod_width, mod_width, 1))
    mod_part = lax.all_to_all(mod_part, "bucket", 0, 0, tiled=True)
    mod_part = jnp.sum(mod_part.reshape(count_b, places, mod_width), axis=0)
    clip_of = (jnp.arange(count_s, dtype=jnp.int32) * local) // clip_length
    chosen = clip_of[:, None] == jnp.arange(places, dtype=jnp.int32)[None, :]
    mod_rows = jnp.sum(jnp.where(chosen[:, :, None], mod_part[None], 0.0), axis=1)
    modulated = lax.all_to_all(mod_rows, "seq", 0, 1, tiled=True)

    tokens_in = tokens.astype(wide)
    normed_full, pre_pull = jax.vjp(pre_attention, tokens_in, modulated, norm_gains)
    normed = ring_gather(normed_full.astype(narrow)).reshape(rows, width)

    null_rows = lax.dynamic_slice_in_dim(null_caption, s * cap_local, cap_local, 0)
    is_null = null_flags[:, None, None] == 1
    words_own = jnp.where(is_null, null_rows[None], captions).reshape(cap_rows, text_width)
    text_rows = text_weight.shape[0]
    block_ids = [0]
    for bit in order_a:
        block_ids = block_ids + [k | bit for k in block_ids]
    ids_b = [0]
    for bit in order_b:
        ids_b = ids_b + [k | bit for k in ids_b]
    from_a_to_b = [block_ids.index(k) for k in ids_b]

    def word_block(k):
        piece = lax.dynamic_slice_in_dim(words_own, jnp.bitwise_xor(b, k) * text_rows, text_rows, 1)
        return flip(piece, k) if k else piece

    words = jnp.concatenate([word_block(k) for k in block_ids], axis=0)
    pairs_a = dense(words, text_weight[:, :width])
    pairs_b = dense(words, text_weight[:, width:])
    pairs_b = jnp.concatenate(
        [pairs_b[i * cap_rows : (i + 1) * cap_rows] for i in from_a_to_b], axis=0
    )
    text_pairs = jnp.concatenate(
        [
            plane_scatter(pairs_a.astype(narrow), order_a),
            plane_scatter(pairs_b.astype(narrow), order_b),
        ],
        axis=1,
    )
    text_outs, text_pull = jax.vjp(text_heads, text_pairs, head_gains[2])
    text_kv = jnp.stack([o.astype(narrow).reshape(cap_rows, count_s, own) for o in text_outs])
    text_kv = lax.all_to_all(text_kv.transpose(2, 0, 1, 3), "seq", 0, 0, tiled=True)
    text_kv = text_kv.reshape(count_s, 2, places, cap_local, own_heads, size)
    text_kv = text_kv.transpose(1, 4, 2, 0, 3, 5).reshape(
        2, own_heads, places, count_s * cap_local, size
    )
    text_keys, text_values = text_kv[0], text_kv[1]

    projected = dense(normed, own_projection)
    gain_q = lax.dynamic_slice_in_dim(head_gains[0], s * own, own, 0)
    gain_k = lax.dynamic_slice_in_dim(head_gains[1], s * own, own, 0)
    raw_q, raw_k, raw_v = (projected[:, i * own : (i + 1) * own] for i in range(3))
    squares = jnp.stack([jnp.sum(raw_q * raw_q, axis=1), jnp.sum(raw_k * raw_k, axis=1)])
    rate = lax.rsqrt(lax.psum(squares, "seq") / width + EPSILON)
    hat_q = raw_q * rate[0][:, None]
    hat_k = raw_k * rate[1][:, None]
    inside = lax.rem(jnp.arange(rows, dtype=jnp.int32), clip_length)
    half = size // 2
    frequency = 10000.0 ** (-jnp.arange(half, dtype=wide) / half)
    angles = inside.astype(wide)[:, None] * frequency[None, :]
    cosine, sine = jnp.cos(angles), jnp.sin(angles)

    def to_heads(values):
        return values.reshape(rows, own_heads, size).transpose(1, 0, 2)

    def from_heads(values):
        return values.transpose(1, 0, 2).reshape(rows, own)

    norm_q = to_heads(hat_q * gain_q)
    query = turn(norm_q, cosine, sine).astype(narrow)
    query_cross = norm_q.astype(narrow)
    key = turn(to_heads(hat_k * gain_k), cosine, sine).astype(narrow)
    value = to_heads(raw_v.astype(narrow))
    scaled = (query * scaling).astype(narrow)
    scaled_cross = (query_cross * scaling).astype(narrow)

    tanh_gates = jnp.tanh(cross_gates)
    own_gates = lax.dynamic_slice_in_dim(tanh_gates, s * own_heads, own_heads, 0)
    scalars = (slot_buckets, caption_lengths, own_gates)
    span = rows + count_s * cap_local
    products = own_heads * rows * span * size * 2
    row_shape = jax.ShapeDtypeStruct((own_heads, 1, rows), wide)
    combined, total, cross_total = call_heads(
        partial(attend_kernel, count_s),
        scalars,
        (
            scaled,
            key,
            value.transpose(0, 2, 1),
            scaled_cross,
            text_keys,
            text_values.transpose(0, 1, 3, 2),
        ),
        (jax.ShapeDtypeStruct((own_heads, size, rows), narrow), row_shape, row_shape),
        2 * products,
        "attend",
    )
    combined = combined.reshape(own, rows).T
    combined = lax.all_to_all(combined, "seq", 0, 1, tiled=True)

    attended = dense(combined, full_output)
    (middle, ffn_full), post_pull = jax.vjp(
        post_attention, attended, tokens_in, modulated, norm_gains
    )
    normed_ffn = ffn_full.astype(narrow)

    own_hidden = hidden_width
    gate_rows = gate_up.shape[0]
    own_gate_up = lax.all_to_all(
        gate_up.reshape(gate_rows, 2, count_b, own_hidden), "bucket", 2, 0, tiled=True
    ).reshape(count_b * gate_rows, 2 * own_hidden)
    gathered, hiddens, pulls, lows = [], [], [], []
    for part, order in halves:
        plane = plane_gather(normed_ffn[part], order)
        hidden_full, pull = jax.vjp(swiglu, dense(plane, own_gate_up))
        hidden = hidden_full.astype(narrow)
        lows.append(plane_scatter(dense(hidden, down_weight), order))
        gathered.append(plane)
        hiddens.append(hidden)
        pulls.append(pull)
    lowered = jnp.concatenate(lows, axis=0)
    mixed, finish_pull = jax.vjp(finish, lowered, middle, modulated, norm_gains)
    grad_lowered, grad_middle, grad_modulated_last, grad_norm_last = finish_pull(
        cotangent.astype(wide)
    )
    grad_lowered_low = grad_lowered.astype(narrow)
    grad_normed_ffn, grad_down, grad_gate_up = [], 0.0, 0.0
    for (part, order), plane, hidden, pull in zip(halves, gathered, hiddens, pulls, strict=True):
        upstream = plane_gather(grad_lowered_low[part], order)
        (grad_gate_values,) = pull(contract_cols(upstream, down_weight))
        grad_gate_low = grad_gate_values.astype(narrow)
        grad_normed_ffn.append(plane_scatter(contract_cols(grad_gate_low, own_gate_up), order))
        grad_down = grad_down + contract_rows(hidden, upstream)
        grad_gate_up = grad_gate_up + contract_rows(plane, grad_gate_low)
    grad_normed_ffn = jnp.concatenate(grad_normed_ffn, axis=0)
    down_share = lax.psum_scatter(
        grad_down.astype(narrow), "seq", scatter_dimension=0, tiled=True
    ).astype(wide)
    gate_share = lax.psum_scatter(
        grad_gate_up.astype(narrow).reshape(count_b, gate_rows, 2 * own_hidden),
        "seq",
        scatter_dimension=1,
        tiled=True,
    )
    share_rows = gate_rows // count_s
    gate_share = lax.all_to_all(gate_share, "bucket", 0, 0, tiled=True)
    gate_share = (
        gate_share.reshape(count_b, share_rows, 2, own_hidden)
        .transpose(1, 2, 0, 3)
        .reshape(share_rows, 2 * count_b * own_hidden)
        .astype(wide)
    )

    grad_attended, grad_tokens_post, grad_modulated_post, grad_norm_post = post_pull(
        (grad_middle, grad_normed_ffn)
    )
    grad_attended_low = grad_attended.astype(narrow)
    grad_combined = contract_cols(grad_attended_low, full_output).astype(narrow)
    grad_output = contract_rows(combined, grad_attended_low).astype(narrow)
    output_share = lax.psum_scatter(
        grad_output, ("bucket", "seq"), scatter_dimension=0, tiled=True
    ).astype(wide)
    grad_heads = to_heads(lax.all_to_all(grad_combined, "seq", 1, 0, tiled=True))
    head_rows = jax.ShapeDtypeStruct((own_heads, rows, size), wide)
    head_columns = jax.ShapeDtypeStruct((own_heads, size, rows), wide)
    text_shape = jax.ShapeDtypeStruct(text_keys.shape, wide)
    grad_query, grad_cross, grad_key, grad_value, grad_text_keys, grad_text_values, grad_gates = (
        call_heads(
            partial(attend_back_kernel, count_s, scaling),
            scalars,
            (
                scaled,
                key,
                key.transpose(0, 2, 1),
                value,
                scaled_cross,
                text_keys,
                text_keys.transpose(0, 1, 3, 2),
                text_values,
                grad_heads,
                total,
                cross_total,
            ),
            (
                head_columns,
                head_columns,
                head_rows,
                head_rows,
                text_shape,
                text_shape,
                row_shape,
            ),
            5 * products,
            "attend_back",
        )
    )

    grad_kv = jnp.stack([grad_text_keys, grad_text_values]).astype(narrow)
    grad_kv = grad_kv.reshape(2, own_heads, places, count_s, cap_local, size)
    grad_kv = grad_kv.transpose(3, 0, 2, 4, 1, 5).reshape(count_s, 2, cap_rows, own)
    grad_kv = lax.all_to_all(grad_kv, "seq", 0, 0, tiled=True)
    grad_kv = grad_kv.transpose(1, 2, 0, 3).reshape(2, cap_rows, width).astype(wide)
    grad_pairs, grad_gain_text = text_pull((grad_kv[0], grad_kv[1]))
    grad_pairs_low = grad_pairs.astype(narrow)
    plane_a = plane_gather(grad_pairs_low[:, :width], order_a)
    plane_b = plane_gather(grad_pairs_low[:, width:], order_b)
    plane_b = jnp.concatenate(
        [
            plane_b[ids_b.index(k) * cap_rows : (ids_b.index(k) + 1) * cap_rows]
            for k in block_ids
        ],
        axis=0,
    )
    grad_text = jnp.concatenate(
        [contract_rows(words, plane_a), contract_rows(words, plane_b)], axis=1
    )
    text_share = lax.psum_scatter(
        grad_text.astype(narrow), "seq", scatter_dimension=0, tiled=True
    ).astype(wide)
    grad_words = (
        contract_cols(plane_a, text_weight[:, :width])
        + contract_cols(plane_b, text_weight[:, width:])
    ).astype(narrow)
    pieces = []
    for i, k in enumerate(block_ids):
        piece = grad_words[i * cap_rows : (i + 1) * cap_rows]
        pieces.append(flip(piece, k) if k else piece)
    pieces = jnp.stack([pieces[block_ids.index(k)] for k in range(count_b)])
    grad_words = jnp.concatenate(
        [
            lax.dynamic_index_in_dim(pieces, jnp.bitwise_xor(b, j), 0, keepdims=False)
            for j in range(count_b)
        ],
        axis=1,
    ).reshape(places, cap_local, text_width)
    grad_captions = jnp.where(is_null, 0.0, grad_words.astype(wide))
    null_local = jnp.sum(jnp.where(is_null, grad_words.astype(wide), 0.0), axis=0).astype(narrow)
    null_share = lax.all_to_all(null_local, "bucket", 0, 0, tiled=True)
    null_share = jnp.sum(null_share.reshape(count_b, -1, text_width).astype(wide), axis=0)
    null_share = lax.ppermute(
        null_share,
        ("bucket", "seq"),
        [(i * count_s + j, j * count_b + i) for i in range(count_b) for j in range(count_s)],
    )

    back_q = turn(grad_query.transpose(0, 2, 1), cosine, -sine) + grad_cross.transpose(0, 2, 1)
    back_q = from_heads(back_q)
    back_k = from_heads(turn(grad_key * 1.0, cosine, -sine))
    back_v = from_heads(grad_value)
    scaled_q, scaled_k = back_q * gain_q, back_k * gain_k
    means = jnp.stack([jnp.sum(scaled_q * hat_q, axis=1), jnp.sum(scaled_k * hat_k, axis=1)])
    means = lax.psum(means, "seq") / width
    grad_projected = jnp.concatenate(
        [
            rate[0][:, None] * (scaled_q - hat_q * means[0][:, None]),
            rate[1][:, None] * (scaled_k - hat_k * means[1][:, None]),
            back_v,
        ],
        axis=1,
    ).astype(narrow)
    grad_projection = contract_rows(normed, grad_projected).astype(narrow)
    proj_share = lax.psum_scatter(grad_projection, "bucket", scatter_dimension=0, tiled=True)
    proj_share = lax.all_to_all(
        proj_share.reshape(count_s, -1, 3 * own), "seq", 0, 0, tiled=True
    )
    proj_share = (
        proj_share.reshape(count_s, -1, 3, own)
        .transpose(1, 2, 0, 3)
        .reshape(-1, 3 * width)
        .astype(wide)
    )
    grad_normed = ring_scatter(
        contract_cols(grad_projected, own_projection).reshape(count_s, local, width)
    )
    grad_tokens_pre, grad_modulated_pre, grad_norm_pre = pre_pull(grad_normed)
    grad_tokens = grad_tokens_pre + grad_tokens_post

    grad_modulated = grad_modulated_pre + grad_modulated_post + grad_modulated_last
    my_clip = (s * local) // clip_length
    placed = jnp.where(
        jnp.arange(places, dtype=jnp.int32)[:, None] == my_clip, grad_modulated, 0.0
    )
    placed = lax.all_gather(lax.psum(placed, "seq"), "bucket", axis=0, tiled=True)
    mod_rows_out = silu_cond.shape[1] // (count_s * count_b)
    cond_own = lax.dynamic_slice_in_dim(cond_columns, s * mod_rows_out, mod_rows_out, 1)
    mod_share = lax.dot_general(
        cond_own.astype(wide), placed, (((0,), (0,)), ((), ())), precision=HIGHEST
    )

    def place(values):
        return lax.dynamic_update_slice_in_dim(jnp.zeros((width,), wide), values, s * own, 0)

    gate_sums = lax.dynamic_update_slice_in_dim(
        jnp.zeros((heads,), wide),
        jnp.sum(grad_gates, axis=(1, 2)) * (1.0 - own_gates * own_gates),
        s * own_heads,
        0,
    )
    small = jnp.concatenate(
        [
            grad_norm_pre + grad_norm_post + grad_norm_last,
            jnp.stack(
                [
                    place(jnp.sum(back_q * hat_q, axis=0)),
                    place(jnp.sum(back_k * hat_k, axis=0)),
                    grad_gain_text,
                    jnp.pad(gate_sums, (0, width - heads)),
                ]
            ),
        ],
        axis=0,
    )
    small = lax.psum(small, ("bucket", "seq"))
    share = width // (count_b * count_s)
    own_small = lax.dynamic_slice_in_dim(small, (b * count_s + s) * share, share, 1)
    return (
        mixed.astype(narrow),
        grad_tokens,
        grad_captions,
        null_share,
        mod_share,
        proj_share,
        text_share,
        output_share,
        gate_share,
        down_share,
        own_small[:4],
        own_small[4:7],
        small[7, :heads],
    )


def solution(mesh):
    whole = P(("bucket", "seq"), None)
    shard = P("bucket", None)
    return jax.shard_map(
        per_device,
        mesh=mesh,
        in_specs=(
            whole,
            shard,
            P("bucket", "seq", None),
            P("bucket"),
            P("bucket"),
            P("bucket"),
            P(),
            shard,
            shard,
            shard,
            shard,
            shard,
            shard,
            P(),
            P(),
            P(),
            whole,
        ),
        out_specs=(
            whole,
            whole,
            P("bucket", "seq", None),
            whole,
            whole,
            whole,
            whole,
            whole,
            whole,
            whole,
            P(None, ("bucket", "seq")),
            P(None, ("bucket", "seq")),
            P(),
        ),
        check_vma=False,
    )
```

time: 3490 us -> 1070 us (0.31)
  waiting for transfers between devices: 2750 us -> 326 us
  matrix products: 412 us -> 116 us
  starting transfers between devices: 1.4 us -> 128 us
  blocking collectives: 41.9 us -> 113 us
  Pallas kernels: 0 us -> 57.9 us
  local copies, waits for them, and re-layouts: 139 us -> 180 us
    reduce_scatter x9 -> x5, waiting for transfers between devices: 2130 us -> 0.04 us  [the longest x1 0.02 us: per_device(): lax.psum_scatter(grad_down.astype(narrow), 'seq', scatter_dimension=0, ti...]
    all_gather x8 -> x2, waiting for transfers between devices: 596 us -> 0.02 us  [the longest x1 0.02 us: per_device(): full_output = lax.all_gather(output_weight, 'bucket', axis=0, tiled=True)]
    ppermute x0 -> x81, waiting for transfers between devices: none -> 247 us  [the longest x74 198 us: flip(): return lax.ppermute(values, 'bucket', [(i, i ^ bits) for i in range(count)])]
    dot_general x93 -> x10, matrix products: 277 us -> 37.4 us  [the longest x9 35.6 us: dense(): return jnp.dot(leading, trailing, preferred_element_type=wide)]
    all_to_all x0 -> x11, waiting for transfers between devices: none -> 78.8 us  [the longest x1 27.9 us: per_device(): lax.all_to_all(gate_up.reshape(gate_rows, 2, count_b, own_hidden), 'bucke...]
    ppermute x0 -> x81, starting transfers between devices: none -> 70.7 us  [the longest x74 66.8 us: flip(): return lax.ppermute(values, 'bucket', [(i, i ^ bits) for i in range(count)])]
    psum x1 -> x3, blocking collectives: 41.9 us -> 103 us  [the longest x1 77 us: per_device(): small = lax.psum(small, ('bucket', 'seq'))]
    pallas_call x0 -> x2, Pallas kernels: none -> 57.9 us  [call_heads(): pl.pallas_call(kernel, grid=(heads,), in_specs=[pl.BlockSpec(memory_space...]
  transfers between devices with their start and end apart: 19 -> 100, of which waited for: 16 -> 43; matrix products, arithmetic and copies ran while one was open for 13% -> 35% of each run, Pallas kernels for 0% -> 5%
where the time goes in v1:
time: 1070 us; the launch traced here: 1060 us
  waiting for transfers between devices  326 us (30%)
  local copies, waits for them, and re-layouts  180 us (17%)
  starting transfers between devices  128 us (12%)
  other arithmetic  122 us (11%)
  matrix products  116 us (11%)
  blocking collectives  113 us (11%)
  Pallas kernels  57.9 us (5%)
  between operations  17.5 us (2%)
    ppermute x74, waiting for transfers between devices, flip(): return lax.ppermute(values, 'bucket', [(i, i ^ bits) for i in range(count)])  198 us
    psum x1, blocking collectives, per_device(): small = lax.psum(small, ('bucket', 'seq'))  77 us
    ppermute x74, starting transfers between devices, flip(): return lax.ppermute(values, 'bucket', [(i, i ^ bits) for i in range(count)])  66.8 us
    pallas_call x2, Pallas kernels, call_heads(): pl.pallas_call(kernel, grid=(heads,), in_specs=[pl.BlockSpec(memory_space...  57.9 us
    unnamed x258, local copies, waits for them, and re-layouts  50.3 us
    dot_general x8, matrix products, contract_rows(): lax.dot_general(leading, trailing, (((0,), (0,)), ((), ())), preferred_el...  46.6 us
    dot_general x9, matrix products, dense(): return jnp.dot(leading, trailing, preferred_element_type=wide)  35.6 us
    dot_general x8, matrix products, contract_cols(): lax.dot_general(leading, trailing, (((1,), (1,)), ((), ())), preferred_el...  32.3 us
  transfers between devices with their start and end apart: 100, of which 43 were waited for; matrix products, arithmetic and copies ran while one was open for 35% of the time, Pallas kernels for 5%

profile of v1, /device:TPU:4, one launch (start us, length us, event | category | flops | bytes accessed | tf_op | source)
XLA Modules:
  0.0 1060.5 jit_solution(16949223236224946629)
XLA Ops:
  108.5 14.5 %collective-permute-done = bf16[256,1536]{1,0:T(8,128)(2,1)} collective-permute-done((bf16[256,1536]{1,0:T(8,128)(2,1)}, bf16[256,1536]{1,0:T(8,128)(2,1)}, u32[]{:S(2)}, u32[]{:S(2)}) %collective-permute-start) | collective-permute-done | bytes 786464 | tf_op jit(solution)/shard_map/ppermute | solution.py:105
  142.1 29.5 %collective-permute-done.14 = bf16[512,1536]{1,0:T(8,128)(2,1)S(1)} collective-permute-done((bf16[512,1536]{1,0:T(8,128)(2,1)S(1)}, bf16[512,1536]{1,0:T(8,128)(2,1)S(1)}, u32[]{:S(2)}, u32[]{:S(2)}) %collective-permute-start.14) | collective-permute-done | bytes 1572896 | tf_op jit(solution)/shard_map/ppermute | solution.py:73
  207.0 9.3 fusion.82
  220.4 15.4 %psum.28 = f32[2,1024]{1,0:T(2,128)S(1)} all-reduce(f32[2,1024]{1,0:T(2,128)S(1)} %pad_maximum_fusion.13), channel_id=1, replica_groups=mesh['bucket'=8,'seq'=4] {'seq'}, use_global_device_ids=true, to_apply=%region_5.6 | all-reduce | flops 2048 | bytes 16384 | tf_op jit(solution)/shard_map/psum | solution.py:342
  288.6 25.3 %attend.1 = (bf16[6,64,1024]{2,1,0:T(8,128)(2,1)S(1)}, f32[6,1,1024]{2,1,0:T(1,128)S(1)}, f32[6,1,1024]{2,1,0:T(1,128)S(1)}) custom-call(s32[1]{0:T(128)S(6)} %copy.312.bucket, s32[4]{0:T(128)S(1)} %copy-done.5, f32[6]{0:T(128)S(1)} %dynamic_slice.88.gates, bf16[6,1024,64]{2,1,0:T(8,128)(2,1)S(1)} %maximum_multiply_fusion.q, ...), custom_call_target="tpu_custom_call" | custom-call | flops 2013265920 | bytes 16777216 | tf_op jit(solution)/shard_map/attend/pallas_call | solution.py:218
  317.1 10.5 all-to-all-start.4
  334.8 10.9 %all-to-all-done.4 = bf16[4,256,384]{2,1,0:T(8,128)(2,1)S(1)} async-done(((bf16[4,256,384]{2,1,0:T(8,128)(2,1)}), bf16[4,256,384]{2,1,0:T(8,128)(2,1)S(1)}, u32[]{:S(2)}, u32[]{:S(2)}) %all-to-all-start.4) | async-done | bytes 786464 | tf_op jit(solution)/shard_map/all_to_all | solution.py:387
  360.5 27.9 %all-to-all-done.5 = bf16[192,2,8,512]{3,1,0,2:T(2,128)(2,1)} async-done(((bf16[192,2,8,512]{3,1,0,2:T(2,128)(2,1)}), bf16[192,2,8,512]{3,1,0,2:T(2,128)(2,1)}, u32[]{:S(2)}, u32[]{:S(2)}) %all-to-all-start.5) | async-done | bytes 3145760 | tf_op jit(solution)/shard_map/all_to_all | solution.py:397
  407.7 8.5 collective-permute-done.18
  418.7 9.4 collective-permute-done.28
  449.6 14.9 %collective-permute-done.24 = bf16[256,1536]{1,0:T(8,128)(2,1)S(1)} collective-permute-done((bf16[256,1536]{1,0:T(8,128)(2,1)S(1)}, bf16[256,1536]{1,0:T(8,128)(2,1)S(1)}, u32[]{:S(2)}, u32[]{:S(2)}) %collective-permute-start.24) | collective-permute-done | bytes 786464 | tf_op jit(solution)/shard_map/ppermute | solution.py:73
  510.1 9.4 collective-permute-done.48
  558.0 11.1 %collective-permute-done.44 = bf16[256,1536]{1,0:T(8,128)(2,1)} collective-permute-done((bf16[256,1536]{1,0:T(8,128)(2,1)}, bf16[256,1536]{1,0:T(8,128)(2,1)}, u32[]{:S(2)}, u32[]{:S(2)}) %collective-permute-start.44) | collective-permute-done | bytes 786464 | tf_op jit(solution)/shard_map/ppermute | solution.py:73
  594.9 10.1 add_convert_fusion
  616.7 32.6 %attend_back.1 = (f32[6,64,1024]{2,1,0:T(8,128)S(1)}, f32[6,64,1024]{2,1,0:T(8,128)}, f32[6,1024,64]{2,1,0:T(8,128)}, f32[6,1024,64]{2,1,0:T(8,128)}, f32[6,4,25...) custom-call(s32[1]{0:T(128)S(6)} %copy.312.bucket, s32[4]{0:T(128)S(1)} %copy-done.5, ...), custom_call_target="tpu_custom_call" | custom-call | flops 5033164800 | bytes 16777216 | tf_op jit(solution)/shard_map/attend_back/pallas_call | solution.py:218
  689.6 10.2 psum.29
  710.9 8.7 convolution_convert_fusion
  719.6 8.9 collective-permute-done.56
  730.5 16.8 %collective-permute-done.57 = bf16[256,1536]{1,0:T(8,128)(2,1)S(1)} collective-permute-done((bf16[256,1536]{1,0:T(8,128)(2,1)S(1)}, bf16[256,1536]{1,0:T(8,128)(2,1)S(1)}, u32[]{:S(2)}, u32[]{:S(2)}) %collective-permute-start.57) | collective-permute-done | bytes 786464 | tf_op jit(solution)/shard_map/ppermute | solution.py:121
  790.6 22.5 %all-to-all-done.7 = bf16[4,2,256,384]{2,3,1,0:T(8,128)(2,1)S(1)} async-done(((bf16[4,2,256,384]{2,3,1,0:T(8,128)(2,1)}), bf16[4,2,256,384]{2,3,1,0:T(8,128)(2,1)S(1)}, u32[]{:S(2)}, u32[]{:S(2)}) %all-to-all-start.7) | async-done | bytes 1572896 | tf_op jit(solution)/shard_map/all_to_all | solution.py:489
  829.4 77.0 %psum.31 = f32[8,1536]{1,0:T(8,128)S(1)} all-reduce(f32[8,1536]{1,0:T(8,128)S(1)} %concatenate.109), channel_id=1, replica_groups=mesh['bucket'=8,'seq'=4] {'bucket','seq'}, use_global_device_ids=true, to_apply=%region_38.39 | all-reduce | flops 12288 | bytes 98304 | tf_op jit(solution)/shard_map/psum | solution.py:601
  915.6 12.6 %collective-permute-done.61 = bf16[256,1536]{0,1:T(8,128)(2,1)S(1)} collective-permute-done((bf16[256,1536]{0,1:T(8,128)(2,1)S(1)}, bf16[256,1536]{0,1:T(8,128)(2,1)S(1)}, u32[]{:S(2)}, u32[]{:S(2)}) %collective-permute-start.61) | collective-permute-done | bytes 786464 | tf_op jit(solution)/shard_map/ppermute | solution.py:73
  977.2 14.7 %collective-permute-done.75 = bf16[256,512]{1,0:T(8,128)(2,1)S(1)} collective-permute-done((bf16[256,512]{1,0:T(8,128)(2,1)S(1)}, bf16[256,512]{1,0:T(8,128)(2,1)S(1)}, u32[]{:S(2)}, u32[]{:S(2)}) %collective-permute-start.75) | collective-permute-done | bytes 262176 | tf_op jit(solution)/shard_map/ppermute | solution.py:73
  1019.7 10.4 all-gather
  (686 shorter events, 621.8 us)
Async XLA Ops:
  7.2 199.8 %all-gather.4.cloned.1.call-start = ((), (), s32[]{:S(2)}) async-start(), calls=%async_computation.16 | async-start | bytes 3981312 | tf_op jit(solution)/shard_map/all_gather | solution.py:281
  24.8 51.8 %all-to-all-start = ((bf16[4,8,192]{2,0,1:T(4,128)(2,1)}), bf16[4,8,192]{2,0,1:T(4,128)(2,1)S(1)}, u32[]{:S(2)}, u32[]{:S(2)}) async-start(bf16[4,8,192]{2,0,1:T(4,128)(2,1)} %copy.185), calls=%async_computation | async-start | bytes 32768 | tf_op jit(solution)/shard_map/all_to_all | solution.py:285
  65.9 57.1 %collective-permute-start.13 = (bf16[1024,1536]{1,0:T(8,128)(2,1)}, bf16[1024,1536]{1,0:T(8,128)(2,1)}, u32[]{:S(2)}, u32[]{:S(2)}) collective-permute-start(bf16[1024,1536]{1,0:T(8,128)(2,1)} %pad_maximum_fusion), channel_id=1, source_target_pairs={{0,4},{4,0},{8,12},{12,8},{16,20},{20,16},{24,28},{28,24},{1,5},{5... | collective-permute-start | bytes 9437192 | tf_op jit(solution)/shard_map/ppermute | solution.py:73
  76.4 50.5 %collective-permute-start.10 = (bf16[1024,1536]{0,1:T(8,128)(2,1)}, bf16[1024,1536]{0,1:T(8,128)(2,1)}, u32[]{:S(2)}, u32[]{:S(2)}) collective-permute-start(bf16[1024,1536]{0,1:T(8,128)(2,1)} %slice.432), channel_id=1, source_target_pairs={{0,4},{4,0},{8,12},{12,8},{16,20},{20,16},{24,28},{28,24},{1,5},{5... | collective-permute-start | bytes 9437192 | tf_op jit(solution)/shard_map/ppermute | solution.py:73
  94.2 257.9 %all-gather.6.cloned.1.call-start = ((), (), s32[]{:S(2)}) async-start(), calls=%async_computation.17 | async-start | bytes 5308416 | tf_op jit(solution)/shard_map/all_gather | solution.py:282
  125.8 45.7 %collective-permute-start.14 = (bf16[512,1536]{1,0:T(8,128)(2,1)S(1)}, bf16[512,1536]{1,0:T(8,128)(2,1)S(1)}, u32[]{:S(2)}, u32[]{:S(2)}) collective-permute-start(bf16[512,1536]{1,0:T(8,128)(2,1)S(1)} %slice.642), channel_id=1, source_target_pairs={{0,8},{4,12},{8,0},{12,4},{16,24},{20,28},{24,16},{28,20},{1,9},{5... | collective-permute-start | bytes 4718600 | tf_op jit(solution)/shard_map/ppermute | solution.py:73
  130.9 44.7 %collective-permute-start.11 = (bf16[512,1536]{0,1:T(8,128)(2,1)S(1)}, bf16[512,1536]{0,1:T(8,128)(2,1)S(1)}, u32[]{:S(2)}, u32[]{:S(2)}) collective-permute-start(bf16[512,1536]{0,1:T(8,128)(2,1)S(1)} %slice.643), channel_id=1, source_target_pairs={{0,16},{4,20},{8,24},{12,28},{16,0},{20,4},{24,8},{28,12},{1,17},{... | collective-permute-start | bytes 4718600 | tf_op jit(solution)/shard_map/ppermute | solution.py:73
  141.1 40.9 %collective-permute-start.2 = (bf16[256,1536]{1,0:T(8,128)(2,1)S(1)}, bf16[256,1536]{1,0:T(8,128)(2,1)S(1)}, u32[]{:S(2)}, u32[]{:S(2)}) collective-permute-start(bf16[256,1536]{1,0:T(8,128)(2,1)S(1)} %collective-permute-done.1), channel_id=1, source_target_pairs={{0,1},{1,2},{2,3},{3,0},{4,5},{5,6},{6,7},{7,4},{8,9},{9,10},{10,1... | collective-permute-start | bytes 2359304 | tf_op jit(solution)/shard_map/ppermute | solution.py:105
  202.3 59.4 %all-to-all-start.3 = ((bf16[4,2,256,384]{2,3,1,0:T(8,128)(2,1)}), bf16[4,2,256,384]{2,3,1,0:T(8,128)(2,1)}, u32[]{:S(2)}, u32[]{:S(2)}) async-start(bf16[4,2,256,384]{2,3,1,0:T(8,128)(2,1)} %maximum_bitcast_fusion.2), calls=%async_computation.3 | async-start | bytes 3145728 | tf_op jit(solution)/shard_map/all_to_all | solution.py:330
  345.7 42.7 %all-to-all-start.5 = ((bf16[192,2,8,512]{3,1,0,2:T(2,128)(2,1)}), bf16[192,2,8,512]{3,1,0,2:T(2,128)(2,1)}, u32[]{:S(2)}, u32[]{:S(2)}) async-start(bf16[192,2,8,512]{3,1,0,2:T(2,128)(2,1)} %copy.203), calls=%async_computation.5 | async-start | bytes 6291456 | tf_op jit(solution)/shard_map/all_to_all | solution.py:397
  351.4 437.1 %reduce-scatter.14.cloned.1.call-start = ((), (), s32[]{:S(2)}) async-start(), calls=%async_computation.23 | async-start | bytes 1966080 | tf_op jit(solution)/shard_map/reduce_scatter | solution.py:424
  358.6 38.3 %collective-permute-start.16 = (bf16[128,1536]{1,0:T(8,128)(2,1)S(1)}, bf16[128,1536]{1,0:T(8,128)(2,1)}, u32[]{:S(2)}, u32[]{:S(2)}) collective-permute-start(bf16[128,1536]{1,0:T(8,128)(2,1)S(1)} %get-tuple-element.133), channel_id=1, source_target_pairs={{0,8},{4,12},{8,0},{12,4},{16,24},{20,28},{24,16},{28,20},{1,9},{5... | collective-permute-start | bytes 1179656 | tf_op jit(solution)/shard_map/ppermute | solution.py:73
  594.9 228.2 %reduce-scatter.12.cloned.1.call-start = ((), (), s32[]{:S(2)}) async-start(), calls=%async_computation.22 | async-start | bytes 3932160 | tf_op jit(solution)/shard_map/reduce_scatter | solution.py:427
  605.1 404.2 %reduce-scatter.6.cloned.1.call-start = ((), (), s32[]{:S(2)}) async-start(), calls=%async_computation.19 | async-start | bytes 3981312 | tf_op jit(solution)/shard_map/reduce_scatter | solution.py:550
  774.9 38.2 %all-to-all-start.7 = ((bf16[4,2,256,384]{2,3,1,0:T(8,128)(2,1)}), bf16[4,2,256,384]{2,3,1,0:T(8,128)(2,1)S(1)}, u32[]{:S(2)}, u32[]{:S(2)}) async-start(bf16[4,2,256,384]{2,3,1,0:T(8,128)(2,1)} %reshape.450), calls=%async_computation.7 | async-start | bytes 3145728 | tf_op jit(solution)/shard_map/all_to_all | solution.py:489
  780.0 239.7 %all-reduce.17.cloned.1.call-start = ((), (), s32[]{:S(2)}) async-start(), calls=%async_computation.18 | async-start | bytes 196608 | tf_op jit(solution)/shard_map/psum | solution.py:571
  783.7 256.8 %reduce-scatter.10.cloned.1.call-start = ((), (), s32[]{:S(2)}) async-start(), calls=%async_computation.21 | async-start | bytes 4866048 | tf_op jit(solution)/shard_map/reduce_scatter | solution.py:448
  820.8 86.1 %collective-permute-start.59 = (bf16[256,1536]{0,1:T(8,128)(2,1)}, bf16[256,1536]{0,1:T(8,128)(2,1)S(1)}, u32[]{:S(2)}, u32[]{:S(2)}) collective-permute-start(bf16[256,1536]{0,1:T(8,128)(2,1)} %get-tuple-element.121), channel_id=1, source_target_pairs={{0,8},{4,12},{8,0},{12,4},{16,24},{20,28},{24,16},{28,20},{1,9},{5... | collective-permute-start | bytes 2359304 | tf_op jit(solution)/shard_map/ppermute | solution.py:73
  822.2 85.7 %collective-permute-start.66 = (bf16[256,1536]{0,1:T(8,128)(2,1)}, bf16[256,1536]{0,1:T(8,128)(2,1)S(1)}, u32[]{:S(2)}, u32[]{:S(2)}) collective-permute-start(bf16[256,1536]{0,1:T(8,128)(2,1)} %get-tuple-element.124), channel_id=1, source_target_pairs={{0,8},{4,12},{8,0},{12,4},{16,24},{20,28},{24,16},{28,20},{1,9},{5... | collective-permute-start | bytes 2359304 | tf_op jit(solution)/shard_map/ppermute | solution.py:73
  823.1 178.4 %all-to-all-start.10 = ((bf16[8,48,1024]{2,1,0:T(8,128)(2,1)}), bf16[8,48,1024]{2,1,0:T(8,128)(2,1)S(1)}, u32[]{:S(2)}, u32[]{:S(2)}) async-start(bf16[8,48,1024]{2,1,0:T(8,128)(2,1)} %reduce-scatter.12.cloned.1.call-done), calls=%async_computation.14 | async-start | bytes 1572864 | tf_op jit(solution)/shard_map/all_to_all | solution.py:434
  827.0 223.3 %reduce-scatter.8.cloned.1.call-start = ((), (), s32[]{:S(2)}) async-start(), calls=%async_computation.20 | async-start | bytes 3932160 | tf_op jit(solution)/shard_map/reduce_scatter | solution.py:505
  827.1 102.2 %collective-permute-start.62 = (bf16[256,1536]{0,1:T(8,128)(2,1)}, bf16[256,1536]{0,1:T(8,128)(2,1)}, u32[]{:S(2)}, u32[]{:S(2)}) collective-permute-start(bf16[256,1536]{0,1:T(8,128)(2,1)} %get-tuple-element.121), channel_id=1, source_target_pairs={{0,4},{4,0},{8,12},{12,8},{16,20},{20,16},{24,28},{28,24},{1,5},{5... | collective-permute-start | bytes 2359304 | tf_op jit(solution)/shard_map/ppermute | solution.py:73
  827.2 84.3 %collective-permute-start.60 = (bf16[256,1536]{0,1:T(8,128)(2,1)}, bf16[256,1536]{0,1:T(8,128)(2,1)}, u32[]{:S(2)}, u32[]{:S(2)}) collective-permute-start(bf16[256,1536]{0,1:T(8,128)(2,1)} %get-tuple-element.121), channel_id=1, source_target_pairs={{0,16},{4,20},{8,24},{12,28},{16,0},{20,4},{24,8},{28,12},{1,17},{... | collective-permute-start | bytes 2359304 | tf_op jit(solution)/shard_map/ppermute | solution.py:73
  827.6 81.3 %collective-permute-start.67 = (bf16[256,1536]{0,1:T(8,128)(2,1)}, bf16[256,1536]{0,1:T(8,128)(2,1)}, u32[]{:S(2)}, u32[]{:S(2)}) collective-permute-start(bf16[256,1536]{0,1:T(8,128)(2,1)} %get-tuple-element.124), channel_id=1, source_target_pairs={{0,16},{4,20},{8,24},{12,28},{16,0},{20,4},{24,8},{28,12},{1,17},{... | collective-permute-start | bytes 2359304 | tf_op jit(solution)/shard_map/ppermute | solution.py:73
  (174 other events, 2188.0 us)
Sparse Core Ops, SparseCore 0:
  16.4 46.2 all-gather.3
  104.7 51.2 all-gather.5
  558.1 33.4 reduce-scatter.13
  605.2 61.6 reduce-scatter.11
  719.8 49.2 reduce-scatter.5
  783.8 42.3 all-reduce.16
  832.6 110.9 reduce-scatter.9
  952.9 59.8 reduce-scatter.7

commit v2 on v1

v2 whole, which is shorter than its diff:
```python
from functools import partial

import jax
import jax.numpy as jnp
from jax import lax
from jax.experimental import pallas as pl
from jax.experimental.pallas import tpu as pltpu
from jax.sharding import PartitionSpec as P

EPSILON = 1e-06
NEGATIVE = -1e30
HIGHEST = lax.Precision.HIGHEST
wide = jnp.float32
narrow = jnp.bfloat16
VMEM_LIMIT = 50 * 2**20


def rms_norm(values, norm_gain):
    return (
        values * lax.rsqrt(jnp.mean(values * values, axis=-1, keepdims=True) + EPSILON) * norm_gain
    )


def dense(leading, trailing):
    return jnp.dot(leading, trailing, preferred_element_type=wide)


def contract_rows(leading, trailing):
    return lax.dot_general(
        leading, trailing, (((0,), (0,)), ((), ())), preferred_element_type=wide
    )


def contract_cols(leading, trailing):
    return lax.dot_general(
        leading, trailing, (((1,), (1,)), ((), ())), preferred_element_type=wide
    )


def pre_attention(tokens_in, modulated, norm_gains):
    model_width = tokens_in.shape[1]
    return rms_norm(tokens_in, norm_gains[0]) * (1.0 + modulated[:, :model_width])


def text_heads(text_pairs, gain):
    model_width = text_pairs.shape[1] // 2
    return (rms_norm(text_pairs[:, :model_width], gain), text_pairs[:, model_width:])


def post_attention(attended, tokens_in, modulated, norm_gains):
    model_width = tokens_in.shape[1]
    middle = tokens_in + jnp.tanh(modulated[:, model_width : 2 * model_width]) * rms_norm(
        attended, norm_gains[1]
    )
    normed_ffn = rms_norm(middle, norm_gains[2]) * (
        1.0 + modulated[:, 2 * model_width : 3 * model_width]
    )
    return (middle, normed_ffn)


def swiglu(gate_values):
    hidden_width = gate_values.shape[1] // 2
    return jax.nn.silu(gate_values[:, :hidden_width]) * gate_values[:, hidden_width:]


def finish(lowered, middle, modulated, norm_gains):
    model_width = middle.shape[1]
    return middle + jnp.tanh(modulated[:, 3 * model_width :]) * rms_norm(lowered, norm_gains[3])


MESH = pl.DeviceIdType.MESH


class Transfers:
    def __init__(self, send, arrive):
        self.send, self.arrive, self.used = send, arrive, 0
        self.open = []

    def start(self, source, target, device):
        copy = pltpu.make_async_remote_copy(
            src_ref=source,
            dst_ref=target,
            send_sem=self.send.at[self.used],
            recv_sem=self.arrive.at[self.used],
            device_id=device,
            device_id_type=MESH,
        )
        self.used += 1
        copy.start()
        self.open.append(copy)
        return copy

    def finish(self):
        for copy in self.open:
            copy.wait_send()


def meet(devices):
    barrier = pltpu.get_barrier_semaphore()
    for device in devices:
        pl.semaphore_signal(barrier, inc=1, device_id=device, device_id_type=MESH)
    pl.semaphore_wait(barrier, len(devices))


def partner(bits):
    return {"bucket": jnp.bitwise_xor(lax.axis_index("bucket"), bits)}


def outer_bits(count):
    return [1 << i for i in range(1, count.bit_length() - 1)]


def block_index(k, count):
    return (k >> 1) + (k & 1) * (count // 2)


def last_bit(block, order):
    return [bit for bit in order if block & bit][-1]


class PlaneExchange:
    def __init__(
        self, count, links, gathered, partial=None, arrived_core=None, arrived_outer=None, natural=False
    ):
        self.count, self.links, self.natural = count, links, natural
        self.index = lax.axis_index("bucket")
        self.gathered, self.partial = gathered, partial
        self.arrived_core, self.arrived_outer = arrived_core, arrived_outer
        bits = outer_bits(count)
        self.orders = (bits, bits[::-1])
        self.outer = [k for k in range(0, count, 2)]
        self.rows = gathered.shape[1] // 2
        self.coming, self.slots = {}, {}
        self.blocks = [0]

    def part(self, ref, block, half):
        return ref.at[block, pl.ds(half * self.rows, self.rows)]

    def place(self, block):
        return jnp.bitwise_xor(self.index, block) if self.natural else block_index(block, self.count)

    def onward(self, half, block, bit):
        source = self.place(block)
        target = source if self.natural else self.place(block | bit)
        self.coming[half, block | bit] = self.links.start(
            self.part(self.gathered, source, half),
            self.part(self.gathered, target, half),
            partner(bit),
        )

    def forward(self, half, block):
        order = self.orders[half]
        later = order if block == 0 else order[order.index(last_bit(block, order)) + 1 :]
        for bit in later:
            self.onward(half, block, bit)

    def forward_core(self, half, block):
        self.onward(half, block, 1)

    def arrive(self, block):
        for half in range(2):
            self.coming[half, block].wait_recv()

    def begin(self):
        for step in range(len(self.orders[0])):
            for half in range(2):
                self.onward(half, 0, self.orders[half][step])
        for half in range(2):
            self.forward_core(half, 0)

    def run_gather(self, compute, scatter=None):
        self.begin()
        compute([0])
        levels = len(self.orders[0])
        self.arrive(1)
        compute([block_index(1, self.count)])
        if scatter is not None:
            self.send_core(1)
        for level in range(1, levels + 1):
            here = [k for k in self.outer if bin(k).count("1") == level]
            steps = [(half, k) for k in here for half in range(2)]
            steps.sort(key=lambda s: [self.orders[s[0]].index(bit) for bit in self.orders[s[0]] if s[1] & bit][::-1])
            for half, k in steps:
                self.coming[half, k].wait_recv()
                self.forward(half, k)
                self.forward_core(half, k)
            if level == 2 and scatter is not None:
                next(scatter)
            compute([block_index(k, self.count) for k in here])
            for k in here:
                self.arrive(k | 1)
            compute([block_index(k | 1, self.count) for k in here])
            for k in here:
                if scatter is not None:
                    self.send_core(k | 1)

    def send_core(self, block):
        place = block_index(block, self.count)
        target = self.arrived_core.at[block >> 1]
        self.slots["core", block & ~1] = self.links.start(self.partial.at[place], target, partner(1))

    def total(self, half, block, slots):
        rows = pl.ds(half * self.rows, self.rows)
        value = self.partial[block >> 1, rows].astype(wide)
        value = value + self.arrived_core[block >> 1, rows].astype(wide)
        for slot in slots:
            value = value + self.arrived_outer[half, slot].astype(wide)
        return value

    def scatter(self, finish):
        slot_of = {}
        waiting = {(half, k): [] for half in range(2) for k in self.outer}
        core_seen = set()
        left = [list(self.outer), list(self.outer)]
        for step in range(len(self.orders[0])):
            jobs = []
            for half in range(2):
                bit = self.orders[half][::-1][step]
                jobs.append([(half, bit, k) for k in left[half] if k & bit])
                left[half] = [k for k in left[half] if not k & bit]
            for pair in zip(*jobs, strict=True):
                for half, bit, k in pair:
                    if k not in core_seen:
                        self.slots["core", k].wait_recv()
                        core_seen.add(k)
                    for copy, _ in waiting[half, k]:
                        copy.wait_recv()
                    rows = pl.ds(half * self.rows, self.rows)
                    total = self.total(half, k, [slot for _, slot in waiting[half, k]])
                    self.partial[k >> 1, rows] = total.astype(narrow)
                    slot = slot_of.setdefault((half, bit, k ^ bit), len([1 for h, *_ in slot_of if h == half]))
                    copy = self.links.start(
                        self.partial.at[k >> 1, rows], self.arrived_outer.at[half, slot], partner(bit)
                    )
                    waiting[half, k ^ bit].append((copy, slot))
                yield
        if 0 not in core_seen:
            self.slots["core", 0].wait_recv()
        for half in range(2):
            for copy, _ in waiting[half, 0]:
                copy.wait_recv()
            finish(half, self.total(half, 0, [slot for _, slot in waiting[half, 0]]))


def plane_partners(count):
    return [partner(bit) for bit in outer_bits(count) + [1]]


def plane_copies(count):
    outer = count // 2
    return 2 * (outer - 1) + 2 * outer, outer + 2 * (outer - 1)


def spans(blocks):
    runs = []
    for block in sorted(blocks):
        if runs and runs[-1][1] == block:
            runs[-1][1] = block + 1
        else:
            runs.append([block, block + 1])
    return runs


def each(blocks, body):
    for first, end in spans(blocks):
        if end - first == 1:
            body(first)
        else:
            lax.fori_loop(first, end, lambda i, _: (body(i), 0)[1], 0)


def ffn_kernel(
    count, x, gate_up, down, lowered, plane_out, values_out, hidden_out,
    plane, partial, core, outer, values, hidden, send, arrive, local,
):
    links = Transfers(send, arrive)
    meet(plane_partners(count))
    units = down.shape[0]
    wide_block = 256
    plane[0] = x[...]
    saved = pltpu.make_async_copy(plane, plane_out, local.at[0])

    def compute(blocks):
        def one(place):
            for start in range(0, units, wide_block):
                columns = slice(start, start + wide_block)
                after = slice(units + start, units + start + wide_block)
                gate = dense(plane[place], gate_up[:, columns])
                up = dense(plane[place], gate_up[:, after])
                values[place, :, columns] = gate
                values[place, :, after] = up
                hidden[place, :, columns] = (jax.nn.silu(gate) * up).astype(narrow)
            partial[place] = dense(hidden[place], down[...]).astype(narrow)

        each(blocks, one)

    exchange = PlaneExchange(count, links, plane, partial, core, outer)
    def finish(half, total):
        lowered[pl.ds(half * exchange.rows, exchange.rows)] = total

    sums = exchange.scatter(finish)
    exchange.run_gather(compute, sums)
    saved.start()
    kept = pltpu.make_async_copy(values, values_out, local.at[1])
    kept.start()
    held = pltpu.make_async_copy(hidden, hidden_out, local.at[2])
    held.start()

    for _ in sums:
        pass
    saved.wait()
    kept.wait()
    held.wait()
    links.finish()


def plane_scratch(count, rows, width):
    outer = count // 2
    return [
        pltpu.VMEM((count, rows, width), narrow),
        pltpu.VMEM((count, rows, width), narrow),
        pltpu.VMEM((outer, rows, width), narrow),
        pltpu.VMEM((2, outer - 1, rows // 2, width), narrow),
    ]


def ffn_forward(count, x, gate_up, down):
    rows, width = x.shape
    units = down.shape[0]
    copies = sum(plane_copies(count))
    vmem, anywhere = pl.BlockSpec(memory_space=pltpu.VMEM), pl.BlockSpec(memory_space=pl.ANY)
    return pl.pallas_call(
        partial(ffn_kernel, count),
        in_specs=[vmem] * 3,
        out_specs=[vmem] + [anywhere] * 3,
        out_shape=[
            jax.ShapeDtypeStruct((rows, width), wide),
            jax.ShapeDtypeStruct((count, rows, width), narrow),
            jax.ShapeDtypeStruct((count, rows, 2 * units), wide),
            jax.ShapeDtypeStruct((count, rows, units), narrow),
        ],
        scratch_shapes=plane_scratch(count, rows, width)
        + [
            pltpu.VMEM((count, rows, 2 * units), wide),
            pltpu.VMEM((count, rows, units), narrow),
            pltpu.SemaphoreType.DMA((copies,)),
            pltpu.SemaphoreType.DMA((copies,)),
            pltpu.SemaphoreType.DMA((3,)),
        ],
        compiler_params=pltpu.CompilerParams(
            collective_id=1, has_side_effects=True, vmem_limit_bytes=60 * 2**20
        ),
        name="ffn_forward",
    )(x, gate_up, down)

def ffn_back_kernel(
    count, g, gate_up, down, values_in, x_in, hidden_in, grad_normed, grad_gate_up, grad_down,
    plane, partial, core, outer, values, grads, taken, send, arrive, local,
):
    links = Transfers(send, arrive)
    fetch = pltpu.make_async_copy(values_in, values, local.at[2])
    fetch.start()
    meet(plane_partners(count))
    units, width = down.shape
    wide_block = 256
    plane[0] = g[...]
    fetched = []

    def compute(places):
        if not fetched:
            fetch.wait()
            fetched.append(True)

        def one(place):
            for start in range(0, units, wide_block):
                columns = slice(start, start + wide_block)
                after = slice(units + start, units + start + wide_block)
                back = contract_cols(plane[place], down[columns])
                gate, up = values[place, :, columns], values[place, :, after]
                sigma = jax.nn.sigmoid(gate)
                grads[place, :, columns] = (
                    back * up * (sigma * (1.0 + gate * (1.0 - sigma)))
                ).astype(narrow)
                grads[place, :, after] = (back * (gate * sigma)).astype(narrow)
            partial[place] = contract_cols(grads[place], gate_up[...]).astype(narrow)

        each(places, one)

    exchange = PlaneExchange(count, links, plane, partial, core, outer)

    def finish(half, total):
        grad_normed[pl.ds(half * exchange.rows, exchange.rows)] = total

    sums = exchange.scatter(finish)
    exchange.run_gather(compute, sums)

    jobs = [(x_in, grads, grad_gate_up, i) for i in range(width // wide_block)]
    jobs += [(hidden_in, plane, grad_down, i) for i in range(units // wide_block)]

    def take(number):
        source, _, _, i = jobs[number]
        columns = pl.ds(i * wide_block, wide_block)
        return pltpu.make_async_copy(
            source.at[:, :, columns], taken.at[number % 2], local.at[number % 2]
        )

    def work(number):
        if number + 1 < len(jobs):
            take(number + 1).start()
        take(number).wait()
        _, upstream, out, i = jobs[number]
        for start in range(0, upstream.shape[2], 512):
            columns = slice(start, start + 512)
            out[i * wide_block : (i + 1) * wide_block, columns] = contract_rows(
                flat(taken[number % 2]), flat(upstream[:, :, columns])
            ).astype(narrow)

    take(0).start()
    done = 0
    for _ in sums:
        for number in range(done, min(done + 3, len(jobs))):
            work(number)
            done += 1
    for number in range(done, len(jobs)):
        work(number)
    links.finish()


def ffn_backward(count, g, gate_up, down, values, x, hidden):
    rows, width = g.shape
    units = down.shape[0]
    copies = sum(plane_copies(count))
    vmem, anywhere = pl.BlockSpec(memory_space=pltpu.VMEM), pl.BlockSpec(memory_space=pl.ANY)
    return pl.pallas_call(
        partial(ffn_back_kernel, count),
        in_specs=[vmem] * 3 + [anywhere] * 3,
        out_specs=[vmem] * 3,
        out_shape=[
            jax.ShapeDtypeStruct((rows, width), wide),
            jax.ShapeDtypeStruct((width, 2 * units), narrow),
            jax.ShapeDtypeStruct((units, width), narrow),
        ],
        scratch_shapes=plane_scratch(count, rows, width)
        + [
            pltpu.VMEM((count, rows, 2 * units), wide),
            pltpu.VMEM((count, rows, 2 * units), narrow),
            pltpu.VMEM((2, count, rows, 256), narrow),
            pltpu.SemaphoreType.DMA((copies,)),
            pltpu.SemaphoreType.DMA((copies,)),
            pltpu.SemaphoreType.DMA((3,)),
        ],
        compiler_params=pltpu.CompilerParams(
            collective_id=2, has_side_effects=True, vmem_limit_bytes=62 * 2**20
        ),
        name="ffn_backward",
    )(g, gate_up, down, values, x, hidden)


def seq_device(index):
    return {"seq": index}


def mod_kernel(
    count, depth, pieces, columns, shard, words, got, mods, gathered, spread, product, back, send,
    arrive,
):
    links = Transfers(send, arrive)
    b, s = lax.axis_index("bucket"), lax.axis_index("seq")
    others = [partner(k) for k in range(1, count)]
    along = [seq_device(lax.rem(s + step, depth)) for step in range(1, depth)]
    meet(others + along)
    first = [
        links.start(pieces.at[jnp.bitwise_xor(b, k)], got.at[k], others[k - 1])
        for k in range(1, count)
    ]
    got[0] = pieces[b]
    gathered[b] = shard[...]
    exchange = PlaneExchange(count, links, gathered, natural=True)
    for copy in first:
        copy.wait_recv()
    for k in range(count):
        product[k] = dense(got[k].astype(narrow), columns[...])
    second = [links.start(product.at[k], back.at[k - 1], others[k - 1]) for k in range(1, count)]
    feature = spread.shape[2]

    def features(target):
        return words.at[:, pl.ds(pl.multiple_of(target * feature, 128), feature)]

    far = [
        links.start(features(jnp.bitwise_xor(b, k)), spread.at[b], others[k - 1])
        for k in range(1, count)
    ]
    spread[b] = words[:, pl.ds(pl.multiple_of(b * feature, 128), feature)]
    total = product[0]
    for k, copy in enumerate(second):
        copy.wait_recv()
        total = total + back[k]
    mods[s] = total
    third = [links.start(mods.at[s], mods.at[s], device) for device in along]
    exchange.run_gather(lambda places: None)
    for copy in third + far:
        copy.wait_recv()
    links.finish()


def modulate(count, depth, pieces, columns, shard, words):
    vmem = pl.BlockSpec(memory_space=pltpu.VMEM)
    places, width = pieces.shape[1], columns.shape[1]
    copies = 3 * (count - 1) + depth - 1 + plane_copies(count)[0]
    return pl.pallas_call(
        partial(mod_kernel, count, depth),
        in_specs=[vmem] * 4,
        out_specs=[vmem] * 4,
        out_shape=[
            jax.ShapeDtypeStruct(pieces.shape, wide),
            jax.ShapeDtypeStruct((depth, places, width), wide),
            jax.ShapeDtypeStruct((count,) + shard.shape, narrow),
            jax.ShapeDtypeStruct((count, words.shape[0], words.shape[1] // count), narrow),
        ],
        scratch_shapes=[
            pltpu.VMEM((count, places, width), wide),
            pltpu.VMEM((count - 1, places, width), wide),
            pltpu.SemaphoreType.DMA((copies,)),
            pltpu.SemaphoreType.DMA((copies,)),
        ],
        compiler_params=pltpu.CompilerParams(
            collective_id=3, has_side_effects=True, vmem_limit_bytes=32 * 2**20
        ),
        name="modulate",
    )(pieces, columns, shard, words)


def small_kernel(count, depth, values, out, along, send, arrive):
    links = Transfers(send, arrive)
    s = lax.axis_index("seq")
    others = [partner(k) for k in range(1, count)]
    line = [seq_device(lax.rem(s + step, depth)) for step in range(1, depth)]
    meet(others + line)
    first = [links.start(values, along.at[i], device) for i, device in enumerate(line)]
    total = values[...]
    for i, copy in enumerate(first):
        copy.wait_recv()
        total = total + along[i]
    out[0] = total
    second = [links.start(out.at[0], out.at[k], others[k - 1]) for k in range(1, count)]
    for copy in second:
        copy.wait_recv()
    links.finish()


def gather_small(count, depth, values, collective_id):
    vmem = pl.BlockSpec(memory_space=pltpu.VMEM)
    copies = count - 1 + depth - 1
    return pl.pallas_call(
        partial(small_kernel, count, depth),
        in_specs=[vmem],
        out_specs=vmem,
        out_shape=jax.ShapeDtypeStruct((count,) + values.shape, wide),
        scratch_shapes=[
            pltpu.VMEM((depth - 1,) + values.shape, wide),
            pltpu.SemaphoreType.DMA((copies,)),
            pltpu.SemaphoreType.DMA((copies,)),
        ],
        compiler_params=pltpu.CompilerParams(
            collective_id=collective_id, has_side_effects=True, vmem_limit_bytes=32 * 2**20
        ),
        name="gather_small",
    )(values)


class Ring:
    def __init__(self, depth, links):
        self.depth, self.links = depth, links
        self.index = lax.axis_index("seq")
        self.right = seq_device(lax.rem(self.index + 1, depth))
        self.left = seq_device(lax.rem(self.index + depth - 1, depth))

    def source(self, step):
        return lax.rem(self.index - step + 2 * self.depth, self.depth)


def start_kernel(
    count, depth, words, text, x, projection, pairs, normed, q, k, v,
    plane, partial, core, outer, send, arrive,
):
    links = Transfers(send, arrive)
    ring = Ring(depth, links)
    b = lax.axis_index("bucket")
    meet(plane_partners(count) + [ring.left, ring.right])
    own = q.shape[2]
    normed[ring.index] = x[...]
    moving = [links.start(x, normed.at[ring.index], ring.right)]

    def project(step):
        place = ring.source(step)
        for i, out in enumerate((q, k, v)):
            out[place] = dense(normed[place], projection[:, i * own : (i + 1) * own])

    def ring_step(step):
        moving[-1].wait_recv()
        place = ring.source(step)
        if step < depth - 1:
            moving.append(links.start(normed.at[place], normed.at[place], ring.right))
        project(step)

    exchange = PlaneExchange(count, links, plane, partial, core, outer)
    width = text.shape[1]

    def pair(block):
        source = words[jnp.bitwise_xor(b, block)]
        place = block_index(block, count)
        for first in range(0, width, 512):
            columns = slice(first, first + 512)
            partial[place, :, columns] = dense(source, text[:, columns]).astype(narrow)
        if block & 1:
            exchange.send_core(block)

    def finish(half, total):
        pairs[pl.ds(half * exchange.rows, exchange.rows)] = total

    sums = exchange.scatter(finish)
    order = sorted(exchange.outer, key=lambda block: (bin(block).count("1"), block))
    order = order[1:] + order[:1]
    levels = len(exchange.orders[0])
    for i, block in enumerate(order):
        pair(block | 1)
        pair(block)
        if i + 1 == levels:
            next(sums)
    project(0)
    step = 1
    for _ in sums:
        if step < depth:
            ring_step(step)
            step += 1
    while step < depth:
        ring_step(step)
        step += 1
    links.finish()


def start_exchange(count, depth, words, text, x, projection):
    vmem = pl.BlockSpec(memory_space=pltpu.VMEM)
    rows, width = x.shape
    own = projection.shape[1] // 3
    cap_rows, pair_width = words.shape[1], text.shape[1]
    copies = plane_copies(count)[1] + depth - 1
    raw = jax.ShapeDtypeStruct((depth, rows, own), wide)
    return pl.pallas_call(
        partial(start_kernel, count, depth),
        in_specs=[vmem] * 4,
        out_specs=[vmem] * 5,
        out_shape=[
            jax.ShapeDtypeStruct((cap_rows, pair_width), wide),
            jax.ShapeDtypeStruct((depth, rows, width), narrow),
            raw,
            raw,
            raw,
        ],
        scratch_shapes=[pltpu.VMEM((1, cap_rows, 128), narrow)]
        + plane_scratch(count, cap_rows, pair_width)[1:]
        + [pltpu.SemaphoreType.DMA((copies,)), pltpu.SemaphoreType.DMA((copies,))],
        compiler_params=pltpu.CompilerParams(
            collective_id=4, has_side_effects=True, vmem_limit_bytes=60 * 2**20
        ),
        name="start_exchange",
    )(words, text, x, projection)


def end_kernel(
    count, depth, pairs, text, words, grads, projection, normed, grad_words, share,
    plane, back, send_sum, ring_in, total, send_low, low_in, send, arrive,
):
    links = Transfers(send, arrive)
    ring = Ring(depth, links)
    b = lax.axis_index("bucket")
    others = [partner(k) for k in range(1, count)]
    meet(others + [ring.left, ring.right])
    plane[0] = pairs[...]
    exchange = PlaneExchange(count, links, plane, plane, plane, plane)
    feature = text.shape[0]
    width = text.shape[1]
    moving = []

    def round_step(step):
        value = contract_cols(grads[ring.source(step + 1)], projection[...])
        if step > 0:
            moving[-1].wait_recv()
            value = value + ring_in[step - 1].astype(wide)
        if step < depth - 1:
            send_sum[step] = value.astype(narrow)
            moving.append(links.start(send_sum.at[step], ring_in.at[step], ring.right))
        else:
            normed[...] = value

    steps = [0]

    def advance():
        if steps[0] < depth:
            round_step(steps[0])
            steps[0] += 1

    arriving = []
    blocks = [None] * count
    for block in range(count):
        blocks[block_index(block, count)] = block

    def compute(places):
        for place in places:
            block = blocks[place]
            for first in range(0, width, 512):
                columns = slice(first, first + 512)
                part = dense(words[jnp.bitwise_xor(b, block)], plane[place, :, columns])
                if place == 0:
                    total[:, columns] = part
                else:
                    total[:, columns] += part
            value = contract_cols(plane[place], text[...]).astype(narrow)
            if block == 0:
                grad_words[b] = value
            else:
                back[place - 1] = value
                arriving.append(
                    links.start(back.at[place - 1], grad_words.at[b], others[block - 1])
                )
        advance()

    exchange.run_gather(compute)
    while steps[0] < depth:
        advance()
    low_rows = feature // depth
    going = []
    for step in range(depth):
        rows = pl.ds(pl.multiple_of(ring.source(step + 1) * low_rows, low_rows), low_rows)
        value = total[rows]
        if step > 0:
            going[-1].wait_recv()
            value = value + low_in[step - 1].astype(wide)
        if step < depth - 1:
            send_low[step] = value.astype(narrow)
            going.append(links.start(send_low.at[step], low_in.at[step], ring.right))
        else:
            share[...] = value
    for copy in arriving:
        copy.wait_recv()
    links.finish()


def end_exchange(count, depth, pairs, text, words, grads, projection):
    vmem = pl.BlockSpec(memory_space=pltpu.VMEM)
    cap_rows, pair_width = pairs.shape
    feature = text.shape[0]
    rows, width = grads.shape[1], projection.shape[0]
    copies = plane_copies(count)[0] + count - 1 + 2 * (depth - 1)
    quarter = (depth - 1, feature // depth, pair_width)
    return pl.pallas_call(
        partial(end_kernel, count, depth),
        in_specs=[vmem] * 5,
        out_specs=[vmem] * 3,
        out_shape=[
            jax.ShapeDtypeStruct((rows, width), wide),
            jax.ShapeDtypeStruct((count, cap_rows, feature), narrow),
            jax.ShapeDtypeStruct((feature // depth, pair_width), wide),
        ],
        scratch_shapes=[
            pltpu.VMEM((count, cap_rows, pair_width), narrow),
            pltpu.VMEM((count - 1, cap_rows, feature), narrow),
            pltpu.VMEM((depth - 1, rows, width), narrow),
            pltpu.VMEM((depth - 1, rows, width), narrow),
            pltpu.VMEM((feature, pair_width), wide),
            pltpu.VMEM(quarter, narrow),
            pltpu.VMEM(quarter, narrow),
            pltpu.SemaphoreType.DMA((copies,)),
            pltpu.SemaphoreType.DMA((copies,)),
        ],
        compiler_params=pltpu.CompilerParams(
            collective_id=5, has_side_effects=True, vmem_limit_bytes=60 * 2**20
        ),
        name="end_exchange",
    )(pairs, text, words, grads, projection)


def head_lanes(values, head, size):
    lane = lax.broadcasted_iota(jnp.int32, values.shape, 1)
    return jnp.where((lane >= head * size) & (lane < (head + 1) * size), values, 0)


def swap_halves(values, size):
    half = size // 2
    lanes = values.shape[1]
    if lanes % 128 == 0:
        lane = lax.broadcasted_iota(jnp.int32, values.shape, 1)
        ahead = pltpu.roll(values, lanes - half, 1)
        behind = pltpu.roll(values, half, 1)
        return jnp.where(lax.rem(lane, size) < half, ahead, behind)
    parts = []
    for start in range(0, lanes, size):
        parts.append(values[:, start + half : start + size])
        parts.append(values[:, start : start + half])
    return jnp.concatenate(parts, axis=1)


def turn(values, cosine, signed_sine, size):
    return values * cosine + swap_halves(values, size) * signed_sine


def flat(values):
    return values.reshape(-1, values.shape[-1])


def scalar_spec():
    return pl.BlockSpec(memory_space=pltpu.SMEM)


def row_sums(values):
    ones = jnp.ones((8, values.shape[1]), wide)
    return lax.dot_general(
        ones, values, (((1,), (1,)), ((), ())), precision=HIGHEST, preferred_element_type=wide
    )[:1]


def loop(count, body):
    if count == 1:
        body(0)
    else:
        lax.fori_loop(0, count, lambda i, _: (body(i), 0)[1], 0)


def lane_block(index, lanes):
    if isinstance(index, int):
        return pl.ds(index * lanes, lanes)
    return pl.ds(pl.multiple_of(index * lanes, 128), lanes)


def block_rows_of(index, rows):
    if isinstance(index, int):
        return pl.ds(index * rows, rows)
    return pl.ds(pl.multiple_of(index * rows, 128), rows)


def forward_kernel(
    count, depth, size, lanes, spans, lengths, gates, raw_q, raw_k, raw_v, gain_q, gain_k, cosine,
    sine, text_own, gate_up, combined, q, k, v, qc, total, cross_total, rates, text, gathered,
    stat, stat_in, self_out, staged, send, arrive, local,
):
    links = Transfers(send, arrive)
    b, s = lax.axis_index("bucket"), lax.axis_index("seq")
    others = [partner(k) for k in range(1, count)]
    turns = [lax.rem(s + step, depth) for step in range(1, depth)]
    along = [seq_device(place) for place in turns]
    meet(others + along)
    block_rows, own = raw_q.shape[1:]
    rows = depth * block_rows
    width = own * depth
    grid, heads = own // lanes, lanes // size
    scaling = size ** (-0.5)
    for i, raw in enumerate((raw_q, raw_k)):
        for block in range(depth):
            place = i * depth + block
            stat[place : place + 1] = row_sums(raw[block] * raw[block])
    stats = [links.start(stat, stat_in.at[i], device) for i, device in enumerate(along)]
    words = [
        links.start(text_own.at[place], text.at[s], device)
        for place, device in zip(turns, along, strict=True)
    ]
    text[s] = text_own[s]
    gate_rows, units = gate_up.shape[0], gathered.shape[1] // 2
    half_width = gate_up.shape[1] // 2
    here = pl.ds(pl.multiple_of(b * gate_rows, 16), gate_rows)
    weights, kept = [], []
    for block in range(count):
        target = jnp.bitwise_xor(b, block)
        for half in range(2):
            source = gate_up.at[
                :, pl.ds(pl.multiple_of(half * half_width + target * units, 128), units)
            ]
            landing = gathered.at[here, pl.ds(half * units, units)]
            if block:
                weights.append(links.start(source, landing, others[block - 1]))
            else:
                copy = pltpu.make_async_copy(source, landing, local.at[half])
                copy.start()
                kept.append(copy)
    for block in range(depth):
        v[block_rows_of(block, block_rows)] = raw_v[block].astype(narrow)
    squares = stat[...]
    for i, copy in enumerate(stats):
        copy.wait_recv()
        squares = squares + stat_in[i]
    rates[...] = lax.rsqrt(squares / width + EPSILON)
    columns = rates[...].T
    for block in range(depth):
        at = block_rows_of(block, block_rows)
        cos, sin = cosine[at], sine[at]
        for group in range(grid):
            span = lane_block(group, lanes)
            norm_q = raw_q[block, :, span] * columns[:, block : block + 1] * gain_q[:, span]
            norm_k = (
                raw_k[block, :, span]
                * columns[:, depth + block : depth + block + 1]
                * gain_k[:, span]
            )
            turned = turn(norm_q, cos, sin, size).astype(narrow).astype(wide)
            q[at, span] = (turned * scaling).astype(narrow)
            qc[at, span] = (norm_q.astype(narrow).astype(wide) * scaling).astype(narrow)
            k[at, span] = turn(norm_k, cos, sin, size).astype(narrow)
    key_index = lax.broadcasted_iota(jnp.int32, (rows, block_rows), 0)

    def attend_self(group):
        span = lane_block(group, lanes)
        value_t = v[:, span].astype(wide).T.astype(narrow)
        for block in range(depth):
            at = block_rows_of(block, block_rows)
            allowed = (key_index >= spans[0, block]) & (key_index < spans[1, block])
            outs = []
            for head in range(heads):
                scores = contract_cols(k[:, span], head_lanes(q[at, span], head, size))
                scores = jnp.where(allowed, scores, NEGATIVE)
                peak = jnp.max(scores, axis=0, keepdims=True)
                shares = jnp.exp(scores - peak)
                mass = jnp.sum(shares, axis=0, keepdims=True)
                part = slice(head * size, (head + 1) * size)
                outs.append(dense(value_t[part], shares.astype(narrow)) / mass)
                total[group, head : head + 1, at] = peak + jnp.log(mass)
            self_out[at, span] = jnp.concatenate(outs, axis=0).T

    loop(grid, attend_self)
    for copy in words:
        copy.wait_recv()
    cap = text.shape[0] * text.shape[3]
    cap_index = lax.broadcasted_iota(jnp.int32, (cap, block_rows), 0)
    results = []
    for step in range(depth):
        block = lax.rem(s + 1 + step, depth)
        at = block_rows_of(block, block_rows)
        clip = spans[2, block]
        live = cap_index < lengths[clip]

        def attend_cross(group):
            span = lane_block(group, lanes)
            text_key = flat(text[:, 0, clip, :, span])
            value_t = flat(text[:, 1, clip, :, span]).astype(wide).T.astype(narrow)
            outs = []
            for head in range(heads):
                scores = contract_cols(text_key, head_lanes(qc[at, span], head, size))
                scores = jnp.where(live, scores, NEGATIVE)
                peak = jnp.max(scores, axis=0, keepdims=True)
                shares = jnp.exp(scores - peak)
                mass = jnp.sum(shares, axis=0, keepdims=True)
                part = slice(head * size, (head + 1) * size)
                gate = gates[group * heads + head]
                outs.append(dense(value_t[part], shares.astype(narrow)) * (gate / mass))
                cross_total[group, head : head + 1, at] = peak + jnp.log(mass)
            staged[step, :, span] = (
                self_out[at, span] + jnp.concatenate(outs, axis=0).T
            ).astype(narrow)

        loop(grid, attend_cross)
        if step < depth - 1:
            results.append(links.start(staged.at[step], combined.at[s], along[step]))
        else:
            combined[s] = staged[step]
    for copy in results + weights:
        copy.wait_recv()
    for copy in kept:
        copy.wait()
    links.finish()


def attention_forward(
    count, depth, size, lanes, scalars, raws, gains, angles, text_own, gate_up
):
    block_rows, own = raws[0].shape[1:]
    rows = depth * block_rows
    grid, heads = own // lanes, lanes // size
    vmem, anywhere = pl.BlockSpec(memory_space=pltpu.VMEM), pl.BlockSpec(memory_space=pl.ANY)
    units = gate_up.shape[1] // (2 * count)
    copies = 3 * (depth - 1) + 2 * (count - 1)
    row_block = jax.ShapeDtypeStruct((rows, own), narrow)
    totals = jax.ShapeDtypeStruct((grid, heads, rows), wide)
    return pl.pallas_call(
        partial(forward_kernel, count, depth, size, lanes),
        in_specs=[scalar_spec()] * 3 + [vmem] * 8 + [anywhere],
        out_specs=[vmem] * 10,
        out_shape=[
            jax.ShapeDtypeStruct((depth, block_rows, own), narrow),
            row_block,
            row_block,
            row_block,
            row_block,
            totals,
            totals,
            jax.ShapeDtypeStruct((2 * depth, block_rows), wide),
            jax.ShapeDtypeStruct(text_own.shape, narrow),
            jax.ShapeDtypeStruct((count * gate_up.shape[0], 2 * units), narrow),
        ],
        scratch_shapes=[
            pltpu.VMEM((2 * depth, block_rows), wide),
            pltpu.VMEM((depth - 1, 2 * depth, block_rows), wide),
            pltpu.VMEM((rows, own), wide),
            pltpu.VMEM((depth, block_rows, own), narrow),
            pltpu.SemaphoreType.DMA((copies,)),
            pltpu.SemaphoreType.DMA((copies,)),
            pltpu.SemaphoreType.DMA((2,)),
        ],
        compiler_params=pltpu.CompilerParams(
            collective_id=8, has_side_effects=True, vmem_limit_bytes=60 * 2**20
        ),
        name="attention_forward",
    )(*scalars, *raws, *gains, *angles, text_own, gate_up)


def backward_kernel(
    count, depth, size, lanes, spans, lengths, gates, upstream, weight, q, k, v, qc, raw_q, raw_k,
    rates, gain_q, gain_k, cosine, sine, text, total, cross_total, small, projected, gain_sums,
    dgate, grad_text, small_out, go, send_go, dqc, back_q, back_k, parts, send_text, stat,
    stat_in, along_in, sum_k, sum_v, send, arrive,
):
    links = Transfers(send, arrive)
    s = lax.axis_index("seq")
    others = [partner(k) for k in range(1, count)]
    turns = [lax.rem(s + step, depth) for step in range(1, depth)]
    along = [seq_device(place) for place in turns]
    meet(others + along)
    block_rows, own = upstream.shape[0], q.shape[1]
    rows = depth * block_rows
    width = own * depth
    grid, heads = own // lanes, lanes // size
    scaling = size ** (-0.5)
    smalls = [links.start(small, along_in.at[i], device) for i, device in enumerate(along)]

    def grad_out(place):
        at = pl.ds(pl.multiple_of(place * own, 64), own)
        return contract_cols(upstream[...], weight[at]).astype(narrow)

    arriving = []
    for i, (place, device) in enumerate(zip(turns, along, strict=True)):
        send_go[i] = grad_out(place)
        arriving.append(links.start(send_go.at[i], go.at[s], device))
    go[s] = grad_out(s)

    cap_local = text.shape[3]
    cap = text.shape[0] * cap_local
    places = text.shape[2]
    cap_index = lax.broadcasted_iota(jnp.int32, (cap, block_rows), 0)
    clips = []
    for step in range(depth):
        block = lax.rem(s - step + depth, depth)
        if step:
            arriving[step - 1].wait_recv()
        at = block_rows_of(block, block_rows)
        clip = spans[2, block]
        clips.append(clip)
        live = cap_index < lengths[clip]

        def back_cross(group):
            span = lane_block(group, lanes)
            text_key = flat(text[:, 0, clip, :, span])
            text_value = flat(text[:, 1, clip, :, span])
            key_t = text_key.astype(wide).T.astype(narrow)
            grads = []
            for head in range(heads):
                gate = gates[group * heads + head]
                query = head_lanes(qc[at, span], head, size)
                grad = head_lanes(go[block, :, span], head, size)
                scores = contract_cols(text_key, query)
                scores = jnp.where(live, scores, NEGATIVE)
                shares = jnp.exp(scores - cross_total[group, head : head + 1, at])
                grad_shares = contract_cols(text_value, grad)
                row = jnp.sum(grad_shares * shares, axis=0, keepdims=True)
                grad_scores = (gate * (shares * (grad_shares - row))).astype(narrow)
                grad_key = dense(grad_scores, query)
                grad_value = gate * dense(shares.astype(narrow), grad)
                if head == 0:
                    parts[step, 0, :, span] = grad_key
                    parts[step, 1, :, span] = grad_value
                else:
                    parts[step, 0, :, span] += grad_key
                    parts[step, 1, :, span] += grad_value
                part = slice(head * size, (head + 1) * size)
                grads.append(dense(key_t[part], grad_scores) * scaling)
                if step == 0:
                    dgate[group, head : head + 1] = row
                else:
                    dgate[group, head : head + 1] += row
            dqc[at, span] = jnp.concatenate(grads, axis=0).T

        loop(grid, back_cross)
    for which in range(2):
        for place in range(places):
            for target in range(depth):
                at = pl.ds(target * cap_local, cap_local)
                value = jnp.zeros((cap_local, own), wide)
                for step in range(depth):
                    value = value + jnp.where(
                        clips[step] == place, parts[step, which, at], 0.0
                    )
                send_text[target, which, place] = value.astype(narrow)
    words = [
        links.start(send_text.at[place], grad_text.at[s], device)
        for place, device in zip(turns, along, strict=True)
    ]
    grad_text[s] = send_text[s]
    sums = small[...]
    for i, copy in enumerate(smalls):
        copy.wait_recv()
        sums = sums + along_in[i]
    small_out[0] = sums
    spread = [links.start(small_out.at[0], small_out.at[k], others[k - 1]) for k in range(1, count)]

    key_index = lax.broadcasted_iota(jnp.int32, (rows, block_rows), 0)

    def back_self(group):
        span = lane_block(group, lanes)
        key_t = k[:, span].astype(wide).T.astype(narrow)
        for block in range(depth):
            at = block_rows_of(block, block_rows)
            allowed = (key_index >= spans[0, block]) & (key_index < spans[1, block])
            grads = []
            for head in range(heads):
                query = head_lanes(q[at, span], head, size)
                grad = head_lanes(go[block, :, span], head, size)
                scores = contract_cols(k[:, span], query)
                scores = jnp.where(allowed, scores, NEGATIVE)
                shares = jnp.exp(scores - total[group, head : head + 1, at])
                grad_shares = contract_cols(v[:, span], grad)
                row = jnp.sum(grad_shares * shares, axis=0, keepdims=True)
                grad_scores = (shares * (grad_shares - row)).astype(narrow)
                if block == 0 and head == 0:
                    sum_v[...] = dense(shares.astype(narrow), grad)
                    sum_k[...] = dense(grad_scores, query)
                else:
                    sum_v[...] += dense(shares.astype(narrow), grad)
                    sum_k[...] += dense(grad_scores, query)
                part = slice(head * size, (head + 1) * size)
                grads.append(dense(key_t[part], grad_scores) * scaling)
            back = jnp.concatenate(grads, axis=0).T
            back_q[at, span] = turn(back, cosine[at], -sine[at], size) + dqc[at, span]
        back_k[:, span] = turn(sum_k[...], cosine[...], -sine[...], size)
        for block in range(depth):
            at = block_rows_of(block, block_rows)
            if isinstance(group, int):
                to = pl.ds(2 * own + group * lanes, lanes)
            else:
                to = pl.ds(pl.multiple_of(2 * own + group * lanes, 128), lanes)
            projected[block, :, to] = sum_v[at].astype(narrow)

    loop(grid, back_self)
    columns = rates[...].T
    pairs = ((raw_q, back_q, gain_q), (raw_k, back_k, gain_k))
    for i, (raw, back, gain) in enumerate(pairs):
        gains = jnp.zeros((1, own), wide)
        for block in range(depth):
            place = i * depth + block
            at = block_rows_of(block, block_rows)
            hat = raw[block] * columns[:, place : place + 1]
            gains = gains + jnp.sum(back[at] * hat, axis=0, keepdims=True)
            stat[place : place + 1] = row_sums(back[at] * gain[...] * hat)
        gain_sums[i : i + 1] = gains
    stats = [links.start(stat, stat_in.at[i], device) for i, device in enumerate(along)]
    means = stat[...]
    for i, copy in enumerate(stats):
        copy.wait_recv()
        means = means + stat_in[i]
    means = (means / width).T
    for i, (raw, back, gain) in enumerate(pairs):
        for block in range(depth):
            place = slice(i * depth + block, i * depth + block + 1)
            at = block_rows_of(block, block_rows)
            rate = columns[:, place]
            hat = raw[block] * rate
            projected[block, :, i * own : (i + 1) * own] = (
                rate * (back[at] * gain[...] - hat * means[:, place])
            ).astype(narrow)
    for copy in words + spread:
        copy.wait_recv()
    links.finish()


def attention_backward(
    count, depth, size, lanes, scalars, upstream, weight, saved, raws, rates, gains, angles, text,
    totals, small,
):
    block_rows, own = raws[0].shape[1:]
    rows = depth * block_rows
    grid, heads = own // lanes, lanes // size
    vmem = pl.BlockSpec(memory_space=pltpu.VMEM)
    copies = 4 * (depth - 1) + count - 1
    cap = text.shape[0] * text.shape[3]
    args = (*scalars, upstream, weight, *saved, *raws, rates, *gains, *angles, text, *totals, small)
    return pl.pallas_call(
        partial(backward_kernel, count, depth, size, lanes),
        in_specs=[scalar_spec()] * 3 + [vmem] * (len(args) - 3),
        out_specs=[vmem] * 5,
        out_shape=[
            jax.ShapeDtypeStruct((depth, block_rows, 3 * own), narrow),
            jax.ShapeDtypeStruct((2, own), wide),
            jax.ShapeDtypeStruct((grid, heads, block_rows), wide),
            jax.ShapeDtypeStruct(text.shape, narrow),
            jax.ShapeDtypeStruct((count,) + small.shape, wide),
        ],
        scratch_shapes=[
            pltpu.VMEM((depth, block_rows, own), narrow),
            pltpu.VMEM((depth - 1, block_rows, own), narrow),
            pltpu.VMEM((rows, own), wide),
            pltpu.VMEM((rows, own), wide),
            pltpu.VMEM((rows, own), wide),
            pltpu.VMEM((depth, 2, cap, own), wide),
            pltpu.VMEM(text.shape, narrow),
            pltpu.VMEM((2 * depth, block_rows), wide),
            pltpu.VMEM((depth - 1, 2 * depth, block_rows), wide),
            pltpu.VMEM((depth - 1,) + small.shape, wide),
            pltpu.VMEM((rows, lanes), wide),
            pltpu.VMEM((rows, lanes), wide),
            pltpu.SemaphoreType.DMA((copies,)),
            pltpu.SemaphoreType.DMA((copies,)),
        ],
        compiler_params=pltpu.CompilerParams(
            collective_id=9, has_side_effects=True, vmem_limit_bytes=60 * 2**20
        ),
        name="attention_backward",
    )(*args)


def per_device(
    tokens,
    condition,
    captions,
    caption_lengths,
    null_flags,
    slot_buckets,
    null_caption,
    modulation,
    projection,
    text_weight,
    output_weight,
    gate_up,
    down_weight,
    norm_gains,
    head_gains,
    cross_gates,
    cotangent,
):
    count_s, count_b = lax.axis_size("seq"), lax.axis_size("bucket")
    s, b = lax.axis_index("seq"), lax.axis_index("bucket")
    assert count_s % 4 == 0
    local, width = tokens.shape
    heads = cross_gates.shape[0]
    size = width // heads
    own_heads = heads // count_s
    own = width // count_s
    rows = local * count_s
    places, cap_local, text_width = captions.shape
    cap_rows = places * cap_local
    bucket = slot_buckets[0]
    clip_length = jnp.where(
        bucket == 0, rows // 4, jnp.where(bucket == 1, rows // 2, rows)
    ).astype(jnp.int32)

    own_hidden = down_weight.shape[0]
    gate_rows = gate_up.shape[0]
    text_rows = text_weight.shape[0]
    null_rows = lax.dynamic_slice_in_dim(null_caption, s * cap_local, cap_local, 0)
    is_null = null_flags[:, None, None] == 1
    words_own = jnp.where(is_null, null_rows[None], captions).reshape(cap_rows, text_width)
    own_projection = jnp.concatenate(
        [
            lax.dynamic_slice_in_dim(projection, i * width + s * own, own, 1)
            for i in range(3)
        ],
        axis=1,
    )

    silu_cond = jax.nn.silu(condition).astype(narrow)
    mod_width = modulation.shape[1] // count_s
    pieces = silu_cond.astype(wide).reshape(places, count_b, -1).transpose(1, 0, 2)
    cond_columns, mods, own_projection, words = modulate(
        count_b,
        count_s,
        pieces,
        lax.dynamic_slice_in_dim(modulation, s * mod_width, mod_width, 1),
        own_projection,
        words_own,
    )
    own_projection = own_projection.reshape(width, 3 * own)
    my_clip = (s * local) // clip_length
    modulated = lax.dynamic_index_in_dim(mods, my_clip, 1, keepdims=False).reshape(1, 4 * width)

    tokens_in = tokens.astype(wide)
    normed_full, pre_pull = jax.vjp(pre_attention, tokens_in, modulated, norm_gains)
    normed_low = normed_full.astype(narrow)
    text_pairs, normed, raw_q, raw_k, raw_v = start_exchange(
        count_b, count_s, words, text_weight, normed_low, own_projection
    )
    text_outs, text_pull = jax.vjp(text_heads, text_pairs, head_gains[2])
    text_own = jnp.stack([o.astype(narrow).reshape(cap_rows, count_s, own) for o in text_outs])
    text_own = text_own.transpose(2, 0, 1, 3).reshape(count_s, 2, places, cap_local, own)

    gains = [lax.dynamic_slice_in_dim(head_gains[i : i + 1], s * own, own, 1) for i in range(2)]
    inside = lax.rem(jnp.arange(rows, dtype=jnp.int32), clip_length)
    half = size // 2
    frequency = 10000.0 ** (-jnp.arange(half, dtype=wide) / half)
    angles = inside.astype(wide)[:, None] * frequency[None, :]
    lanes = 128 if own % 128 == 0 else own
    block_heads = lanes // size
    cosine = jnp.tile(jnp.cos(angles), (1, 2 * block_heads))
    sine = jnp.tile(
        jnp.concatenate([-jnp.sin(angles), jnp.sin(angles)], axis=1), (1, block_heads)
    )
    tanh_gates = jnp.tanh(cross_gates)
    own_gates = lax.dynamic_slice_in_dim(tanh_gates, s * own_heads, own_heads, 0)
    clip_of = (jnp.arange(count_s, dtype=jnp.int32) * local) // clip_length
    spans = jnp.stack([clip_of * clip_length, (clip_of + 1) * clip_length, clip_of])
    scalars = (spans, caption_lengths, own_gates)
    full_output, text_own = lax.optimization_barrier((output_weight, text_own))
    full_output = lax.all_gather(full_output, "bucket", axis=0, tiled=True)
    combined, *saved, total, cross_total, rates, text_kv, own_gate_up = attention_forward(
        count_b,
        count_s,
        size,
        lanes,
        scalars,
        (raw_q, raw_k, raw_v),
        gains,
        (cosine, sine),
        text_own,
        gate_up,
    )
    combined = combined.transpose(1, 0, 2).reshape(local, width)

    attended = dense(combined, full_output)
    (middle, ffn_full), post_pull = jax.vjp(
        post_attention, attended, tokens_in, modulated, norm_gains
    )
    normed_ffn = ffn_full.astype(narrow)

    lowered, plane, gate_values, hidden = ffn_forward(
        count_b, normed_ffn, own_gate_up, down_weight
    )
    mixed, finish_pull = jax.vjp(finish, lowered, middle, modulated, norm_gains)
    grad_lowered, grad_middle, grad_modulated_last, grad_norm_last = finish_pull(
        cotangent.astype(wide)
    )
    grad_lowered_low = grad_lowered.astype(narrow)
    grad_normed_ffn, grad_gate_up, grad_down = ffn_backward(
        count_b, grad_lowered_low, own_gate_up, down_weight, gate_values, plane, hidden
    )
    down_share = lax.psum_scatter(
        grad_down, "seq", scatter_dimension=0, tiled=True
    ).astype(wide)
    gate_share = lax.psum_scatter(
        grad_gate_up.reshape(count_b, gate_rows, 2 * own_hidden),
        "seq",
        scatter_dimension=1,
        tiled=True,
    )
    share_rows = gate_rows // count_s
    gate_share = lax.all_to_all(gate_share, "bucket", 0, 0, tiled=True)
    gate_share = (
        gate_share.reshape(count_b, share_rows, 2, own_hidden)
        .transpose(1, 2, 0, 3)
        .reshape(share_rows, 2 * count_b * own_hidden)
        .astype(wide)
    )

    grad_attended, grad_tokens_post, grad_modulated_post, grad_norm_post = post_pull(
        (grad_middle, grad_normed_ffn)
    )
    grad_attended_low = grad_attended.astype(narrow)
    grad_output = contract_rows(combined, grad_attended_low).astype(narrow)
    output_share = lax.psum_scatter(
        grad_output, ("bucket", "seq"), scatter_dimension=0, tiled=True
    ).astype(wide)
    own_place = jnp.arange(places, dtype=jnp.int32)[:, None] == my_clip
    grad_rows = (grad_modulated_post + grad_modulated_last)[:, width:].reshape(3, 1, width)
    grad_projected, gain_sums, grad_gates, grad_kv, early = attention_backward(
        count_b,
        count_s,
        size,
        lanes,
        scalars,
        grad_attended_low,
        full_output,
        saved,
        (raw_q, raw_k),
        rates,
        gains,
        (cosine, sine),
        text_kv,
        (total, cross_total),
        jnp.where(own_place[None], grad_rows, 0.0).reshape(3 * places, width),
    )
    early = early.reshape(count_b, 3, places, width)

    grad_kv = grad_kv.reshape(count_s, 2, cap_rows, own)
    grad_kv = grad_kv.transpose(1, 2, 0, 3).reshape(2, cap_rows, width).astype(wide)
    grad_pairs, grad_gain_text = text_pull((grad_kv[0], grad_kv[1]))
    grad_pairs_low = grad_pairs.astype(narrow)
    grad_normed, grad_words, text_share = end_exchange(
        count_b,
        count_s,
        grad_pairs_low,
        text_weight,
        words.transpose(0, 2, 1),
        grad_projected,
        own_projection,
    )
    grad_words = grad_words.transpose(1, 0, 2).reshape(places, cap_local, text_width)
    grad_captions = jnp.where(is_null, 0.0, grad_words.astype(wide))
    null_local = jnp.sum(jnp.where(is_null, grad_words.astype(wide), 0.0), axis=0).astype(narrow)
    null_share = lax.all_to_all(null_local, "bucket", 0, 0, tiled=True)
    null_share = jnp.sum(null_share.reshape(count_b, -1, text_width).astype(wide), axis=0)
    null_share = lax.ppermute(
        null_share,
        ("bucket", "seq"),
        [(i * count_s + j, j * count_b + i) for i in range(count_b) for j in range(count_s)],
    )

    grad_projection = contract_rows(flat(normed), flat(grad_projected)).astype(narrow)
    proj_share = lax.all_to_all(grad_projection, "bucket", 0, 0, tiled=True)
    proj_share = jnp.sum(
        proj_share.reshape(count_b, -1, 3 * own).astype(wide), axis=0
    ).astype(narrow)
    proj_share = lax.all_to_all(proj_share.reshape(count_s, -1, 3 * own), "seq", 0, 0, tiled=True)
    proj_share = (
        proj_share.reshape(count_s, -1, 3, own)
        .transpose(1, 2, 0, 3)
        .reshape(-1, 3 * width)
        .astype(wide)
    )
    grad_tokens_pre, grad_modulated_pre, grad_norm_pre = pre_pull(grad_normed)
    grad_tokens = grad_tokens_pre + grad_tokens_post

    share = width // (count_b * count_s)
    def place(values):
        return lax.dynamic_update_slice_in_dim(jnp.zeros((width,), wide), values, s * own, 0)

    gate_sums = lax.dynamic_update_slice_in_dim(
        jnp.zeros((heads,), wide),
        jnp.sum(grad_gates, axis=2).reshape(own_heads) * (1.0 - own_gates * own_gates),
        s * own_heads,
        0,
    )
    small = jnp.concatenate(
        [
            jnp.where(own_place, grad_modulated_pre[:, :width], 0.0),
            grad_norm_pre + grad_norm_post + grad_norm_last,
            jnp.stack(
                [
                    place(gain_sums[0]),
                    place(gain_sums[1]),
                    grad_gain_text,
                    jnp.pad(gate_sums, (0, width - heads)),
                ]
            ),
        ],
        axis=0,
    )
    small = gather_small(count_b, count_s, small, 7)
    grad_mod_rows = jnp.concatenate([small[:, None, :places], early], axis=1)
    cond_own = lax.dynamic_slice_in_dim(cond_columns, s * share, share, 2)
    mod_share = lax.dot_general(
        flat(cond_own),
        grad_mod_rows.transpose(0, 2, 1, 3).reshape(count_b * places, 4 * width),
        (((0,), (0,)), ((), ())),
        precision=HIGHEST,
    )
    sums = jnp.sum(small[:, places:], axis=0)
    own_sums = lax.dynamic_slice_in_dim(sums, (b * count_s + s) * share, share, 1)
    return (
        mixed.astype(narrow),
        grad_tokens,
        grad_captions,
        null_share,
        mod_share,
        proj_share,
        text_share,
        output_share,
        gate_share,
        down_share,
        own_sums[:4],
        own_sums[4:7],
        sums[7, :heads],
    )


def solution(mesh):
    whole = P(("bucket", "seq"), None)
    shard = P("bucket", None)
    return jax.shard_map(
        per_device,
        mesh=mesh,
        in_specs=(
            whole,
            shard,
            P("bucket", "seq", None),
            P("bucket"),
            P("bucket"),
            P("bucket"),
            P(),
            shard,
            shard,
            shard,
            shard,
            shard,
            shard,
            P(),
            P(),
            P(),
            whole,
        ),
        out_specs=(
            whole,
            whole,
            P("bucket", "seq", None),
            whole,
            whole,
            whole,
            whole,
            whole,
            whole,
            whole,
            P(None, ("bucket", "seq")),
            P(None, ("bucket", "seq")),
            P(),
        ),
        check_vma=False,
    )
```

time: 1070 us -> 819 us (0.77)
  Pallas kernels: 57.9 us -> 627 us
  waiting for transfers between devices: 326 us -> 18.7 us
  local copies, waits for them, and re-layouts: 180 us -> 50.6 us
  blocking collectives: 113 us -> 0 us
  starting transfers between devices: 128 us -> 22 us
  matrix products: 116 us -> 18.4 us
  other arithmetic: 122 us -> 56.2 us
    pallas_call x2 -> x8, Pallas kernels: 57.9 us -> 627 us  [the longest x1 169 us: end_exchange(): pl.pallas_call(partial(end_kernel, count, depth), in_specs=[vmem] * 5, ou...]
    ppermute x80 -> x0, waiting for transfers between devices: 245 us -> none  [the longest x74 198 us: flip(): return lax.ppermute(values, 'bucket', [(i, i ^ bits) for i in range(count)])]
    psum x3 -> x0, blocking collectives: 103 us -> none  [the longest x1 77 us: per_device(): small = lax.psum(small, ('bucket', 'seq'))]
    all_to_all x8 -> x1, waiting for transfers between devices: 73.8 us -> 0.01 us  [per_device(): proj_share = lax.all_to_all(grad_projection, 'bucket', 0, 0, tiled=True)]
    ppermute x80 -> x0, starting transfers between devices: 67.9 us -> none  [the longest x74 66.8 us: flip(): return lax.ppermute(values, 'bucket', [(i, i ^ bits) for i in range(count)])]
    all_to_all x8 -> x1, starting transfers between devices: 44.1 us -> 5.02 us  [per_device(): proj_share = lax.all_to_all(grad_projection, 'bucket', 0, 0, tiled=True)]
    unnamed x258 -> x60, local copies, waits for them, and re-layouts: 50.3 us -> 11.7 us
    reshape x14 -> x1, local copies, waits for them, and re-layouts: 38 us -> 0.08 us  [per_device(): jnp.sum(grad_gates, axis=2).reshape(own_heads)]
  transfers between devices with their start and end apart: 100 -> 9, of which waited for: 43 -> 3; matrix products, arithmetic and copies ran while one was open for 35% -> 10% of each run, Pallas kernels for 5% -> 46%
where the time goes in v2:
time: 819 us; the launch traced here: 809 us
  Pallas kernels  627 us (77%)
  other arithmetic  56.2 us (7%)
  local copies, waits for them, and re-layouts  50.6 us (6%)
  starting transfers between devices  22 us (3%)
  waiting for transfers between devices  18.7 us (2%)
  matrix products  18.4 us (2%)
  between operations  15.4 us (2%)
    pallas_call x1, Pallas kernels, end_exchange(): pl.pallas_call(partial(end_kernel, count, depth), in_specs=[vmem] * 5, ou...  169 us
    pallas_call x1, Pallas kernels, attention_backward(): pl.pallas_call(partial(backward_kernel, count, depth, size, lanes), in_sp...  114 us
    pallas_call x1, Pallas kernels, start_exchange(): pl.pallas_call(partial(start_kernel, count, depth), in_specs=[vmem] * 4,...  73.9 us
    pallas_call x1, Pallas kernels, ffn_backward(): pl.pallas_call(partial(ffn_back_kernel, count), in_specs=[vmem] * 3 + [an...  68.5 us
    pallas_call x1, Pallas kernels, attention_forward(): pl.pallas_call(partial(forward_kernel, count, depth, size, lanes), in_spe...  64.6 us
    pallas_call x1, Pallas kernels, ffn_forward(): pl.pallas_call(partial(ffn_kernel, count), in_specs=[vmem] * 3, out_specs...  62.9 us
    pallas_call x1, Pallas kernels, modulate(): pl.pallas_call(partial(mod_kernel, count, depth), in_specs=[vmem] * 4, ou...  50.9 us
    pallas_call x1, Pallas kernels, gather_small(): pl.pallas_call(partial(small_kernel, count, depth), in_specs=[vmem], out_...  23.5 us
  transfers between devices with their start and end apart: 9, of which 3 were waited for; matrix products, arithmetic and copies ran while one was open for 10% of the time, Pallas kernels for 46%

profile of v2, /device:TPU:4, one launch (start us, length us, event | category | flops | bytes accessed | tf_op | source)
XLA Modules:
  0.0 808.7 jit_solution(16374837804404556536)
XLA Ops:
  14.7 50.9 %modulate.1 = (f32[8,4,192]{2,1,0:T(4,128)S(1)}, f32[4,4,1536]{2,1,0:T(4,128)S(1)}, bf16[8,192,1152]{2,1,0:T(8,128)(2,1)S(1)}, bf16[8,256,512]{2,1,0:T(8,128)(2,1)S(1)}) custom-call(f32[8,4,192]{2,1,0:T(4,128)S(1)} %bitcast.66, bf16[192,1536]{1,0:T(8,128)(2,1)S(1)} %constant_dynamic-slice_fusion.9.columns, bf16[192,1152]{1,0:T(8,128)(2,1)S(1)} %pad_maximum_fusion.shard, ...), custom_call_target="tpu_custom_call" | custom-call | tf_op jit(solution)/shard_map/modulate/pallas_call | solution.py:510
  70.1 73.9 %start_exchange.1 = (f32[256,3072]{1,0:T(8,128)}, bf16[4,256,1536]{2,1,0:T(8,128)(2,1)}, f32[4,256,384]{2,1,0:T(8,128)}, f32[4,256,384]{2,1,0:T(8,128)}, f32[4,256,384]{2,1,0:T(8,128)}) custom-call(bf16[8,256,512]{2,1,0:T(8,128)(2,1)} %copy-done.1, bf16[512,3072]{1,0:T(8,128)(2,1)} %text.3, bf16[256,1536]{1,0:T(8,128)(2,1)} %fusion.10.x, ...), custom_call_target="tpu_custom_call" | custom-call | tf_op jit(solution)/shard_map/start_exchange/pallas_call | solution.py:649
  159.8 64.6 %attention_forward.1 = (bf16[4,256,384]{2,1,0:T(8,128)(2,1)}, bf16[1024,384]{1,0:T(8,128)(2,1)}, bf16[1024,384]{1,0:T(8,128)(2,1)}, bf16[1024,384]{1,0:T(8,128)(...) custom-call(s32[3,4]{1,0:T(4,128)} %pad_add_fusion.3.spans, ...), custom_call_target="tpu_custom_call" | custom-call | tf_op jit(solution)/shard_map/attention_forward/pallas_call | solution.py:981
  225.8 4.1 multiply_reduce_fusion.10
  232.4 62.9 %ffn_forward.1 = (f32[256,1536]{1,0:T(8,128)}, bf16[8,256,1536]{2,1,0:T(8,128)(2,1)}, f32[8,256,1024]{2,1,0:T(8,128)}, bf16[8,256,512]{2,1,0:T(8,128)(2,1)}) custom-call(bf16[256,1536]{1,0:T(8,128)(2,1)} %multiply_convert_fusion.x, bf16[1536,1024]{1,0:T(8,128)(2,1)} %get-tuple-element.59.gate_up, bf16[512,1536]{1,0:T(8,128)(2,1)} %down.3), custom_call_target="tpu_custom_call" | custom-call | tf_op jit(solution)/shard_map/ffn_forward/pallas_call | solution.py:332
  300.3 68.5 %ffn_backward.1 = (f32[256,1536]{1,0:T(8,128)}, bf16[1536,1024]{1,0:T(8,128)(2,1)}, bf16[512,1536]{1,0:T(8,128)(2,1)}) custom-call(bf16[256,1536]{1,0:T(8,128)(2,1)} %get-tuple-element.117.g, bf16[1536,1024]{1,0:T(8,128)(2,1)} %get-tuple-element.59.gate_up, bf16[512,1536]{1,0:T(8,128)(2,1)} %down.3, f32[8,256,1024]{2,1,0:T(8,128)} %get-tuple-element.61.values_in, ...), custom_call_target="tpu_custom_call" | custom-call | tf_op jit(solution)/shard_map/ffn_backward/pallas_call | solution.py:434
  376.2 4.4 multiply_reduce_fusion.1
  384.2 113.9 %attention_backward.1 = (bf16[4,256,1152]{2,1,0:T(8,128)(2,1)}, f32[2,384]{1,0:T(2,128)}, f32[3,2,256]{2,1,0:T(2,128)}, bf16[4,2,4,64,384]{4,3,2,1,0:T(8,128)(2,1)}, f32[8,12,1536]{2,1,0:T(8,128)}) custom-call(s32[3,4]{1,0:T(4,128)} %pad_add_fusion.3.spans, s32[4]{0:T(128)} %lengths.3, f32[6]{0:T(128)} %dynamic_slice.40.gates, ...), custom_call_target="tpu_custom_call" | custom-call | tf_op jit(solution)/shard_map/attention_backward/pallas_call | solution.py:1191
  499.0 8.7 %fusion = bf16[1536,1152]{1,0:T(8,128)(2,1)} fusion(bf16[4,256,1536]{2,1,0:T(8,128)(2,1)} %get-tuple-element.81, bf16[4,256,1152]{2,1,0:T(8,128)(2,1)} %get-tuple-element.74.grads), kind=kOutput, calls=%fused_computation.1 | convolution fusion | flops 3625648128 | bytes 9043968 | tf_op jit(solution)/shard_map/dot_general | solution.py:29
  507.6 5.0 all-to-all-start.1
  518.1 3.5 convolution_convert_fusion
  527.1 169.2 %end_exchange.1 = (f32[256,1536]{1,0:T(8,128)}, bf16[8,256,512]{2,1,0:T(8,128)(2,1)}, f32[128,3072]{1,0:T(8,128)}) custom-call(bf16[256,3072]{1,0:T(8,128)(2,1)} %add_convert_fusion.pairs, bf16[512,3072]{1,0:T(8,128)(2,1)} %text.3, bf16[8,512,256]{2,1,0:T(8,128)(2,1)} %bitcast.70, bf16[4,256,1152]{2,1,0:T(8,128)(2,1)} %get-tuple-element.74.grads, ...), custom_call_target="tpu_custom_call" | custom-call | tf_op jit(solution)/shard_map/end_exchange/pallas_call | solution.py:756
  699.0 23.5 %gather_small.1 = f32[8,12,1536]{2,1,0:T(8,128)S(1)} custom-call(f32[12,1536]{1,0:T(8,128)S(1)} %concatenate.14.values), custom_call_target="tpu_custom_call" | custom-call | tf_op jit(solution)/shard_map/gather_small/pallas_call | solution.py:554
  725.5 4.4 copy.76
  729.9 5.0 reshape.355
  734.9 6.0 select_reduce_fusion
  740.9 5.1 all-to-all-start
  747.1 3.4 reduce_sum.281
  750.4 3.9 all-to-all-done
  754.3 4.0 all-to-all-start.2
  758.4 3.5 fusion.17
  761.9 7.2 all-to-all-done.2
  769.1 5.8 all-to-all-start.3
  782.3 7.5 collective-permute-done
  (185 shorter events, 84.4 us)
Async XLA Ops:
  7.2 218.6 %all-gather.2.cloned.1.call-start = ((), (), s32[]{:S(2)}) async-start(), calls=%async_computation.7 | async-start | bytes 5308416 | tf_op jit(solution)/shard_map/all_gather | solution.py:1316
  11.9 2.4 copy-start.16
  14.6 54.1 %copy-start.23 = (f32[4,1536]{1,0:T(4,128)S(1)}, f32[4,1536]{1,0:T(4,128)}, u32[]{:S(2)}) copy-start(f32[4,1536]{1,0:T(4,128)} %param.30) | copy-start | bytes 73732
  14.7 54.2 %copy-start.5 = (bf16[256,1536]{1,0:T(8,128)(2,1)S(1)}, bf16[256,1536]{1,0:T(8,128)(2,1)}, u32[]{:S(2)}) copy-start(bf16[256,1536]{1,0:T(8,128)(2,1)} %param.17) | copy-start | bytes 2359300
  144.0 3.3 copy-start.24
  144.0 3.3 copy-start.6
  154.9 614.2 %reduce-scatter.6.cloned.1.call-start = ((), (), s32[]{:S(2)}) async-start(), calls=%async_computation.9 | async-start | bytes 3932160 | tf_op jit(solution)/shard_map/reduce_scatter | solution.py:1351
  225.7 4.1 copy-start.14
  231.0 67.3 %copy-start.3 = (f32[256,1536]{1,0:T(8,128)}, f32[256,1536]{1,0:T(8,128)S(1)}, u32[]{:S(2)}) copy-start(f32[256,1536]{1,0:T(8,128)S(1)} %get-tuple-element.109) | copy-start | bytes 4718596
  232.4 64.7 %copy-start.12 = (bf16[256,1536]{1,0:T(8,128)(2,1)S(1)}, bf16[256,1536]{1,0:T(8,128)(2,1)}, u32[]{:S(2)}) copy-start(bf16[256,1536]{1,0:T(8,128)(2,1)} %param.33) | copy-start | bytes 2359300
  368.8 421.0 %reduce-scatter.8.cloned.1.call-start = ((), (), s32[]{:S(2)}) async-start(), calls=%async_computation.10 | async-start | bytes 1966080 | tf_op jit(solution)/shard_map/reduce_scatter | solution.py:1348
  373.1 3.0 copy-start.4
  373.1 3.0 copy-start.9
  507.6 5.0 copy-start.20
  507.6 233.3 %all-to-all-start.1 = ((bf16[8,192,1152]{2,1,0:T(8,128)(2,1)}), bf16[8,192,1152]{2,1,0:T(8,128)(2,1)}, u32[]{:S(2)}, u32[]{:S(2)}) async-start(bf16[8,192,1152]{2,1,0:T(8,128)(2,1)} %bitcast.79), calls=%async_computation.1 | async-start | bytes 7077888 | tf_op jit(solution)/shard_map/all_to_all | solution.py:1420
  512.6 281.4 %reduce-scatter.4.cloned.1.call-start = ((), (), s32[]{:S(2)}) async-start(), calls=%async_computation.8 | async-start | bytes 4866048 | tf_op jit(solution)/shard_map/reduce_scatter | solution.py:1371
  696.3 2.5 copy-start.25
  740.9 13.4 %all-to-all-start = ((bf16[8,8,4096]{2,1,0:T(8,128)(2,1)}), bf16[8,8,4096]{2,1,0:T(8,128)(2,1)S(1)}, u32[]{:S(2)}, u32[]{:S(2)}) async-start(bf16[8,8,4096]{2,1,0:T(8,128)(2,1)} %bitcast.52), calls=%async_computation | async-start | bytes 1048576 | tf_op jit(solution)/shard_map/all_to_all | solution.py:1411
  754.3 7.6 copy-start.17
  754.3 14.8 %all-to-all-start.2 = ((bf16[4,48,1152]{2,1,0:T(8,128)(2,1)}), bf16[4,48,1152]{2,1,0:T(8,128)(2,1)S(1)}, u32[]{:S(2)}, u32[]{:S(2)}) async-start(bf16[4,48,1152]{2,1,0:T(8,128)(2,1)} %bitcast.22), calls=%async_computation.2 | async-start | bytes 884736 | tf_op jit(solution)/shard_map/all_to_all | solution.py:1424
  758.4 16.5 %copy-start.22 = (f32[8,1536]{1,0:T(8,128)}, f32[8,1536]{1,0:T(8,128)S(1)}, u32[]{:S(2)}) copy-start(f32[8,1536]{1,0:T(8,128)S(1)} %slice_reduce_fusion) | copy-start | bytes 147460
  769.1 26.5 %all-to-all-start.3 = ((bf16[8,48,1024]{2,1,0:T(8,128)(2,1)}), bf16[8,48,1024]{2,1,0:T(8,128)(2,1)S(1)}, u32[]{:S(2)}, u32[]{:S(2)}) async-start(bf16[8,48,1024]{2,1,0:T(8,128)(2,1)} %reduce-scatter.6.cloned.1.call-done), calls=%async_computation.5 | async-start | bytes 1572864 | tf_op jit(solution)/shard_map/all_to_all | solution.py:1358
  779.1 10.7 %collective-permute-start = (f32[8,4096]{1,0:T(8,128)S(1)}, f32[8,4096]{1,0:T(8,128)S(1)}, u32[]{:S(2)}, u32[]{:S(2)}) collective-permute-start(f32[8,4096]{1,0:T(8,128)S(1)} %convert_reduce_fusion), channel_id=1, source_target_pairs={{0,0},{1,8},{2,16},{3,24},{4,1},{5,9},{6,17},{7,25},{8,2},{9,10},{... | collective-permute-start | bytes 393224 | tf_op jit(solution)/shard_map/ppermute | solution.py:1413
  798.1 2.7 copy-start.19
  (12 other events, 19.2 us)
Sparse Core Ops, SparseCore 0:
  155.0 52.4 all-gather.1
  369.0 82.5 reduce-scatter.5
  453.8 60.8 reduce-scatter.7
  521.8 174.0 reduce-scatter.3

commit v3 on v2

--- a/solution.py
+++ b/solution.py
@@ -120,7 +120,8 @@
 
 class PlaneExchange:
     def __init__(
-        self, count, links, gathered, partial=None, arrived_core=None, arrived_outer=None, natural=False
+        self, count, links, gathered=None, partial=None, arrived_core=None, arrived_outer=None,
+        natural=False,
     ):
         self.count, self.links, self.natural = count, links, natural
         self.index = lax.axis_index("bucket")
@@ -129,7 +130,7 @@
         bits = outer_bits(count)
         self.orders = (bits, bits[::-1])
         self.outer = [k for k in range(0, count, 2)]
-        self.rows = gathered.shape[1] // 2
+        self.rows = (partial if gathered is None else gathered).shape[1] // 2
         self.coming, self.slots = {}, {}
         self.blocks = [0]
 
@@ -178,12 +179,7 @@
             self.send_core(1)
         for level in range(1, levels + 1):
             here = [k for k in self.outer if bin(k).count("1") == level]
-            steps = [(half, k) for k in here for half in range(2)]
-            steps.sort(key=lambda s: [self.orders[s[0]].index(bit) for bit in self.orders[s[0]] if s[1] & bit][::-1])
-            for half, k in steps:
-                self.coming[half, k].wait_recv()
-                self.forward(half, k)
-                self.forward_core(half, k)
+            self.forward_level(here)
             if level == 2 and scatter is not None:
                 next(scatter)
             compute([block_index(k, self.count) for k in here])
@@ -194,14 +190,35 @@
                 if scatter is not None:
                     self.send_core(k | 1)
 
+    def gather(self):
+        self.begin()
+        yield
+        for level in range(1, len(self.orders[0]) + 1):
+            self.forward_level([k for k in self.outer if bin(k).count("1") == level])
+            yield
+        for block in self.outer:
+            self.arrive(block | 1)
+
+    def forward_level(self, here):
+        steps = [(half, k) for k in here for half in range(2)]
+        steps.sort(
+            key=lambda s: [
+                self.orders[s[0]].index(bit) for bit in self.orders[s[0]] if s[1] & bit
+            ][::-1]
+        )
+        for half, k in steps:
+            self.coming[half, k].wait_recv()
+            self.forward(half, k)
+            self.forward_core(half, k)
+
     def send_core(self, block):
-        place = block_index(block, self.count)
+        place = self.place(block)
         target = self.arrived_core.at[block >> 1]
         self.slots["core", block & ~1] = self.links.start(self.partial.at[place], target, partner(1))
 
     def total(self, half, block, slots):
         rows = pl.ds(half * self.rows, self.rows)
-        value = self.partial[block >> 1, rows].astype(wide)
+        value = self.partial[self.place(block), rows].astype(wide)
         value = value + self.arrived_core[block >> 1, rows].astype(wide)
         for slot in slots:
             value = value + self.arrived_outer[half, slot].astype(wide)
@@ -227,10 +244,12 @@
                         copy.wait_recv()
                     rows = pl.ds(half * self.rows, self.rows)
                     total = self.total(half, k, [slot for _, slot in waiting[half, k]])
-                    self.partial[k >> 1, rows] = total.astype(narrow)
+                    self.partial[self.place(k), rows] = total.astype(narrow)
                     slot = slot_of.setdefault((half, bit, k ^ bit), len([1 for h, *_ in slot_of if h == half]))
                     copy = self.links.start(
-                        self.partial.at[k >> 1, rows], self.arrived_outer.at[half, slot], partner(bit)
+                        self.partial.at[self.place(k), rows],
+                        self.arrived_outer.at[half, slot],
+                        partner(bit),
                     )
                     waiting[half, k ^ bit].append((copy, slot))
                 yield
@@ -426,6 +445,39 @@
     links.finish()
 
 
+class GradientRing:
+    def __init__(self, ring, own, held):
+        self.ring, self.own, self.held = ring, own, held
+        self.copies = []
+
+    def piece(self, which, step):
+        place = self.ring.source(step + 1)
+        return self.own[0].at[:, place] if which == 0 else self.own[1].at[place]
+
+    def first(self, landing):
+        for which in range(2):
+            self.copies.append(
+                self.ring.links.start(self.piece(which, 0), landing[which], self.ring.right)
+            )
+
+    def arrived(self):
+        for copy in self.copies:
+            copy.wait_recv()
+        self.copies = []
+
+    def value(self, which, step):
+        return self.piece(which, step)[...].astype(wide) + self.held[which][...].astype(wide)
+
+    def onward(self, step, going, landing):
+        self.arrived()
+        for which in range(2):
+            going[which][...] = self.value(which, step).astype(narrow)
+            self.copies.append(
+                self.ring.links.start(going[which], landing[which], self.ring.right)
+            )
+        self.held = landing
+
+
 def ffn_backward(count, g, gate_up, down, values, x, hidden):
     rows, width = g.shape
     units = down.shape[0]
@@ -460,11 +512,24 @@
     return {"seq": index}
 
 
-def mod_kernel(
-    count, depth, pieces, columns, shard, words, got, mods, gathered, spread, product, back, send,
-    arrive,
+class Ring:
+    def __init__(self, depth, links):
+        self.depth, self.links = depth, links
+        self.index = lax.axis_index("seq")
+        self.right = seq_device(lax.rem(self.index + 1, depth))
+        self.left = seq_device(lax.rem(self.index + depth - 1, depth))
+
+    def source(self, step):
+        return lax.rem(self.index - step + 2 * self.depth, self.depth)
+
+
+def start_kernel(
+    count, depth, clip, pieces, columns, shard, words, text, x, gain,
+    got, mods, projection, spread, pairs, normed, q, k, v, rates,
+    product, back, stat, stat_in, partial, core, outer, send, arrive,
 ):
     links = Transfers(send, arrive)
+    ring = Ring(depth, links)
     b, s = lax.axis_index("bucket"), lax.axis_index("seq")
     others = [partner(k) for k in range(1, count)]
     along = [seq_device(lax.rem(s + step, depth)) for step in range(1, depth)]
@@ -474,202 +539,161 @@
         for k in range(1, count)
     ]
     got[0] = pieces[b]
-    gathered[b] = shard[...]
-    exchange = PlaneExchange(count, links, gathered, natural=True)
+    feature, width = text.shape
+
+    def features(target):
+        return words.at[:, pl.ds(pl.multiple_of(target * feature, 128), feature)]
+
+    projection[b] = shard[...]
+    spread[b] = words[:, pl.ds(pl.multiple_of(b * feature, 128), feature)]
     for copy in first:
         copy.wait_recv()
-    for k in range(count):
-        product[k] = dense(got[k].astype(narrow), columns[...])
-    second = [links.start(product.at[k], back.at[k - 1], others[k - 1]) for k in range(1, count)]
-    feature = spread.shape[2]
-
-    def features(target):
-        return words.at[:, pl.ds(pl.multiple_of(target * feature, 128), feature)]
-
-    far = [
-        links.start(features(jnp.bitwise_xor(b, k)), spread.at[b], others[k - 1])
-        for k in range(1, count)
+    for block in range(count):
+        product[block] = dense(got[block].astype(narrow), columns[...])
+    second = [
+        links.start(product.at[block], back.at[block - 1], others[block - 1])
+        for block in range(1, count)
     ]
-    spread[b] = words[:, pl.ds(pl.multiple_of(b * feature, 128), feature)]
+    far = {}
+    for block in sorted(range(1, count), key=lambda block: (bin(block >> 1).count("1"), block & 1)):
+        far[block] = links.start(
+            features(jnp.bitwise_xor(b, block)), spread.at[b], others[block - 1]
+        )
+    shards = PlaneExchange(count, links, projection, natural=True).gather()
+    next(shards)
+
     total = product[0]
-    for k, copy in enumerate(second):
+    for i, copy in enumerate(second):
         copy.wait_recv()
-        total = total + back[k]
+        total = total + back[i]
     mods[s] = total
     third = [links.start(mods.at[s], mods.at[s], device) for device in along]
-    exchange.run_gather(lambda places: None)
-    for copy in third + far:
+    for copy in third:
         copy.wait_recv()
-    links.finish()
-
-
-def modulate(count, depth, pieces, columns, shard, words):
-    vmem = pl.BlockSpec(memory_space=pltpu.VMEM)
-    places, width = pieces.shape[1], columns.shape[1]
-    copies = 3 * (count - 1) + depth - 1 + plane_copies(count)[0]
-    return pl.pallas_call(
-        partial(mod_kernel, count, depth),
-        in_specs=[vmem] * 4,
-        out_specs=[vmem] * 4,
-        out_shape=[
-            jax.ShapeDtypeStruct(pieces.shape, wide),
-            jax.ShapeDtypeStruct((depth, places, width), wide),
-            jax.ShapeDtypeStruct((count,) + shard.shape, narrow),
-            jax.ShapeDtypeStruct((count, words.shape[0], words.shape[1] // count), narrow),
-        ],
-        scratch_shapes=[
-            pltpu.VMEM((count, places, width), wide),
-            pltpu.VMEM((count - 1, places, width), wide),
-            pltpu.SemaphoreType.DMA((copies,)),
-            pltpu.SemaphoreType.DMA((copies,)),
-        ],
-        compiler_params=pltpu.CompilerParams(
-            collective_id=3, has_side_effects=True, vmem_limit_bytes=32 * 2**20
-        ),
-        name="modulate",
-    )(pieces, columns, shard, words)
-
-
-def small_kernel(count, depth, values, out, along, send, arrive):
-    links = Transfers(send, arrive)
-    s = lax.axis_index("seq")
-    others = [partner(k) for k in range(1, count)]
-    line = [seq_device(lax.rem(s + step, depth)) for step in range(1, depth)]
-    meet(others + line)
-    first = [links.start(values, along.at[i], device) for i, device in enumerate(line)]
-    total = values[...]
-    for i, copy in enumerate(first):
-        copy.wait_recv()
-        total = total + along[i]
-    out[0] = total
-    second = [links.start(out.at[0], out.at[k], others[k - 1]) for k in range(1, count)]
-    for copy in second:
-        copy.wait_recv()
-    links.finish()
-
-
-def gather_small(count, depth, values, collective_id):
-    vmem = pl.BlockSpec(memory_space=pltpu.VMEM)
-    copies = count - 1 + depth - 1
-    return pl.pallas_call(
-        partial(small_kernel, count, depth),
-        in_specs=[vmem],
-        out_specs=vmem,
-        out_shape=jax.ShapeDtypeStruct((count,) + values.shape, wide),
-        scratch_shapes=[
-            pltpu.VMEM((depth - 1,) + values.shape, wide),
-            pltpu.SemaphoreType.DMA((copies,)),
-            pltpu.SemaphoreType.DMA((copies,)),
-        ],
-        compiler_params=pltpu.CompilerParams(
-            collective_id=collective_id, has_side_effects=True, vmem_limit_bytes=32 * 2**20
-        ),
-        name="gather_small",
-    )(values)
-
-
-class Ring:
-    def __init__(self, depth, links):
-        self.depth, self.links = depth, links
-        self.index = lax.axis_index("seq")
-        self.right = seq_device(lax.rem(self.index + 1, depth))
-        self.left = seq_device(lax.rem(self.index + depth - 1, depth))
-
-    def source(self, step):
-        return lax.rem(self.index - step + 2 * self.depth, self.depth)
-
-
-def start_kernel(
-    count, depth, words, text, x, projection, pairs, normed, q, k, v,
-    plane, partial, core, outer, send, arrive,
-):
-    links = Transfers(send, arrive)
-    ring = Ring(depth, links)
-    b = lax.axis_index("bucket")
-    meet(plane_partners(count) + [ring.left, ring.right])
+    places = mods.shape[1]
+    parts = []
+    for i in range(depth // 4):
+        part = jnp.zeros((1, mods.shape[2]), wide)
+        for place in range(places):
+            part = part + jnp.where(clip[0] == place, mods[i, place : place + 1], 0.0)
+        parts.append(part)
+    scale = parts[0] if len(parts) == 1 else jnp.concatenate(parts, axis=1)
+    value = x[...].astype(wide)
+    rate = lax.rsqrt(jnp.mean(value * value, axis=1, keepdims=True) + EPSILON)
+    normed[s] = (value * rate * gain[...] * (1.0 + scale)).astype(narrow)
+    moving = [links.start(normed.at[s], normed.at[s], ring.right)]
+
+    exchange = PlaneExchange(count, links, None, partial, core, outer)
+
+    def pair(block):
+        if block:
+            far[block].wait_recv()
+        source = spread[jnp.bitwise_xor(b, block)]
+        place = block_index(block, count)
+        for start in range(0, width, 512):
+            span = slice(start, start + 512)
+            partial[place, :, span] = dense(source, text[:, span]).astype(narrow)
+        if block & 1:
+            exchange.send_core(block)
+
+    def finish(half, total):
+        pairs[pl.ds(half * exchange.rows, exchange.rows)] = total
+
+    sums = exchange.scatter(finish)
+    order = sorted(exchange.outer, key=lambda block: (bin(block).count("1"), block))
+    order = order[1:] + order[:1]
+    levels = len(exchange.orders[0])
+    for block in order[:levels]:
+        pair(block | 1)
+        pair(block)
+    next(sums)
+    for block in order[levels:]:
+        pair(block | 1)
+        pair(block)
+    next(sums)
     own = q.shape[2]
-    normed[ring.index] = x[...]
-    moving = [links.start(x, normed.at[ring.index], ring.right)]
 
     def project(step):
         place = ring.source(step)
         for i, out in enumerate((q, k, v)):
-            out[place] = dense(normed[place], projection[:, i * own : (i + 1) * own])
-
-    def ring_step(step):
+            span = slice(i * own, (i + 1) * own)
+            weight = projection[:, :, span]
+            out[place] = dense(normed[place], flat(weight))
+
+    def onward(step):
         moving[-1].wait_recv()
         place = ring.source(step)
         if step < depth - 1:
             moving.append(links.start(normed.at[place], normed.at[place], ring.right))
+
+    onward(1)
+    for _ in shards:
+        pass
+    project(0)
+    project(1)
+    for step in range(2, depth):
+        if step == depth - 1:
+            next(sums)
+        onward(step)
         project(step)
-
-    exchange = PlaneExchange(count, links, plane, partial, core, outer)
-    width = text.shape[1]
-
-    def pair(block):
-        source = words[jnp.bitwise_xor(b, block)]
-        place = block_index(block, count)
-        for first in range(0, width, 512):
-            columns = slice(first, first + 512)
-            partial[place, :, columns] = dense(source, text[:, columns]).astype(narrow)
-        if block & 1:
-            exchange.send_core(block)
-
-    def finish(half, total):
-        pairs[pl.ds(half * exchange.rows, exchange.rows)] = total
-
-    sums = exchange.scatter(finish)
-    order = sorted(exchange.outer, key=lambda block: (bin(block).count("1"), block))
-    order = order[1:] + order[:1]
-    levels = len(exchange.orders[0])
-    for i, block in enumerate(order):
-        pair(block | 1)
-        pair(block)
-        if i + 1 == levels:
-            next(sums)
-    project(0)
-    step = 1
+    for i, raw in enumerate((q, k)):
+        for block in range(depth):
+            place = i * depth + block
+            stat[place : place + 1] = row_sums(raw[block] * raw[block])
+    stats = [links.start(stat, stat_in.at[i], device) for i, device in enumerate(along)]
     for _ in sums:
-        if step < depth:
-            ring_step(step)
-            step += 1
-    while step < depth:
-        ring_step(step)
-        step += 1
+        pass
+    squares = stat[...]
+    for i, copy in enumerate(stats):
+        copy.wait_recv()
+        squares = squares + stat_in[i]
+    rates[...] = lax.rsqrt(squares / (own * depth) + EPSILON)
     links.finish()
 
 
-def start_exchange(count, depth, words, text, x, projection):
+def start_exchange(count, depth, clip, pieces, columns, shard, words, text, x, gain):
     vmem = pl.BlockSpec(memory_space=pltpu.VMEM)
     rows, width = x.shape
-    own = projection.shape[1] // 3
-    cap_rows, pair_width = words.shape[1], text.shape[1]
-    copies = plane_copies(count)[1] + depth - 1
+    own = shard.shape[1] // 3
+    cap_rows, pair_width = words.shape[0], text.shape[1]
+    places, mod_width = pieces.shape[1], columns.shape[1]
+    copies = sum(plane_copies(count)) + 3 * (count - 1) + 3 * (depth - 1)
     raw = jax.ShapeDtypeStruct((depth, rows, own), wide)
     return pl.pallas_call(
         partial(start_kernel, count, depth),
-        in_specs=[vmem] * 4,
-        out_specs=[vmem] * 5,
+        in_specs=[scalar_spec()] + [vmem] * 7,
+        out_specs=[vmem] * 10,
         out_shape=[
+            jax.ShapeDtypeStruct(pieces.shape, wide),
+            jax.ShapeDtypeStruct((depth, places, mod_width), wide),
+            jax.ShapeDtypeStruct((count,) + shard.shape, narrow),
+            jax.ShapeDtypeStruct((count, cap_rows, words.shape[1] // count), narrow),
             jax.ShapeDtypeStruct((cap_rows, pair_width), wide),
             jax.ShapeDtypeStruct((depth, rows, width), narrow),
             raw,
             raw,
             raw,
+            jax.ShapeDtypeStruct((2 * depth, rows), wide),
         ],
-        scratch_shapes=[pltpu.VMEM((1, cap_rows, 128), narrow)]
+        scratch_shapes=[
+            pltpu.VMEM((count, places, mod_width), wide),
+            pltpu.VMEM((count - 1, places, mod_width), wide),
+            pltpu.VMEM((2 * depth, rows), wide),
+            pltpu.VMEM((depth - 1, 2 * depth, rows), wide),
+        ]
         + plane_scratch(count, cap_rows, pair_width)[1:]
         + [pltpu.SemaphoreType.DMA((copies,)), pltpu.SemaphoreType.DMA((copies,))],
         compiler_params=pltpu.CompilerParams(
             collective_id=4, has_side_effects=True, vmem_limit_bytes=60 * 2**20
         ),
         name="start_exchange",
-    )(words, text, x, projection)
+    )(clip, pieces, columns, shard, words, text, x, gain)
 
 
 def end_kernel(
-    count, depth, pairs, text, words, grads, projection, normed, grad_words, share,
-    plane, back, send_sum, ring_in, total, send_low, low_in, send, arrive,
+    count, depth, pairs, text, words, grads, projection, grad_gate, grad_down, gate_held, down_held,
+    normed, grad_words, grad_weight, gate_next, down_next,
+    plane, back, send_sum, ring_in, total, gate_go, down_go, send, arrive,
 ):
     links = Transfers(send, arrive)
     ring = Ring(depth, links)
@@ -677,9 +701,9 @@
     others = [partner(k) for k in range(1, count)]
     meet(others + [ring.left, ring.right])
     plane[0] = pairs[...]
-    exchange = PlaneExchange(count, links, plane, plane, plane, plane)
-    feature = text.shape[0]
-    width = text.shape[1]
+    exchange = PlaneExchange(count, links, plane)
+    feature, width = text.shape
+    own_columns = pl.ds(pl.multiple_of(b * feature, 128), feature)
     moving = []
 
     def round_step(step):
@@ -695,10 +719,14 @@
 
     steps = [0]
 
+    weights = GradientRing(ring, (grad_gate, grad_down), (gate_held, down_held))
+
     def advance():
-        if steps[0] < depth:
+        if steps[0] < depth - 1:
             round_step(steps[0])
             steps[0] += 1
+            if steps[0] == depth - 1:
+                weights.onward(1, (gate_go, down_go), (gate_next, down_next))
 
     arriving = []
     blocks = [None] * count
@@ -708,31 +736,98 @@
     def compute(places):
         for place in places:
             block = blocks[place]
+            features = words[jnp.bitwise_xor(b, block)].astype(wide).T.astype(narrow)
             for first in range(0, width, 512):
                 columns = slice(first, first + 512)
-                part = dense(words[jnp.bitwise_xor(b, block)], plane[place, :, columns])
+                part = dense(features, plane[place, :, columns])
                 if place == 0:
                     total[:, columns] = part
                 else:
                     total[:, columns] += part
             value = contract_cols(plane[place], text[...]).astype(narrow)
             if block == 0:
-                grad_words[b] = value
+                grad_words[:, own_columns] = value
             else:
                 back[place - 1] = value
                 arriving.append(
-                    links.start(back.at[place - 1], grad_words.at[b], others[block - 1])
+                    links.start(
+                        back.at[place - 1], grad_words.at[:, own_columns], others[block - 1]
+                    )
                 )
         advance()
 
     exchange.run_gather(compute)
-    while steps[0] < depth:
+    while steps[0] < depth - 1:
         advance()
-    low_rows = feature // depth
+    round_step(depth - 1)
+    grad_weight[...] = total[...].astype(narrow)
+    for copy in arriving + weights.copies:
+        copy.wait_recv()
+    links.finish()
+
+
+def end_exchange(count, depth, pairs, text, words, grads, projection, ffn_grads, held):
+    vmem = pl.BlockSpec(memory_space=pltpu.VMEM)
+    cap_rows, pair_width = pairs.shape
+    feature = text.shape[0]
+    rows, width = grads.shape[1], projection.shape[0]
+    copies = plane_copies(count)[0] + count - 1 + depth - 1 + 2
+    return pl.pallas_call(
+        partial(end_kernel, count, depth),
+        in_specs=[vmem] * 9,
+        out_specs=[vmem] * 5,
+        out_shape=[
+            jax.ShapeDtypeStruct((rows, width), wide),
+            jax.ShapeDtypeStruct((cap_rows, count * feature), narrow),
+            jax.ShapeDtypeStruct((feature, pair_width), narrow),
+            jax.ShapeDtypeStruct(held[0].shape, narrow),
+            jax.ShapeDtypeStruct(held[1].shape, narrow),
+        ],
+        scratch_shapes=[
+            pltpu.VMEM((count, cap_rows, pair_width), narrow),
+            pltpu.VMEM((count - 1, cap_rows, feature), narrow),
+            pltpu.VMEM((depth - 1, rows, width), narrow),
+            pltpu.VMEM((depth - 1, rows, width), narrow),
+            pltpu.VMEM((feature, pair_width), wide),
+            pltpu.VMEM(held[0].shape, narrow),
+            pltpu.VMEM(held[1].shape, narrow),
+            pltpu.SemaphoreType.DMA((copies,)),
+            pltpu.SemaphoreType.DMA((copies,)),
+        ],
+        compiler_params=pltpu.CompilerParams(
+            collective_id=5, has_side_effects=True, vmem_limit_bytes=63 * 2**20
+        ),
+        name="end_exchange",
+    )(pairs, text, words, grads, projection, *ffn_grads, *held)
+
+
+def sum_kernel(
+    count, depth, flags, text, combined, upstream, normed, grads, grad_gate, grad_down, gate_held,
+    down_held, words, row, small, down_share, text_share, output_share, proj_share, gate_share, null_share, rows_out, small_out,
+    out_part, out_core, out_outer, proj_part, proj_core, proj_outer, send_low, low_in, out_go,
+    out_come, proj_go, proj_come, gate, gate_come, null, null_come, small_come, small_go,
+    small_land, gate_go, down_go, gate_land, down_land, send, arrive,
+):
+    links = Transfers(send, arrive)
+    ring = Ring(depth, links)
+    b, s = lax.axis_index("bucket"), lax.axis_index("seq")
+    others = [partner(k) for k in range(1, count)]
+    turns = [lax.rem(s + step, depth) for step in range(1, depth)]
+    along = [seq_device(place) for place in turns]
+    meet(others + along)
+
+    rows_out[0, s] = row[...]
+    tiny = []
+    for i, (place, device) in enumerate(zip(turns, along, strict=True)):
+        tiny.append(links.start(row, rows_out.at[0, s], device))
+        tiny.append(links.start(small.at[place], small_come.at[i], device))
+
+    low_rows = text.shape[0] // depth
     going = []
-    for step in range(depth):
-        rows = pl.ds(pl.multiple_of(ring.source(step + 1) * low_rows, low_rows), low_rows)
-        value = total[rows]
+
+    def text_step(step):
+        rows = pl.ds(pl.multiple_of(ring.source(step + 1) * low_rows, 16), low_rows)
+        value = text[rows].astype(wide)
         if step > 0:
             going[-1].wait_recv()
             value = value + low_in[step - 1].astype(wide)
@@ -740,44 +835,215 @@
             send_low[step] = value.astype(narrow)
             going.append(links.start(send_low.at[step], low_in.at[step], ring.right))
         else:
-            share[...] = value
-    for copy in arriving:
+            text_share[...] = value
+
+    weights = GradientRing(ring, (grad_gate, grad_down), (gate_held, down_held))
+
+    def weights_step(step):
+        slot = step - 2
+        weights.onward(
+            step,
+            (gate_go.at[slot], down_go.at[slot]),
+            (gate_land.at[slot], down_land.at[slot]),
+        )
+
+    text_step(0)
+    weights_step(2)
+
+    share = out_go.shape[1]
+    pair = 2 * out_part.shape[1]
+
+    def fill(part, leading, trailing):
+        for first in range(0, count, 2):
+            value = contract_rows(leading[:, first // 2 * pair : (first // 2 + 1) * pair], trailing)
+            value = value.astype(narrow)
+            part[first] = value[: pair // 2]
+            part[first + 1] = value[pair // 2 :]
+
+    def plane_sum(part, core, outer, go):
+        exchange = PlaneExchange(count, links, None, part, core, outer, natural=True)
+        for block in range(1, count, 2):
+            exchange.send_core(block)
+
+        def finish(half, total):
+            low = total.astype(narrow)
+            for i in range(depth // 2):
+                go[half * (depth // 2) + i] = low[i * share : (i + 1) * share]
+
+        return exchange.scatter(finish)
+
+    fill(out_part, combined[...], upstream[...])
+    out_sums = plane_sum(out_part, out_core, out_outer, out_go)
+    fill(proj_part, flat(normed[...]), flat(grads[...]))
+    proj_sums = plane_sum(proj_part, proj_core, proj_outer, proj_go)
+    for _ in range(count // 4):
+        next(out_sums)
+    for _ in range(count // 4):
+        next(proj_sums)
+    text_step(1)
+
+    places = flags.shape[0]
+    cap_local = words.shape[0] // places
+    null_rows = null.shape[1]
+    for k in range(count):
+        value = jnp.zeros((null_rows, words.shape[1]), wide)
+        for place in range(places):
+            first = place * cap_local + k * null_rows
+            part = words[first : first + null_rows].astype(wide)
+            value = value + jnp.where(flags[place] == 1, part, 0.0)
+        null[k] = value
+    next(out_sums)
+    next(proj_sums)
+    nulls = [
+        links.start(null.at[jnp.bitwise_xor(b, k)], null_come.at[k - 1], others[k - 1])
+        for k in range(1, count)
+    ]
+
+    def drain(sums):
+        for _ in sums:
+            pass
+
+    def seq_sends(go, come):
+        come[s] = go[s]
+        return [
+            links.start(go.at[place], come.at[s], device)
+            for place, device in zip(turns, along, strict=True)
+        ]
+
+    for step in range(3, depth - 1):
+        weights_step(step)
+    weights.arrived()
+    gate[...] = weights.value(0, depth - 1).astype(narrow)
+    far = [
+        links.start(gate.at[jnp.bitwise_xor(b, k)], gate_come.at[b], others[k - 1])
+        for k in range(1, count)
+    ]
+    gate_come[b] = gate[b]
+    down_share[...] = weights.value(1, depth - 1)
+    own_small = small[s]
+    for copy in tiny:
         copy.wait_recv()
+    for i in range(depth - 1):
+        own_small = own_small + small_come[i]
+    small_go[...] = own_small
+    spread = []
+    for k in range(1, count):
+        spread.append(links.start(rows_out.at[0], rows_out.at[k], others[k - 1]))
+        spread.append(
+            links.start(
+                small_go.at[jnp.bitwise_xor(b, k)], small_land.at[k - 1], others[k - 1]
+            )
+        )
+    drain(out_sums)
+    out_far = seq_sends(out_go, out_come)
+    drain(proj_sums)
+    proj_far = seq_sends(proj_go, proj_come)
+    for step in range(2, depth - 1):
+        text_step(step)
+    total = null[b]
+    for i, copy in enumerate(nulls):
+        copy.wait_recv()
+        total = total + null_come[i]
+    null_share[...] = total
+    for copy in spread:
+        copy.wait_recv()
+    sums = small_go[b]
+    for i in range(count - 1):
+        sums = sums + small_land[i]
+    small_out[...] = sums
+    for copy in far:
+        copy.wait_recv()
+    units = gate.shape[2] // 2
+    for block in range(count):
+        for half in range(2):
+            first = half * count * units + block * units
+            gate_share[:, first : first + units] = gate_come[
+                block, :, half * units : (half + 1) * units
+            ].astype(wide)
+    for copy in out_far + proj_far:
+        copy.wait_recv()
+    text_step(depth - 1)
+    total = out_come[0].astype(wide)
+    for i in range(1, depth):
+        total = total + out_come[i].astype(wide)
+    output_share[...] = total
+    own = proj_come.shape[2] // 3
+    for i in range(3):
+        for source in range(depth):
+            first = i * depth * own + source * own
+            proj_share[:, first : first + own] = proj_come[
+                source, :, i * own : (i + 1) * own
+            ].astype(wide)
     links.finish()
 
 
-def end_exchange(count, depth, pairs, text, words, grads, projection):
+def final_sums(
+    count, depth, flags, text, combined, upstream, normed, grads, ffn_grads, held, words, row, small
+):
     vmem = pl.BlockSpec(memory_space=pltpu.VMEM)
-    cap_rows, pair_width = pairs.shape
-    feature = text.shape[0]
-    rows, width = grads.shape[1], projection.shape[0]
-    copies = plane_copies(count)[0] + count - 1 + 2 * (depth - 1)
+    feature, pair_width = text.shape
+    width = combined.shape[1]
+    own3 = grads.shape[2]
+    share = width // (count * depth)
+    null_rows = words.shape[0] // flags.shape[0] // count
+    text_width = words.shape[1]
+    outer = count // 2
+    block_rows = width // count
     quarter = (depth - 1, feature // depth, pair_width)
+
+    def plane_sums(columns):
+        return [
+            pltpu.VMEM((count, block_rows, columns), narrow),
+            pltpu.VMEM((outer, block_rows, columns), narrow),
+            pltpu.VMEM((2, outer - 1, block_rows // 2, columns), narrow),
+        ]
+
+    copies = 2 * (depth - 1) + depth - 1 + 2 * plane_copies(count)[1] + 4 * (count - 1)
+    copies += 2 * (depth - 1) + 2 * (depth - 3)
+    gate, down = held
+    gates = pltpu.VMEM(gate.shape, narrow)
     return pl.pallas_call(
-        partial(end_kernel, count, depth),
-        in_specs=[vmem] * 5,
-        out_specs=[vmem] * 3,
+        partial(sum_kernel, count, depth),
+        in_specs=[scalar_spec()] + [vmem] * 12,
+        out_specs=[vmem] * 8,
         out_shape=[
-            jax.ShapeDtypeStruct((rows, width), wide),
-            jax.ShapeDtypeStruct((count, cap_rows, feature), narrow),
+            jax.ShapeDtypeStruct(down.shape, wide),
             jax.ShapeDtypeStruct((feature // depth, pair_width), wide),
+            jax.ShapeDtypeStruct((share, width), wide),
+            jax.ShapeDtypeStruct((share, depth * own3), wide),
+            jax.ShapeDtypeStruct((share, count * gate.shape[2]), wide),
+            jax.ShapeDtypeStruct((null_rows, text_width), wide),
+            jax.ShapeDtypeStruct((count, depth) + row.shape, wide),
+            jax.ShapeDtypeStruct(small.shape[2:], wide),
         ],
-        scratch_shapes=[
-            pltpu.VMEM((count, cap_rows, pair_width), narrow),
-            pltpu.VMEM((count - 1, cap_rows, feature), narrow),
-            pltpu.VMEM((depth - 1, rows, width), narrow),
-            pltpu.VMEM((depth - 1, rows, width), narrow),
-            pltpu.VMEM((feature, pair_width), wide),
+        scratch_shapes=plane_sums(width)
+        + plane_sums(own3)
+        + [
             pltpu.VMEM(quarter, narrow),
             pltpu.VMEM(quarter, narrow),
+            pltpu.VMEM((depth, share, width), narrow),
+            pltpu.VMEM((depth, share, width), narrow),
+            pltpu.VMEM((depth, share, own3), narrow),
+            pltpu.VMEM((depth, share, own3), narrow),
+            gates,
+            gates,
+            pltpu.VMEM((count, null_rows, text_width), wide),
+            pltpu.VMEM((count - 1, null_rows, text_width), wide),
+            pltpu.VMEM((depth - 1,) + small.shape[1:], wide),
+            pltpu.VMEM(small.shape[1:], wide),
+            pltpu.VMEM((count - 1,) + small.shape[2:], wide),
+            pltpu.VMEM((depth - 3,) + gate.shape, narrow),
+            pltpu.VMEM((depth - 3,) + down.shape, narrow),
+            pltpu.VMEM((depth - 3,) + gate.shape, narrow),
+            pltpu.VMEM((depth - 3,) + down.shape, narrow),
             pltpu.SemaphoreType.DMA((copies,)),
             pltpu.SemaphoreType.DMA((copies,)),
         ],
         compiler_params=pltpu.CompilerParams(
-            collective_id=5, has_side_effects=True, vmem_limit_bytes=60 * 2**20
+            collective_id=10, has_side_effects=True, vmem_limit_bytes=60 * 2**20
         ),
-        name="end_exchange",
-    )(pairs, text, words, grads, projection)
+        name="final_sums",
+    )(flags, text, combined, upstream, normed, grads, *ffn_grads, *held, words, row, small)
 
 
 def head_lanes(values, head, size):
@@ -839,9 +1105,9 @@
 
 
 def forward_kernel(
-    count, depth, size, lanes, spans, lengths, gates, raw_q, raw_k, raw_v, gain_q, gain_k, cosine,
-    sine, text_own, gate_up, combined, q, k, v, qc, total, cross_total, rates, text, gathered,
-    stat, stat_in, self_out, staged, send, arrive, local,
+    count, depth, size, lanes, spans, lengths, gates, raw_q, raw_k, raw_v, rates, gain_q, gain_k,
+    cosine, sine, text_own, gate_up, combined, q, k, v, qc, total, cross_total, text, gathered,
+    self_out, staged, send, arrive, local,
 ):
     links = Transfers(send, arrive)
     b, s = lax.axis_index("bucket"), lax.axis_index("seq")
@@ -854,11 +1120,6 @@
     width = own * depth
     grid, heads = own // lanes, lanes // size
     scaling = size ** (-0.5)
-    for i, raw in enumerate((raw_q, raw_k)):
-        for block in range(depth):
-            place = i * depth + block
-            stat[place : place + 1] = row_sums(raw[block] * raw[block])
-    stats = [links.start(stat, stat_in.at[i], device) for i, device in enumerate(along)]
     words = [
         links.start(text_own.at[place], text.at[s], device)
         for place, device in zip(turns, along, strict=True)
@@ -883,11 +1144,6 @@
                 kept.append(copy)
     for block in range(depth):
         v[block_rows_of(block, block_rows)] = raw_v[block].astype(narrow)
-    squares = stat[...]
-    for i, copy in enumerate(stats):
-        copy.wait_recv()
-        squares = squares + stat_in[i]
-    rates[...] = lax.rsqrt(squares / width + EPSILON)
     columns = rates[...].T
     for block in range(depth):
         at = block_rows_of(block, block_rows)
@@ -968,20 +1224,20 @@
 
 
 def attention_forward(
-    count, depth, size, lanes, scalars, raws, gains, angles, text_own, gate_up
+    count, depth, size, lanes, scalars, raws, rates, gains, angles, text_own, gate_up
 ):
     block_rows, own = raws[0].shape[1:]
     rows = depth * block_rows
     grid, heads = own // lanes, lanes // size
     vmem, anywhere = pl.BlockSpec(memory_space=pltpu.VMEM), pl.BlockSpec(memory_space=pl.ANY)
     units = gate_up.shape[1] // (2 * count)
-    copies = 3 * (depth - 1) + 2 * (count - 1)
+    copies = 2 * (depth - 1) + 2 * (count - 1)
     row_block = jax.ShapeDtypeStruct((rows, own), narrow)
     totals = jax.ShapeDtypeStruct((grid, heads, rows), wide)
     return pl.pallas_call(
         partial(forward_kernel, count, depth, size, lanes),
-        in_specs=[scalar_spec()] * 3 + [vmem] * 8 + [anywhere],
-        out_specs=[vmem] * 10,
+        in_specs=[scalar_spec()] * 3 + [vmem] * 9 + [anywhere],
+        out_specs=[vmem] * 9,
         out_shape=[
             jax.ShapeDtypeStruct((depth, block_rows, own), narrow),
             row_block,
@@ -990,13 +1246,10 @@
             row_block,
             totals,
             totals,
-            jax.ShapeDtypeStruct((2 * depth, block_rows), wide),
             jax.ShapeDtypeStruct(text_own.shape, narrow),
             jax.ShapeDtypeStruct((count * gate_up.shape[0], 2 * units), narrow),
         ],
         scratch_shapes=[
-            pltpu.VMEM((2 * depth, block_rows), wide),
-            pltpu.VMEM((depth - 1, 2 * depth, block_rows), wide),
             pltpu.VMEM((rows, own), wide),
             pltpu.VMEM((depth, block_rows, own), narrow),
             pltpu.SemaphoreType.DMA((copies,)),
@@ -1007,14 +1260,14 @@
             collective_id=8, has_side_effects=True, vmem_limit_bytes=60 * 2**20
         ),
         name="attention_forward",
-    )(*scalars, *raws, *gains, *angles, text_own, gate_up)
+    )(*scalars, *raws, rates, *gains, *angles, text_own, gate_up)
 
 
 def backward_kernel(
     count, depth, size, lanes, spans, lengths, gates, upstream, weight, q, k, v, qc, raw_q, raw_k,
-    rates, gain_q, gain_k, cosine, sine, text, total, cross_total, small, projected, gain_sums,
-    dgate, grad_text, small_out, go, send_go, dqc, back_q, back_k, parts, send_text, stat,
-    stat_in, along_in, sum_k, sum_v, send, arrive,
+    rates, gain_q, gain_k, cosine, sine, text, total, cross_total, small, grad_gate, grad_down,
+    projected, gain_sums, dgate, grad_text, small_out, gate_held, down_held, go, send_go, dqc, back_q, back_k, parts, send_text, stat,
+    stat_in, sum_k, sum_v, send, arrive,
 ):
     links = Transfers(send, arrive)
     s = lax.axis_index("seq")
@@ -1027,7 +1280,9 @@
     width = own * depth
     grid, heads = own // lanes, lanes // size
     scaling = size ** (-0.5)
-    smalls = [links.start(small, along_in.at[i], device) for i, device in enumerate(along)]
+
+    small_out[0, s] = small[...]
+    smalls = [links.start(small, small_out.at[0, s], device) for device in along]
 
     def grad_out(place):
         at = pl.ds(pl.multiple_of(place * own, 64), own)
@@ -1038,6 +1293,8 @@
         send_go[i] = grad_out(place)
         arriving.append(links.start(send_go.at[i], go.at[s], device))
     go[s] = grad_out(s)
+    ring = Ring(depth, links)
+    weights = GradientRing(ring, (grad_gate, grad_down), None)
 
     cap_local = text.shape[3]
     cap = text.shape[0] * cap_local
@@ -1048,6 +1305,8 @@
         block = lax.rem(s - step + depth, depth)
         if step:
             arriving[step - 1].wait_recv()
+        if step == depth - 1:
+            weights.first((gate_held, down_held))
         at = block_rows_of(block, block_rows)
         clip = spans[2, block]
         clips.append(clip)
@@ -1101,11 +1360,8 @@
         for place, device in zip(turns, along, strict=True)
     ]
     grad_text[s] = send_text[s]
-    sums = small[...]
-    for i, copy in enumerate(smalls):
+    for copy in smalls:
         copy.wait_recv()
-        sums = sums + along_in[i]
-    small_out[0] = sums
     spread = [links.start(small_out.at[0], small_out.at[k], others[k - 1]) for k in range(1, count)]
 
     key_index = lax.broadcasted_iota(jnp.int32, (rows, block_rows), 0)
@@ -1172,32 +1428,35 @@
             projected[block, :, i * own : (i + 1) * own] = (
                 rate * (back[at] * gain[...] - hat * means[:, place])
             ).astype(narrow)
-    for copy in words + spread:
+    for copy in words + spread + weights.copies:
         copy.wait_recv()
     links.finish()
 
 
 def attention_backward(
     count, depth, size, lanes, scalars, upstream, weight, saved, raws, rates, gains, angles, text,
-    totals, small,
+    totals, small, ffn_grads,
 ):
     block_rows, own = raws[0].shape[1:]
     rows = depth * block_rows
     grid, heads = own // lanes, lanes // size
     vmem = pl.BlockSpec(memory_space=pltpu.VMEM)
-    copies = 4 * (depth - 1) + count - 1
+    copies = 4 * (depth - 1) + count - 1 + 2
     cap = text.shape[0] * text.shape[3]
     args = (*scalars, upstream, weight, *saved, *raws, rates, *gains, *angles, text, *totals, small)
+    args = args + tuple(ffn_grads)
     return pl.pallas_call(
         partial(backward_kernel, count, depth, size, lanes),
         in_specs=[scalar_spec()] * 3 + [vmem] * (len(args) - 3),
-        out_specs=[vmem] * 5,
+        out_specs=[vmem] * 7,
         out_shape=[
             jax.ShapeDtypeStruct((depth, block_rows, 3 * own), narrow),
             jax.ShapeDtypeStruct((2, own), wide),
             jax.ShapeDtypeStruct((grid, heads, block_rows), wide),
             jax.ShapeDtypeStruct(text.shape, narrow),
-            jax.ShapeDtypeStruct((count,) + small.shape, wide),
+            jax.ShapeDtypeStruct((count, depth) + small.shape, wide),
+            jax.ShapeDtypeStruct(ffn_grads[0].shape[:1] + ffn_grads[0].shape[2:], narrow),
+            jax.ShapeDtypeStruct(ffn_grads[1].shape[1:], narrow),
         ],
         scratch_shapes=[
             pltpu.VMEM((depth, block_rows, own), narrow),
@@ -1209,7 +1468,6 @@
             pltpu.VMEM(text.shape, narrow),
             pltpu.VMEM((2 * depth, block_rows), wide),
             pltpu.VMEM((depth - 1, 2 * depth, block_rows), wide),
-            pltpu.VMEM((depth - 1,) + small.shape, wide),
             pltpu.VMEM((rows, lanes), wide),
             pltpu.VMEM((rows, lanes), wide),
             pltpu.SemaphoreType.DMA((copies,)),
@@ -1274,24 +1532,35 @@
     silu_cond = jax.nn.silu(condition).astype(narrow)
     mod_width = modulation.shape[1] // count_s
     pieces = silu_cond.astype(wide).reshape(places, count_b, -1).transpose(1, 0, 2)
-    cond_columns, mods, own_projection, words = modulate(
+    my_clip = (s * local) // clip_length
+    (
+        cond_columns,
+        mods,
+        own_projection,
+        words,
+        text_pairs,
+        normed,
+        raw_q,
+        raw_k,
+        raw_v,
+        rates,
+    ) = start_exchange(
         count_b,
         count_s,
+        my_clip.astype(jnp.int32)[None],
         pieces,
         lax.dynamic_slice_in_dim(modulation, s * mod_width, mod_width, 1),
         own_projection,
         words_own,
+        text_weight,
+        tokens,
+        norm_gains[:1],
     )
     own_projection = own_projection.reshape(width, 3 * own)
-    my_clip = (s * local) // clip_length
     modulated = lax.dynamic_index_in_dim(mods, my_clip, 1, keepdims=False).reshape(1, 4 * width)
-
     tokens_in = tokens.astype(wide)
-    normed_full, pre_pull = jax.vjp(pre_attention, tokens_in, modulated, norm_gains)
-    normed_low = normed_full.astype(narrow)
-    text_pairs, normed, raw_q, raw_k, raw_v = start_exchange(
-        count_b, count_s, words, text_weight, normed_low, own_projection
-    )
+    _, pre_pull = jax.vjp(pre_attention, tokens_in, modulated, norm_gains)
+
     text_outs, text_pull = jax.vjp(text_heads, text_pairs, head_gains[2])
     text_own = jnp.stack([o.astype(narrow).reshape(cap_rows, count_s, own) for o in text_outs])
     text_own = text_own.transpose(2, 0, 1, 3).reshape(count_s, 2, places, cap_local, own)
@@ -1314,13 +1583,14 @@
     scalars = (spans, caption_lengths, own_gates)
     full_output, text_own = lax.optimization_barrier((output_weight, text_own))
     full_output = lax.all_gather(full_output, "bucket", axis=0, tiled=True)
-    combined, *saved, total, cross_total, rates, text_kv, own_gate_up = attention_forward(
+    combined, *saved, total, cross_total, text_kv, own_gate_up = attention_forward(
         count_b,
         count_s,
         size,
         lanes,
         scalars,
         (raw_q, raw_k, raw_v),
+        rates,
         gains,
         (cosine, sine),
         text_own,
@@ -1345,35 +1615,17 @@
     grad_normed_ffn, grad_gate_up, grad_down = ffn_backward(
         count_b, grad_lowered_low, own_gate_up, down_weight, gate_values, plane, hidden
     )
-    down_share = lax.psum_scatter(
-        grad_down, "seq", scatter_dimension=0, tiled=True
-    ).astype(wide)
-    gate_share = lax.psum_scatter(
-        grad_gate_up.reshape(count_b, gate_rows, 2 * own_hidden),
-        "seq",
-        scatter_dimension=1,
-        tiled=True,
-    )
-    share_rows = gate_rows // count_s
-    gate_share = lax.all_to_all(gate_share, "bucket", 0, 0, tiled=True)
-    gate_share = (
-        gate_share.reshape(count_b, share_rows, 2, own_hidden)
-        .transpose(1, 2, 0, 3)
-        .reshape(share_rows, 2 * count_b * own_hidden)
-        .astype(wide)
+    share = width // (count_b * count_s)
+    ffn_grads = (
+        grad_gate_up.reshape(count_b, count_s, share, 2 * own_hidden),
+        grad_down.reshape(count_s, own_hidden // count_s, width),
     )
 
     grad_attended, grad_tokens_post, grad_modulated_post, grad_norm_post = post_pull(
         (grad_middle, grad_normed_ffn)
     )
     grad_attended_low = grad_attended.astype(narrow)
-    grad_output = contract_rows(combined, grad_attended_low).astype(narrow)
-    output_share = lax.psum_scatter(
-        grad_output, ("bucket", "seq"), scatter_dimension=0, tiled=True
-    ).astype(wide)
-    own_place = jnp.arange(places, dtype=jnp.int32)[:, None] == my_clip
-    grad_rows = (grad_modulated_post + grad_modulated_last)[:, width:].reshape(3, 1, width)
-    grad_projected, gain_sums, grad_gates, grad_kv, early = attention_backward(
+    grad_projected, gain_sums, grad_gates, grad_kv, early, *held = attention_backward(
         count_b,
         count_s,
         size,
@@ -1388,50 +1640,28 @@
         (cosine, sine),
         text_kv,
         (total, cross_total),
-        jnp.where(own_place[None], grad_rows, 0.0).reshape(3 * places, width),
-    )
-    early = early.reshape(count_b, 3, places, width)
+        (grad_modulated_post + grad_modulated_last)[:, width:],
+        ffn_grads,
+    )
 
     grad_kv = grad_kv.reshape(count_s, 2, cap_rows, own)
     grad_kv = grad_kv.transpose(1, 2, 0, 3).reshape(2, cap_rows, width).astype(wide)
     grad_pairs, grad_gain_text = text_pull((grad_kv[0], grad_kv[1]))
     grad_pairs_low = grad_pairs.astype(narrow)
-    grad_normed, grad_words, text_share = end_exchange(
+    grad_normed, grad_words, grad_text, *held = end_exchange(
         count_b,
         count_s,
         grad_pairs_low,
         text_weight,
-        words.transpose(0, 2, 1),
+        words,
         grad_projected,
         own_projection,
-    )
-    grad_words = grad_words.transpose(1, 0, 2).reshape(places, cap_local, text_width)
-    grad_captions = jnp.where(is_null, 0.0, grad_words.astype(wide))
-    null_local = jnp.sum(jnp.where(is_null, grad_words.astype(wide), 0.0), axis=0).astype(narrow)
-    null_share = lax.all_to_all(null_local, "bucket", 0, 0, tiled=True)
-    null_share = jnp.sum(null_share.reshape(count_b, -1, text_width).astype(wide), axis=0)
-    null_share = lax.ppermute(
-        null_share,
-        ("bucket", "seq"),
-        [(i * count_s + j, j * count_b + i) for i in range(count_b) for j in range(count_s)],
-    )
-
-    grad_projection = contract_rows(flat(normed), flat(grad_projected)).astype(narrow)
-    proj_share = lax.all_to_all(grad_projection, "bucket", 0, 0, tiled=True)
-    proj_share = jnp.sum(
-        proj_share.reshape(count_b, -1, 3 * own).astype(wide), axis=0
-    ).astype(narrow)
-    proj_share = lax.all_to_all(proj_share.reshape(count_s, -1, 3 * own), "seq", 0, 0, tiled=True)
-    proj_share = (
-        proj_share.reshape(count_s, -1, 3, own)
-        .transpose(1, 2, 0, 3)
-        .reshape(-1, 3 * width)
-        .astype(wide)
+        ffn_grads,
+        held,
     )
     grad_tokens_pre, grad_modulated_pre, grad_norm_pre = pre_pull(grad_normed)
     grad_tokens = grad_tokens_pre + grad_tokens_post
 
-    share = width // (count_b * count_s)
     def place(values):
         return lax.dynamic_update_slice_in_dim(jnp.zeros((width,), wide), values, s * own, 0)
 
@@ -1443,30 +1673,67 @@
     )
     small = jnp.concatenate(
         [
-            jnp.where(own_place, grad_modulated_pre[:, :width], 0.0),
             grad_norm_pre + grad_norm_post + grad_norm_last,
             jnp.stack(
                 [
                     place(gain_sums[0]),
                     place(gain_sums[1]),
                     grad_gain_text,
-                    jnp.pad(gate_sums, (0, width - heads)),
+                    jnp.zeros((width,), wide),
                 ]
             ),
         ],
         axis=0,
     )
-    small = gather_small(count_b, count_s, small, 7)
-    grad_mod_rows = jnp.concatenate([small[:, None, :places], early], axis=1)
+    own_clip = (jnp.arange(places, dtype=jnp.int32) == my_clip).astype(wide)
+    row = jnp.concatenate(
+        [
+            jnp.pad(gate_sums, (0, 128 - heads)),
+            jnp.pad(own_clip, (0, width - 128 - places)),
+        ]
+    )
+    row = jnp.stack([grad_modulated_pre[0, :width], row], axis=0)
+    (
+        down_share,
+        text_share,
+        output_share,
+        proj_share,
+        gate_share,
+        null_share,
+        grad_rows,
+        own_sums,
+    ) = final_sums(
+        count_b,
+        count_s,
+        null_flags,
+        grad_text,
+        combined,
+        grad_attended_low,
+        normed,
+        grad_projected,
+        ffn_grads,
+        held,
+        grad_words,
+        row,
+        small.reshape(8, count_b, count_s, share).transpose(2, 1, 0, 3),
+    )
+    null_share = lax.ppermute(
+        null_share,
+        ("bucket", "seq"),
+        [(i * count_s + j, j * count_b + i) for i in range(count_b) for j in range(count_s)],
+    )
+    grad_words = grad_words.reshape(places, cap_local, text_width).astype(wide)
+    grad_captions = jnp.where(is_null, 0.0, grad_words)
+
     cond_own = lax.dynamic_slice_in_dim(cond_columns, s * share, share, 2)
+    at_clip = grad_rows[:, :, 1, 128 : 128 + places]
+    cond_rows = jnp.sum(at_clip[:, :, :, None] * cond_own[:, None], axis=2)
     mod_share = lax.dot_general(
-        flat(cond_own),
-        grad_mod_rows.transpose(0, 2, 1, 3).reshape(count_b * places, 4 * width),
+        flat(cond_rows),
+        jnp.concatenate([flat(grad_rows[:, :, 0]), flat(early)], axis=1),
         (((0,), (0,)), ((), ())),
         precision=HIGHEST,
     )
-    sums = jnp.sum(small[:, places:], axis=0)
-    own_sums = lax.dynamic_slice_in_dim(sums, (b * count_s + s) * share, share, 1)
     return (
         mixed.astype(narrow),
         grad_tokens,
@@ -1480,7 +1747,7 @@
         down_share,
         own_sums[:4],
         own_sums[4:7],
-        sums[7, :heads],
+        jnp.sum(grad_rows[:, :, 1, :heads], axis=(0, 1)),
     )
 
 

time: 819 us -> 746 us (0.911)
  starting transfers between devices: 22 us -> 1.95 us
  other arithmetic: 56.2 us -> 40.4 us
  matrix products: 18.4 us -> 6.02 us
  local copies, waits for them, and re-layouts: 50.6 us -> 38.6 us
  waiting for transfers between devices: 18.7 us -> 8.68 us
    all_to_all x4 -> x0, starting transfers between devices: 19.9 us -> none  [the longest x1 5.75 us: per_device(): gate_share = lax.all_to_all(gate_share, 'bucket', 0, 0, tiled=True)]
    pallas_call x1, Pallas kernels: 114 us -> 94.5 us  [attention_backward(): pl.pallas_call(partial(backward_kernel, count, depth, size, lanes), in_sp...]
    pallas_call x4 -> x3, Pallas kernels: 317 us -> 335 us  [the longest x1 122 us: start_exchange(): pl.pallas_call(partial(start_kernel, count, depth), in_specs=[scalar_spec...]
    convert_element_type x7 -> x0, local copies, waits for them, and re-layouts: 14.1 us -> none  [the longest x2 9.48 us: per_device(): grad_captions = jnp.where(is_null, 0.0, grad_words.astype(wide))]
    dot_general x3 -> x1, matrix products: 14.3 us -> 2.14 us  [per_device(): lax.dot_general(flat(cond_rows), jnp.concatenate([flat(grad_rows[:, :, 0]...]
    all_to_all x4 -> x0, waiting for transfers between devices: 11.1 us -> none  [the longest x1 7.21 us: per_device(): lax.all_to_all(proj_share.reshape(count_s, -1, 3 * own), 'seq', 0, 0, til...]
  transfers between devices with their start and end apart: 9 -> 2, of which waited for: 3 -> 1; matrix products, arithmetic and copies ran while one was open for 10% -> 2% of each run, Pallas kernels for 46% -> 8%
where the time goes in v3:
time: 746 us; the launch traced here: 734 us
  Pallas kernels  623 us (84%)
  other arithmetic  40.4 us (5%)
  local copies, waits for them, and re-layouts  38.6 us (5%)
  between operations  15.8 us (2%)
  waiting for transfers between devices  8.68 us (1%)
    pallas_call x1, Pallas kernels, start_exchange(): pl.pallas_call(partial(start_kernel, count, depth), in_specs=[scalar_spec...  122 us
    pallas_call x1, Pallas kernels, final_sums(): pl.pallas_call(partial(sum_kernel, count, depth), in_specs=[scalar_spec()...  114 us
    pallas_call x1, Pallas kernels, end_exchange(): pl.pallas_call(partial(end_kernel, count, depth), in_specs=[vmem] * 9, ou...  98.7 us
    pallas_call x1, Pallas kernels, attention_backward(): pl.pallas_call(partial(backward_kernel, count, depth, size, lanes), in_sp...  94.5 us
    pallas_call x1, Pallas kernels, ffn_backward(): pl.pallas_call(partial(ffn_back_kernel, count), in_specs=[vmem] * 3 + [an...  68.7 us
    pallas_call x1, Pallas kernels, ffn_forward(): pl.pallas_call(partial(ffn_kernel, count), in_specs=[vmem] * 3, out_specs...  63.3 us
    pallas_call x1, Pallas kernels, attention_forward(): pl.pallas_call(partial(forward_kernel, count, depth, size, lanes), in_spe...  61.2 us
  transfers between devices with their start and end apart: 2, of which 1 were waited for; matrix products, arithmetic and copies ran while one was open for 2% of the time, Pallas kernels for 8%

profile of v3, /device:TPU:4, one launch (start us, length us, event | category | flops | bytes accessed | tf_op | source)
XLA Modules:
  0.0 734.1 jit_solution(15743194792511780611)
XLA Ops:
  11.6 1.9 constant_dynamic-slice_fusion.8.columns
  18.3 122.1 %start_exchange.1 = (f32[8,4,192]{2,1,0:T(4,128)}, f32[4,4,1536]{2,1,0:T(4,128)}, bf16[8,192,1152]{2,1,0:T(8,128)(2,1)}, bf16[8,256,512]{2,1,0:T(8,128)(2,1)}, f...) custom-call(s32[1]{0:T(128)} %bitcast.1.clip, ...), custom_call_target="tpu_custom_call" | custom-call | tf_op jit(solution)/shard_map/start_exchange/pallas_call | solution.py:662
  140.4 2.4 slice.135
  142.8 1.7 multiply_reduce_fusion.11
  144.6 2.4 stack_reshape.7
  148.1 1.8 stack_reshape.6
  157.3 61.2 %attention_forward.1 = (bf16[4,256,384]{2,1,0:T(8,128)(2,1)}, bf16[1024,384]{1,0:T(8,128)(2,1)}, bf16[1024,384]{1,0:T(8,128)(2,1)}, bf16[1024,384]{1,0:T(8,128)(...) custom-call(s32[3,4]{1,0:T(4,128)} %pad_add_fusion.3.spans, ...), custom_call_target="tpu_custom_call" | custom-call | tf_op jit(solution)/shard_map/attention_forward/pallas_call | solution.py:1237
  221.7 3.9 multiply_reduce_fusion.10
  227.9 63.3 %ffn_forward.1 = (f32[256,1536]{1,0:T(8,128)}, bf16[8,256,1536]{2,1,0:T(8,128)(2,1)}, f32[8,256,1024]{2,1,0:T(8,128)}, bf16[8,256,512]{2,1,0:T(8,128)(2,1)}) custom-call(bf16[256,1536]{1,0:T(8,128)(2,1)} %multiply_convert_fusion.x, bf16[1536,1024]{1,0:T(8,128)(2,1)} %get-tuple-element.70.gate_up, bf16[512,1536]{1,0:T(8,128)(2,1)} %down.3), custom_call_target="tpu_custom_call" | custom-call | tf_op jit(solution)/shard_map/ffn_forward/pallas_call | solution.py:351
  294.2 1.9 fusion.12
  296.1 68.7 %ffn_backward.1 = (f32[256,1536]{1,0:T(8,128)}, bf16[1536,1024]{1,0:T(8,128)(2,1)}, bf16[512,1536]{1,0:T(8,128)(2,1)}) custom-call(bf16[256,1536]{1,0:T(8,128)(2,1)} %get-tuple-element.139.g, bf16[1536,1024]{1,0:T(8,128)(2,1)} %get-tuple-element.70.gate_up, bf16[512,1536]{1,0:T(8,128)(2,1)} %down.3, f32[8,256,1024]{2,1,0:T(8,128)} %get-tuple-element.72.values_in, ...), custom_call_target="tpu_custom_call" | custom-call | tf_op jit(solution)/shard_map/ffn_backward/pallas_call | solution.py:486
  364.8 2.7 multiply_reduce_fusion.2
  367.6 2.8 multiply_reduce_fusion.1
  372.4 94.5 %attention_backward.1 = (bf16[4,256,1152]{2,1,0:T(8,128)(2,1)}, f32[2,384]{1,0:T(2,128)}, f32[3,2,256]{2,1,0:T(2,128)}, bf16[4,2,4,64,384]{4,3,2,1,0:T(8,128)(2,...) custom-call(s32[3,4]{1,0:T(4,128)} %pad_add_fusion.3.spans, s32[4]{0:T(128)} %lengths.3, ...), custom_call_target="tpu_custom_call" | custom-call | tf_op jit(solution)/shard_map/attention_backward/pallas_call | solution.py:1448
  468.6 2.0 copy.85
  471.3 1.8 copy-done.1
  476.7 98.7 %end_exchange.1 = (f32[256,1536]{1,0:T(8,128)}, bf16[256,4096]{1,0:T(8,128)(2,1)}, bf16[512,3072]{1,0:T(8,128)(2,1)}, bf16[8,48,1024]{2,1,0:T(8,128)(2,1)}, bf16[128,1536]{1,0:T(8,128)(2,1)}) custom-call(bf16[256,3072]{1,0:T(8,128)(2,1)} %add_convert_fusion.pairs, bf16[512,3072]{1,0:T(8,128)(2,1)} %text.3, bf16[8,256,512]{2,1,0:T(8,128)(2,1)} %get-tuple-element.86.words, ...), custom_call_target="tpu_custom_call" | custom-call | tf_op jit(solution)/shard_map/end_exchange/pallas_call | solution.py:775
  575.5 3.0 fusion.9
  580.6 114.1 %final_sums.1 = (f32[128,1536]{1,0:T(8,128)}, f32[128,3072]{1,0:T(8,128)}, f32[48,1536]{1,0:T(8,128)}, f32[48,4608]{1,0:T(8,128)}, f32[48,8192]{1,0:T(8,128)}, /...) custom-call(s32[4]{0:T(128)} %flags.1, bf16[512,3072]{1,0:T(8,128)(2,1)} %get-tuple-element.93.text, ...), custom_call_target="tpu_custom_call" | custom-call | tf_op jit(solution)/shard_map/final_sums/pallas_call | solution.py:1005
  698.3 2.5 fusion.14
  700.8 2.6 convert_select_fusion
  703.4 1.9 collective-permute-start
  707.5 2.1 fusion.17
  712.2 8.6 %collective-permute-done = f32[8,4096]{1,0:T(8,128)S(1)} collective-permute-done((f32[8,4096]{1,0:T(8,128)S(1)}, f32[8,4096]{1,0:T(8,128)S(1)}, u32[]{:S(2)}, u32[]{:S(2)}) %collective-permute-start) | collective-permute-done | bytes 131104 | tf_op jit(solution)/shard_map/ppermute | solution.py:1720
  (181 shorter events, 49.5 us)
Async XLA Ops:
  7.2 214.5 %all-gather.2.cloned.1.call-start = ((), (), s32[]{:S(2)}) async-start(), calls=%async_computation | async-start | bytes 5308416 | tf_op jit(solution)/shard_map/all_gather | solution.py:1585
  9.4 566.0 %copy-start.23 = (f32[1536]{0:T(1024)}, f32[1536]{0:T(1024)S(1)}, u32[]{:S(2)}) copy-start(f32[1536]{0:T(1024)S(1)} %get-tuple-element.127) | copy-start | bytes 18436
  11.6 5.1 copy-start.33
  13.5 3.2 copy-start.15
  140.4 4.1 copy-start.26
  142.8 4.2 copy-start
  219.8 5.8 copy-start.13
  221.6 353.8 %copy-start.22 = (f32[1536]{0:T(1024)}, f32[1536]{0:T(1024)S(1)}, u32[]{:S(2)}) copy-start(f32[1536]{0:T(1024)S(1)} %get-tuple-element.123) | copy-start | bytes 18436
  221.7 3.9 copy-start.7
  226.7 247.2 %copy-start.28 = (f32[256]{0:T(256)}, f32[256]{0:T(256)S(1)}, u32[]{:S(2)}) copy-start(f32[256]{0:T(256)S(1)} %get-tuple-element.141) | copy-start | bytes 3076
  227.9 65.0 %copy-start.10 = (bf16[256,1536]{1,0:T(8,128)(2,1)S(1)}, bf16[256,1536]{1,0:T(8,128)(2,1)}, u32[]{:S(2)}) copy-start(bf16[256,1536]{1,0:T(8,128)(2,1)} %param.33) | copy-start | bytes 2359300
  364.8 2.7 copy-start.5
  364.8 2.7 copy-start.11
  474.0 101.4 %copy-start.27 = (f32[256]{0:T(256)}, f32[256]{0:T(256)S(1)}, u32[]{:S(2)}) copy-start(f32[256]{0:T(256)S(1)} %fusion.30) | copy-start | bytes 3076
  476.7 98.8 %copy-start.8 = (bf16[256,1536]{1,0:T(8,128)(2,1)S(1)}, bf16[256,1536]{1,0:T(8,128)(2,1)}, u32[]{:S(2)}) copy-start(bf16[256,1536]{1,0:T(8,128)(2,1)} %x.23) | copy-start | bytes 2359300
  575.4 3.3 copy-start.32
  580.6 117.7 %copy-start.3 = (f32[256,1536]{1,0:T(8,128)S(1)}, f32[256,1536]{1,0:T(8,128)}, u32[]{:S(2)}) copy-start(f32[256,1536]{1,0:T(8,128)} %copy-done.2) | copy-start | bytes 4718596
  580.6 117.7 %copy-start.12 = (f32[256,1536]{1,0:T(8,128)S(1)}, f32[256,1536]{1,0:T(8,128)}, u32[]{:S(2)}) copy-start(f32[256,1536]{1,0:T(8,128)} %get-tuple-element.91) | copy-start | bytes 4718596
  700.8 4.5 copy-start.25
  700.8 4.7 copy-start.24
  700.8 4.7 copy-start.20
  703.4 17.4 %collective-permute-start = (f32[8,4096]{1,0:T(8,128)S(1)}, f32[8,4096]{1,0:T(8,128)S(1)}, u32[]{:S(2)}, u32[]{:S(2)}) collective-permute-start(f32[8,4096]{1,0:T(8,128)S(1)} %copy-done.35), channel_id=1, source_target_pairs={{0,0},{1,8},{2,16},{3,24},{4,1},{5,9},{6,17},{7,25},{8,2},{9,10},{... | collective-permute-start | bytes 393224 | tf_op jit(solution)/shard_map/ppermute | solution.py:1720
  707.4 14.0 %copy-start.18 = (f32[48,4608]{1,0:T(8,128)S(1)}, f32[48,4608]{1,0:T(8,128)}, u32[]{:S(2)}) copy-start(f32[48,4608]{1,0:T(8,128)} %get-tuple-element.175) | copy-start | bytes 2654212
  707.5 14.9 %copy-start.17 = (f32[128,3072]{1,0:T(8,128)S(1)}, f32[128,3072]{1,0:T(8,128)}, u32[]{:S(2)}) copy-start(f32[128,3072]{1,0:T(8,128)} %get-tuple-element.176) | copy-start | bytes 4718596
  (15 other events, 26.5 us)
Sparse Core Ops, SparseCore 0:
  152.6 57.1 all-gather.1

commit v4 on v3

--- a/solution.py
+++ b/solution.py
@@ -445,14 +445,36 @@
     links.finish()
 
 
+class Late:
+    def __init__(self, source, target, semaphore):
+        self.copy = pltpu.make_async_copy(source, target, semaphore)
+        self.target, self.there = target, False
+        self.copy.start()
+
+    def get(self):
+        if not self.there:
+            self.copy.wait()
+            self.there = True
+        return self.target
+
+
 class GradientRing:
     def __init__(self, ring, own, held):
         self.ring, self.own, self.held = ring, own, held
-        self.copies = []
+        self.copies, self.pieces = [], {}
 
     def piece(self, which, step):
         place = self.ring.source(step + 1)
         return self.own[0].at[:, place] if which == 0 else self.own[1].at[place]
+
+    def fetch(self, first, targets, semaphores):
+        for slot in range(targets[0].shape[0]):
+            for which in range(2):
+                self.pieces[which, first + slot] = Late(
+                    self.piece(which, first + slot),
+                    targets[which].at[slot],
+                    semaphores.at[2 * slot + which],
+                )
 
     def first(self, landing):
         for which in range(2):
@@ -466,7 +488,8 @@
         self.copies = []
 
     def value(self, which, step):
-        return self.piece(which, step)[...].astype(wide) + self.held[which][...].astype(wide)
+        piece = self.pieces[which, step].get()
+        return piece[...].astype(wide) + self.held[which][...].astype(wide)
 
     def onward(self, step, going, landing):
         self.arrived()
@@ -524,8 +547,8 @@
 
 
 def start_kernel(
-    count, depth, clip, pieces, columns, shard, words, text, x, gain,
-    got, mods, projection, spread, pairs, normed, q, k, v, rates,
+    count, depth, clip, pieces, columns, shard, words, text, x, gain, text_gain,
+    got, mods, projection, spread, pairs, text_own, normed, q, k, v, rates,
     product, back, stat, stat_in, partial, core, outer, send, arrive,
 ):
     links = Transfers(send, arrive)
@@ -598,6 +621,18 @@
 
     def finish(half, total):
         pairs[pl.ds(half * exchange.rows, exchange.rows)] = total
+        keys = total[:, : width // 2]
+        rate = lax.rsqrt(jnp.mean(keys * keys, axis=1, keepdims=True) + EPSILON)
+        kinds = (keys * rate * text_gain[...]).astype(narrow), total[:, width // 2 :].astype(narrow)
+        cap_local, part = text_own.shape[3:]
+        for kind, value in enumerate(kinds):
+            for i in range(exchange.rows // cap_local):
+                place = half * (exchange.rows // cap_local) + i
+                rows = slice(i * cap_local, (i + 1) * cap_local)
+                for target in range(depth):
+                    text_own[target, kind, place] = value[
+                        rows, target * part : (target + 1) * part
+                    ]
 
     sums = exchange.scatter(finish)
     order = sorted(exchange.outer, key=lambda block: (bin(block).count("1"), block))
@@ -651,7 +686,9 @@
     links.finish()
 
 
-def start_exchange(count, depth, clip, pieces, columns, shard, words, text, x, gain):
+def start_exchange(
+    count, depth, clip, pieces, columns, shard, words, text, x, gain, text_gain
+):
     vmem = pl.BlockSpec(memory_space=pltpu.VMEM)
     rows, width = x.shape
     own = shard.shape[1] // 3
@@ -661,14 +698,15 @@
     raw = jax.ShapeDtypeStruct((depth, rows, own), wide)
     return pl.pallas_call(
         partial(start_kernel, count, depth),
-        in_specs=[scalar_spec()] + [vmem] * 7,
-        out_specs=[vmem] * 10,
+        in_specs=[scalar_spec()] + [vmem] * 8,
+        out_specs=[vmem] * 11,
         out_shape=[
             jax.ShapeDtypeStruct(pieces.shape, wide),
             jax.ShapeDtypeStruct((depth, places, mod_width), wide),
             jax.ShapeDtypeStruct((count,) + shard.shape, narrow),
             jax.ShapeDtypeStruct((count, cap_rows, words.shape[1] // count), narrow),
             jax.ShapeDtypeStruct((cap_rows, pair_width), wide),
+            jax.ShapeDtypeStruct((depth, 2, places, cap_rows // places, own), narrow),
             jax.ShapeDtypeStruct((depth, rows, width), narrow),
             raw,
             raw,
@@ -687,16 +725,29 @@
             collective_id=4, has_side_effects=True, vmem_limit_bytes=60 * 2**20
         ),
         name="start_exchange",
-    )(clip, pieces, columns, shard, words, text, x, gain)
+    )(clip, pieces, columns, shard, words, text, x, gain, text_gain)
 
 
 def end_kernel(
-    count, depth, pairs, text, words, grads, projection, grad_gate, grad_down, gate_held, down_held,
-    normed, grad_words, grad_weight, gate_next, down_next,
+    count, depth, pairs, text_hbm, words_hbm, grads_hbm, projection_hbm, grad_gate, grad_down,
+    gate_held, down_held, normed, grad_words, grad_weight, gate_next, down_next,
+    text, words, grads, projection, gate_piece, down_piece, local,
     plane, back, send_sum, ring_in, total, gate_go, down_go, send, arrive,
 ):
     links = Transfers(send, arrive)
     ring = Ring(depth, links)
+    late = [
+        Late(source, target, local.at[2 + i])
+        for i, (source, target) in enumerate(
+            zip(
+                (text_hbm, words_hbm, grads_hbm, projection_hbm),
+                (text, words, grads, projection),
+                strict=True,
+            )
+        )
+    ]
+    weights = GradientRing(ring, (grad_gate, grad_down), (gate_held, down_held))
+    weights.fetch(1, (gate_piece, down_piece), local)
     b = lax.axis_index("bucket")
     others = [partner(k) for k in range(1, count)]
     meet(others + [ring.left, ring.right])
@@ -719,8 +770,6 @@
 
     steps = [0]
 
-    weights = GradientRing(ring, (grad_gate, grad_down), (gate_held, down_held))
-
     def advance():
         if steps[0] < depth - 1:
             round_step(steps[0])
@@ -734,6 +783,8 @@
         blocks[block_index(block, count)] = block
 
     def compute(places):
+        for copy in late:
+            copy.get()
         for place in places:
             block = blocks[place]
             features = words[jnp.bitwise_xor(b, block)].astype(wide).T.astype(narrow)
@@ -774,7 +825,7 @@
     copies = plane_copies(count)[0] + count - 1 + depth - 1 + 2
     return pl.pallas_call(
         partial(end_kernel, count, depth),
-        in_specs=[vmem] * 9,
+        in_specs=[vmem] + [pl.BlockSpec(memory_space=pl.ANY)] * 6 + [vmem] * 2,
         out_specs=[vmem] * 5,
         out_shape=[
             jax.ShapeDtypeStruct((rows, width), wide),
@@ -784,6 +835,13 @@
             jax.ShapeDtypeStruct(held[1].shape, narrow),
         ],
         scratch_shapes=[
+            pltpu.VMEM(text.shape, narrow),
+            pltpu.VMEM(words.shape, narrow),
+            pltpu.VMEM(grads.shape, narrow),
+            pltpu.VMEM(projection.shape, narrow),
+            pltpu.VMEM((1,) + held[0].shape, narrow),
+            pltpu.VMEM((1,) + held[1].shape, narrow),
+            pltpu.SemaphoreType.DMA((6,)),
             pltpu.VMEM((count, cap_rows, pair_width), narrow),
             pltpu.VMEM((count - 1, cap_rows, feature), narrow),
             pltpu.VMEM((depth - 1, rows, width), narrow),
@@ -802,14 +860,22 @@
 
 
 def sum_kernel(
-    count, depth, flags, text, combined, upstream, normed, grads, grad_gate, grad_down, gate_held,
-    down_held, words, row, small, down_share, text_share, output_share, proj_share, gate_share, null_share, rows_out, small_out,
-    out_part, out_core, out_outer, proj_part, proj_core, proj_outer, send_low, low_in, out_go,
+    count, depth, flags, text, combined, upstream, normed_hbm, grads_hbm, grad_gate, grad_down,
+    gate_held, down_held, words_hbm, row, small, down_share, text_share, output_share, proj_share, gate_share, null_share, rows_out, small_out,
+    normed, grads, words, gate_piece, down_piece, local, out_part, out_core, out_outer, proj_part, proj_core, proj_outer, send_low, low_in, out_go,
     out_come, proj_go, proj_come, gate, gate_come, null, null_come, small_come, small_go,
     small_land, gate_go, down_go, gate_land, down_land, send, arrive,
 ):
     links = Transfers(send, arrive)
     ring = Ring(depth, links)
+    late = [
+        Late(source, target, local.at[i])
+        for i, (source, target) in enumerate(
+            zip((normed_hbm, grads_hbm, words_hbm), (normed, grads, words), strict=True)
+        )
+    ]
+    weights = GradientRing(ring, (grad_gate, grad_down), (gate_held, down_held))
+    weights.fetch(2, (gate_piece, down_piece), local.at[pl.ds(3, 2 * (depth - 2))])
     b, s = lax.axis_index("bucket"), lax.axis_index("seq")
     others = [partner(k) for k in range(1, count)]
     turns = [lax.rem(s + step, depth) for step in range(1, depth)]
@@ -837,8 +903,6 @@
         else:
             text_share[...] = value
 
-    weights = GradientRing(ring, (grad_gate, grad_down), (gate_held, down_held))
-
     def weights_step(step):
         slot = step - 2
         weights.onward(
@@ -874,6 +938,8 @@
 
     fill(out_part, combined[...], upstream[...])
     out_sums = plane_sum(out_part, out_core, out_outer, out_go)
+    for copy in late:
+        copy.get()
     fill(proj_part, flat(normed[...]), flat(grads[...]))
     proj_sums = plane_sum(proj_part, proj_core, proj_outer, proj_go)
     for _ in range(count // 4):
@@ -1002,9 +1068,15 @@
     copies += 2 * (depth - 1) + 2 * (depth - 3)
     gate, down = held
     gates = pltpu.VMEM(gate.shape, narrow)
+    anywhere = pl.BlockSpec(memory_space=pl.ANY)
     return pl.pallas_call(
         partial(sum_kernel, count, depth),
-        in_specs=[scalar_spec()] + [vmem] * 12,
+        in_specs=[scalar_spec()]
+        + [vmem] * 3
+        + [anywhere] * 4
+        + [vmem] * 2
+        + [anywhere]
+        + [vmem] * 2,
         out_specs=[vmem] * 8,
         out_shape=[
             jax.ShapeDtypeStruct(down.shape, wide),
@@ -1016,7 +1088,15 @@
             jax.ShapeDtypeStruct((count, depth) + row.shape, wide),
             jax.ShapeDtypeStruct(small.shape[2:], wide),
         ],
-        scratch_shapes=plane_sums(width)
+        scratch_shapes=[
+            pltpu.VMEM(normed.shape, narrow),
+            pltpu.VMEM(grads.shape, narrow),
+            pltpu.VMEM(words.shape, narrow),
+            pltpu.VMEM((depth - 2,) + gate.shape, narrow),
+            pltpu.VMEM((depth - 2,) + down.shape, narrow),
+            pltpu.SemaphoreType.DMA((3 + 2 * (depth - 2),)),
+        ]
+        + plane_sums(width)
         + plane_sums(own3)
         + [
             pltpu.VMEM(quarter, narrow),
@@ -1264,9 +1344,11 @@
 
 
 def backward_kernel(
-    count, depth, size, lanes, spans, lengths, gates, upstream, weight, q, k, v, qc, raw_q, raw_k,
-    rates, gain_q, gain_k, cosine, sine, text, total, cross_total, small, grad_gate, grad_down,
-    projected, gain_sums, dgate, grad_text, small_out, gate_held, down_held, go, send_go, dqc, back_q, back_k, parts, send_text, stat,
+    count, depth, size, lanes, spans, lengths, gates, upstream, weight, q, k_hbm, v_hbm, qc, raw_q_hbm,
+    raw_k_hbm, rates, gain_q, gain_k, cosine, sine, text, total, cross_total, small, text_gain, text_pairs,
+    grad_gate, grad_down,
+    projected, gain_sums, dgate, grad_pairs, text_gain_sum, small_out, gate_held, down_held,
+    k, v, raw_q, raw_k, cosine_in, sine_in, pairs_in, local, grad_text, go, send_go, dqc, back_q, back_k, parts, send_text, stat,
     stat_in, sum_k, sum_v, send, arrive,
 ):
     links = Transfers(send, arrive)
@@ -1274,6 +1356,17 @@
     others = [partner(k) for k in range(1, count)]
     turns = [lax.rem(s + step, depth) for step in range(1, depth)]
     along = [seq_device(place) for place in turns]
+    late = [
+        Late(source, target, local.at[i])
+        for i, (source, target) in enumerate(
+            zip(
+                (k_hbm, v_hbm, raw_q_hbm, raw_k_hbm, cosine, sine, text_pairs),
+                (k, v, raw_q, raw_k, cosine_in, sine_in, pairs_in),
+                strict=True,
+            )
+        )
+    ]
+    cosine, sine = cosine_in, sine_in
     meet(others + along)
     block_rows, own = upstream.shape[0], q.shape[1]
     rows = depth * block_rows
@@ -1364,6 +1457,8 @@
         copy.wait_recv()
     spread = [links.start(small_out.at[0], small_out.at[k], others[k - 1]) for k in range(1, count)]
 
+    for copy in late:
+        copy.get()
     key_index = lax.broadcasted_iota(jnp.int32, (rows, block_rows), 0)
 
     def back_self(group):
@@ -1428,14 +1523,38 @@
             projected[block, :, i * own : (i + 1) * own] = (
                 rate * (back[at] * gain[...] - hat * means[:, place])
             ).astype(narrow)
-    for copy in words + spread + weights.copies:
+    for copy in words:
+        copy.wait_recv()
+
+    for target in range(depth):
+        text_gain_sum[:, target * own : (target + 1) * own] = jnp.zeros((1, own), wide)
+    for place in range(places):
+        at = slice(place * cap_local, (place + 1) * cap_local)
+        keys = pairs_in[at, :width]
+        rate = lax.rsqrt(jnp.mean(keys * keys, axis=1, keepdims=True) + EPSILON)
+        mean = jnp.zeros((cap_local, 1), wide)
+        for target in range(depth):
+            span = slice(target * own, (target + 1) * own)
+            hat = pairs_in[at, span] * rate
+            grad = grad_text[target, 0, place].astype(wide)
+            mean = mean + jnp.sum(grad * text_gain[:, span] * hat, axis=1, keepdims=True)
+            text_gain_sum[:, span] += jnp.sum(grad * hat, axis=0, keepdims=True)
+        mean = mean / width
+        for target in range(depth):
+            span = slice(target * own, (target + 1) * own)
+            hat = pairs_in[at, span] * rate
+            grad = grad_text[target, 0, place].astype(wide)
+            grad_pairs[at, span] = (rate * (grad * text_gain[:, span] - hat * mean)).astype(narrow)
+            after = slice(width + target * own, width + (target + 1) * own)
+            grad_pairs[at, after] = grad_text[target, 1, place]
+    for copy in spread + weights.copies:
         copy.wait_recv()
     links.finish()
 
 
 def attention_backward(
     count, depth, size, lanes, scalars, upstream, weight, saved, raws, rates, gains, angles, text,
-    totals, small, ffn_grads,
+    totals, small, text_gain, text_pairs, ffn_grads,
 ):
     block_rows, own = raws[0].shape[1:]
     rows = depth * block_rows
@@ -1444,21 +1563,35 @@
     copies = 4 * (depth - 1) + count - 1 + 2
     cap = text.shape[0] * text.shape[3]
     args = (*scalars, upstream, weight, *saved, *raws, rates, *gains, *angles, text, *totals, small)
-    args = args + tuple(ffn_grads)
+    args = args + (text_gain, text_pairs) + tuple(ffn_grads)
+    anywhere = pl.BlockSpec(memory_space=pl.ANY)
+    specs = [scalar_spec()] * 3 + [vmem] * (len(args) - 3)
+    for i in (6, 7, 9, 10, 14, 15, len(args) - 3, len(args) - 2, len(args) - 1):
+        specs[i] = anywhere
     return pl.pallas_call(
         partial(backward_kernel, count, depth, size, lanes),
-        in_specs=[scalar_spec()] * 3 + [vmem] * (len(args) - 3),
-        out_specs=[vmem] * 7,
+        in_specs=specs,
+        out_specs=[vmem] * 8,
         out_shape=[
             jax.ShapeDtypeStruct((depth, block_rows, 3 * own), narrow),
             jax.ShapeDtypeStruct((2, own), wide),
             jax.ShapeDtypeStruct((grid, heads, block_rows), wide),
-            jax.ShapeDtypeStruct(text.shape, narrow),
+            jax.ShapeDtypeStruct(text_pairs.shape, narrow),
+            jax.ShapeDtypeStruct((1, own * depth), wide),
             jax.ShapeDtypeStruct((count, depth) + small.shape, wide),
             jax.ShapeDtypeStruct(ffn_grads[0].shape[:1] + ffn_grads[0].shape[2:], narrow),
             jax.ShapeDtypeStruct(ffn_grads[1].shape[1:], narrow),
         ],
         scratch_shapes=[
+            pltpu.VMEM((rows, own), narrow),
+            pltpu.VMEM((rows, own), narrow),
+            pltpu.VMEM(raws[0].shape, wide),
+            pltpu.VMEM(raws[1].shape, wide),
+            pltpu.VMEM(angles[0].shape, wide),
+            pltpu.VMEM(angles[1].shape, wide),
+            pltpu.VMEM(text_pairs.shape, wide),
+            pltpu.SemaphoreType.DMA((7,)),
+            pltpu.VMEM(text.shape, narrow),
             pltpu.VMEM((depth, block_rows, own), narrow),
             pltpu.VMEM((depth - 1, block_rows, own), narrow),
             pltpu.VMEM((rows, own), wide),
@@ -1539,6 +1672,7 @@
         own_projection,
         words,
         text_pairs,
+        text_own,
         normed,
         raw_q,
         raw_k,
@@ -1555,15 +1689,12 @@
         text_weight,
         tokens,
         norm_gains[:1],
+        head_gains[2:],
     )
     own_projection = own_projection.reshape(width, 3 * own)
     modulated = lax.dynamic_index_in_dim(mods, my_clip, 1, keepdims=False).reshape(1, 4 * width)
     tokens_in = tokens.astype(wide)
     _, pre_pull = jax.vjp(pre_attention, tokens_in, modulated, norm_gains)
-
-    text_outs, text_pull = jax.vjp(text_heads, text_pairs, head_gains[2])
-    text_own = jnp.stack([o.astype(narrow).reshape(cap_rows, count_s, own) for o in text_outs])
-    text_own = text_own.transpose(2, 0, 1, 3).reshape(count_s, 2, places, cap_local, own)
 
     gains = [lax.dynamic_slice_in_dim(head_gains[i : i + 1], s * own, own, 1) for i in range(2)]
     inside = lax.rem(jnp.arange(rows, dtype=jnp.int32), clip_length)
@@ -1625,29 +1756,29 @@
         (grad_middle, grad_normed_ffn)
     )
     grad_attended_low = grad_attended.astype(narrow)
-    grad_projected, gain_sums, grad_gates, grad_kv, early, *held = attention_backward(
-        count_b,
-        count_s,
-        size,
-        lanes,
-        scalars,
-        grad_attended_low,
-        full_output,
-        saved,
-        (raw_q, raw_k),
-        rates,
-        gains,
-        (cosine, sine),
-        text_kv,
-        (total, cross_total),
-        (grad_modulated_post + grad_modulated_last)[:, width:],
-        ffn_grads,
-    )
-
-    grad_kv = grad_kv.reshape(count_s, 2, cap_rows, own)
-    grad_kv = grad_kv.transpose(1, 2, 0, 3).reshape(2, cap_rows, width).astype(wide)
-    grad_pairs, grad_gain_text = text_pull((grad_kv[0], grad_kv[1]))
-    grad_pairs_low = grad_pairs.astype(narrow)
+    grad_projected, gain_sums, grad_gates, grad_pairs_low, text_gain_sum, early, *held = (
+        attention_backward(
+            count_b,
+            count_s,
+            size,
+            lanes,
+            scalars,
+            grad_attended_low,
+            full_output,
+            saved,
+            (raw_q, raw_k),
+            rates,
+            gains,
+            (cosine, sine),
+            text_kv,
+            (total, cross_total),
+            (grad_modulated_post + grad_modulated_last)[:, width:],
+            head_gains[2:],
+            text_pairs,
+            ffn_grads,
+        )
+    )
+
     grad_normed, grad_words, grad_text, *held = end_exchange(
         count_b,
         count_s,
@@ -1678,7 +1809,7 @@
                 [
                     place(gain_sums[0]),
                     place(gain_sums[1]),
-                    grad_gain_text,
+                    text_gain_sum[0],
                     jnp.zeros((width,), wide),
                 ]
             ),

time: 746 us -> 716 us (0.960)
  local copies, waits for them, and re-layouts: 38.6 us -> 26.8 us
  Pallas kernels: 623 us -> 612 us
  transfers between devices with their start and end apart: 2 -> 2, of which waited for: 1 -> 1; matrix products, arithmetic and copies ran while one was open for 2% -> 2% of each run, Pallas kernels for 8% -> 9%
where the time goes in v4:
time: 716 us; the launch traced here: 705 us
  Pallas kernels  612 us (85%)
  other arithmetic  33 us (5%)
  local copies, waits for them, and re-layouts  26.8 us (4%)
  between operations  15.8 us (2%)
  waiting for transfers between devices  8.68 us (1%)
    pallas_call x1, Pallas kernels, start_exchange(): pl.pallas_call(partial(start_kernel, count, depth), in_specs=[scalar_spec...  122 us
    pallas_call x1, Pallas kernels, final_sums(): pl.pallas_call(partial(sum_kernel, count, depth), in_specs=[scalar_spec()...  111 us
    pallas_call x1, Pallas kernels, end_exchange(): pl.pallas_call(partial(end_kernel, count, depth), in_specs=[vmem] + [pl.B...  94.6 us
    pallas_call x1, Pallas kernels, attention_backward(): pl.pallas_call(partial(backward_kernel, count, depth, size, lanes), in_sp...  92.3 us
    pallas_call x1, Pallas kernels, ffn_backward(): pl.pallas_call(partial(ffn_back_kernel, count), in_specs=[vmem] * 3 + [an...  68.5 us
    pallas_call x1, Pallas kernels, ffn_forward(): pl.pallas_call(partial(ffn_kernel, count), in_specs=[vmem] * 3, out_specs...  63 us
    pallas_call x1, Pallas kernels, attention_forward(): pl.pallas_call(partial(forward_kernel, count, depth, size, lanes), in_spe...  61.2 us
  transfers between devices with their start and end apart: 2, of which 1 were waited for; matrix products, arithmetic and copies ran while one was open for 2% of the time, Pallas kernels for 9%

profile of v4, /device:TPU:4, one launch (start us, length us, event | category | flops | bytes accessed | tf_op | source)
XLA Modules:
  0.0 704.7 jit_solution(2012185955552403868)
XLA Ops:
  7.9 1.5 slice_reduce_fusion.5
  11.6 1.5 fusion.33
  13.0 1.9 constant_dynamic-slice_fusion.8.columns
  18.1 1.6 broadcast_select_fusion
  19.7 122.4 %start_exchange.1 = (f32[8,4,192]{2,1,0:T(4,128)}, f32[4,4,1536]{2,1,0:T(4,128)}, bf16[8,192,1152]{2,1,0:T(8,128)(2,1)}, bf16[8,256,512]{2,1,0:T(8,128)(2,1)}, f...) custom-call(s32[1]{0:T(128)} %bitcast.1.clip, ...), custom_call_target="tpu_custom_call" | custom-call | tf_op jit(solution)/shard_map/start_exchange/pallas_call | solution.py:699
  147.1 61.2 %attention_forward.1 = (bf16[4,256,384]{2,1,0:T(8,128)(2,1)}, bf16[1024,384]{1,0:T(8,128)(2,1)}, bf16[1024,384]{1,0:T(8,128)(2,1)}, bf16[1024,384]{1,0:T(8,128)(...) custom-call(s32[3,4]{1,0:T(4,128)} %pad_add_fusion.3.spans, ...), custom_call_target="tpu_custom_call" | custom-call | tf_op jit(solution)/shard_map/attention_forward/pallas_call | solution.py:1317
  211.4 3.9 multiply_reduce_fusion.8
  217.6 63.0 %ffn_forward.1 = (f32[256,1536]{1,0:T(8,128)}, bf16[8,256,1536]{2,1,0:T(8,128)(2,1)}, f32[8,256,1024]{2,1,0:T(8,128)}, bf16[8,256,512]{2,1,0:T(8,128)(2,1)}) custom-call(bf16[256,1536]{1,0:T(8,128)(2,1)} %multiply_convert_fusion.x, bf16[1536,1024]{1,0:T(8,128)(2,1)} %get-tuple-element.72.gate_up, bf16[512,1536]{1,0:T(8,128)(2,1)} %down.3), custom_call_target="tpu_custom_call" | custom-call | tf_op jit(solution)/shard_map/ffn_forward/pallas_call | solution.py:351
  280.6 1.7 multiply_reduce_fusion.6
  283.6 1.9 fusion.12
  285.5 68.5 %ffn_backward.1 = (f32[256,1536]{1,0:T(8,128)}, bf16[1536,1024]{1,0:T(8,128)(2,1)}, bf16[512,1536]{1,0:T(8,128)(2,1)}) custom-call(bf16[256,1536]{1,0:T(8,128)(2,1)} %get-tuple-element.139.g, bf16[1536,1024]{1,0:T(8,128)(2,1)} %get-tuple-element.72.gate_up, bf16[512,1536]{1,0:T(8,128)(2,1)} %down.3, f32[8,256,1024]{2,1,0:T(8,128)} %get-tuple-element.74.values_in, ...), custom_call_target="tpu_custom_call" | custom-call | tf_op jit(solution)/shard_map/ffn_backward/pallas_call | solution.py:509
  354.0 2.7 multiply_reduce_fusion.1
  356.7 2.8 multiply_reduce_fusion
  361.6 92.3 %attention_backward.1 = (bf16[4,256,1152]{2,1,0:T(8,128)(2,1)}, f32[2,384]{1,0:T(2,128)}, f32[3,2,256]{2,1,0:T(2,128)}, bf16[256,3072]{1,0:T(8,128)(2,1)}, f32[1...) custom-call(s32[3,4]{1,0:T(4,128)} %pad_add_fusion.3.spans, ...), custom_call_target="tpu_custom_call" | custom-call | tf_op jit(solution)/shard_map/attention_backward/pallas_call | solution.py:1571
  455.1 94.6 %end_exchange.1 = (f32[256,1536]{1,0:T(8,128)}, bf16[256,4096]{1,0:T(8,128)(2,1)}, bf16[512,3072]{1,0:T(8,128)(2,1)}, bf16[8,48,1024]{2,1,0:T(8,128)(2,1)}, bf16[128,1536]{1,0:T(8,128)(2,1)}) custom-call(bf16[256,3072]{1,0:T(8,128)(2,1)} %get-tuple-element.88.pairs, bf16[512,3072]{1,0:T(8,128)(2,1)} %text_hbm.1, ...), custom_call_target="tpu_custom_call" | custom-call | tf_op jit(solution)/shard_map/end_exchange/pallas_call | solution.py:826
  549.8 3.0 fusion.9
  554.6 110.5 %final_sums.1 = (f32[128,1536]{1,0:T(8,128)}, f32[128,3072]{1,0:T(8,128)}, f32[48,1536]{1,0:T(8,128)}, f32[48,4608]{1,0:T(8,128)}, f32[48,8192]{1,0:T(8,128)}, /...) custom-call(s32[4]{0:T(128)} %flags.1, bf16[512,3072]{1,0:T(8,128)(2,1)} %get-tuple-element.96.text, ...), custom_call_target="tpu_custom_call" | custom-call | tf_op jit(solution)/shard_map/final_sums/pallas_call | solution.py:1072
  666.5 1.5 slice_reduce_fusion
  668.8 2.5 fusion.14
  671.3 2.6 convert_select_fusion
  673.9 1.9 collective-permute-start
  676.0 1.6 reduce.10
  678.0 2.1 fusion.17
  682.6 8.6 %collective-permute-done = f32[8,4096]{1,0:T(8,128)S(1)} collective-permute-done((f32[8,4096]{1,0:T(8,128)S(1)}, f32[8,4096]{1,0:T(8,128)S(1)}, u32[]{:S(2)}, u32[]{:S(2)}) %collective-permute-start) | collective-permute-done | bytes 131104 | tf_op jit(solution)/shard_map/ppermute | solution.py:1851
  (148 shorter events, 33.0 us)
Async XLA Ops:
  7.2 204.2 %all-gather.2.cloned.1.call-start = ((), (), s32[]{:S(2)}) async-start(), calls=%async_computation | async-start | bytes 5308416 | tf_op jit(solution)/shard_map/all_gather | solution.py:1716
  9.4 540.4 %copy-start.20 = (f32[1536]{0:T(1024)}, f32[1536]{0:T(1024)S(1)}, u32[]{:S(2)}) copy-start(f32[1536]{0:T(1024)S(1)} %get-tuple-element.129) | copy-start | bytes 18436
  11.6 6.5 copy-start.29
  14.9 3.2 copy-start.12
  19.7 122.4 %copy-start.32 = (f32[24]{0:T(128)S(1)}, f32[24]{0:T(128)}, u32[]{:S(2)}) copy-start(f32[24]{0:T(128)} %param.32) | copy-start | bytes 292
  209.5 5.8 copy-start.11
  211.4 338.4 %copy-start.19 = (f32[1536]{0:T(1024)}, f32[1536]{0:T(1024)S(1)}, u32[]{:S(2)}) copy-start(f32[1536]{0:T(1024)S(1)} %get-tuple-element.125) | copy-start | bytes 18436
  211.4 3.9 copy-start.5
  216.4 143.2 %copy-start.24 = (f32[256]{0:T(256)}, f32[256]{0:T(256)S(1)}, u32[]{:S(2)}) copy-start(f32[256]{0:T(256)S(1)} %get-tuple-element.141) | copy-start | bytes 3076
  217.6 64.7 %copy-start.8 = (bf16[256,1536]{1,0:T(8,128)(2,1)S(1)}, bf16[256,1536]{1,0:T(8,128)(2,1)}, u32[]{:S(2)}) copy-start(bf16[256,1536]{1,0:T(8,128)(2,1)} %param.33) | copy-start | bytes 2359300
  354.0 2.8 copy-start.3
  354.0 2.8 copy-start.9
  359.6 190.2 %copy-start.23 = (f32[256]{0:T(256)}, f32[256]{0:T(256)S(1)}, u32[]{:S(2)}) copy-start(f32[256]{0:T(256)S(1)} %fusion.29) | copy-start | bytes 3076
  455.1 94.7 %copy-start.6 = (bf16[256,1536]{1,0:T(8,128)(2,1)S(1)}, bf16[256,1536]{1,0:T(8,128)(2,1)}, u32[]{:S(2)}) copy-start(bf16[256,1536]{1,0:T(8,128)(2,1)} %x.19) | copy-start | bytes 2359300
  549.7 3.1 copy-start.28
  549.7 3.2 copy-start.26
  554.5 114.2 %copy-start.1 = (f32[256,1536]{1,0:T(8,128)S(1)}, f32[256,1536]{1,0:T(8,128)}, u32[]{:S(2)}) copy-start(f32[256,1536]{1,0:T(8,128)} %copy-done) | copy-start | bytes 4718596
  554.6 114.2 %copy-start.10 = (f32[256,1536]{1,0:T(8,128)S(1)}, f32[256,1536]{1,0:T(8,128)}, u32[]{:S(2)}) copy-start(f32[256,1536]{1,0:T(8,128)} %get-tuple-element.94) | copy-start | bytes 4718596
  671.2 4.5 copy-start.22
  671.2 4.7 copy-start.21
  671.2 4.7 copy-start.17
  673.9 17.4 %collective-permute-start = (f32[8,4096]{1,0:T(8,128)S(1)}, f32[8,4096]{1,0:T(8,128)S(1)}, u32[]{:S(2)}, u32[]{:S(2)}) collective-permute-start(f32[8,4096]{1,0:T(8,128)S(1)} %copy-done.31), channel_id=1, source_target_pairs={{0,0},{1,8},{2,16},{3,24},{4,1},{5,9},{6,17},{7,25},{8,2},{9,10},{... | collective-permute-start | bytes 393224 | tf_op jit(solution)/shard_map/ppermute | solution.py:1851
  677.9 14.0 %copy-start.15 = (f32[48,4608]{1,0:T(8,128)S(1)}, f32[48,4608]{1,0:T(8,128)}, u32[]{:S(2)}) copy-start(f32[48,4608]{1,0:T(8,128)} %get-tuple-element.175) | copy-start | bytes 2654212
  678.0 14.8 %copy-start.14 = (f32[128,3072]{1,0:T(8,128)S(1)}, f32[128,3072]{1,0:T(8,128)}, u32[]{:S(2)}) copy-start(f32[128,3072]{1,0:T(8,128)} %get-tuple-element.176) | copy-start | bytes 4718596
  (11 other events, 20.6 us)
Sparse Core Ops, SparseCore 0:
  142.2 56.9 all-gather.1

commit v5 on v4

--- a/solution.py
+++ b/solution.py
@@ -288,11 +288,25 @@
             lax.fori_loop(first, end, lambda i, _: (body(i), 0)[1], 0)
 
 
+class Late:
+    def __init__(self, source, target, semaphore):
+        self.copy = pltpu.make_async_copy(source, target, semaphore)
+        self.target, self.there = target, False
+        self.copy.start()
+
+    def get(self):
+        if not self.there:
+            self.copy.wait()
+            self.there = True
+        return self.target
+
+
 def ffn_kernel(
-    count, x, gate_up, down, lowered, plane_out, values_out, hidden_out,
-    plane, partial, core, outer, values, hidden, send, arrive, local,
+    count, x, gate_up_hbm, down_hbm, lowered, plane_out, values_out, hidden_out,
+    gate_up, down, plane, partial, core, outer, values, hidden, send, arrive, local,
 ):
     links = Transfers(send, arrive)
+    late = Late(gate_up_hbm, gate_up, local.at[3]), Late(down_hbm, down, local.at[4])
     meet(plane_partners(count))
     units = down.shape[0]
     wide_block = 256
@@ -300,6 +314,9 @@
     saved = pltpu.make_async_copy(plane, plane_out, local.at[0])
 
     def compute(blocks):
+        for copy in late:
+            copy.get()
+
         def one(place):
             for start in range(0, units, wide_block):
                 columns = slice(start, start + wide_block)
@@ -350,7 +367,7 @@
     vmem, anywhere = pl.BlockSpec(memory_space=pltpu.VMEM), pl.BlockSpec(memory_space=pl.ANY)
     return pl.pallas_call(
         partial(ffn_kernel, count),
-        in_specs=[vmem] * 3,
+        in_specs=[vmem] + [anywhere] * 2,
         out_specs=[vmem] + [anywhere] * 3,
         out_shape=[
             jax.ShapeDtypeStruct((rows, width), wide),
@@ -358,13 +375,14 @@
             jax.ShapeDtypeStruct((count, rows, 2 * units), wide),
             jax.ShapeDtypeStruct((count, rows, units), narrow),
         ],
-        scratch_shapes=plane_scratch(count, rows, width)
+        scratch_shapes=[pltpu.VMEM(gate_up.shape, narrow), pltpu.VMEM(down.shape, narrow)]
+        + plane_scratch(count, rows, width)
         + [
             pltpu.VMEM((count, rows, 2 * units), wide),
             pltpu.VMEM((count, rows, units), narrow),
             pltpu.SemaphoreType.DMA((copies,)),
             pltpu.SemaphoreType.DMA((copies,)),
-            pltpu.SemaphoreType.DMA((3,)),
+            pltpu.SemaphoreType.DMA((5,)),
         ],
         compiler_params=pltpu.CompilerParams(
             collective_id=1, has_side_effects=True, vmem_limit_bytes=60 * 2**20
@@ -373,10 +391,12 @@
     )(x, gate_up, down)
 
 def ffn_back_kernel(
-    count, g, gate_up, down, values_in, x_in, hidden_in, grad_normed, grad_gate_up, grad_down,
-    plane, partial, core, outer, values, grads, taken, send, arrive, local,
+    count, g, gate_up_hbm, down_hbm, values_in, x_in, hidden_in, grad_normed, grad_gate_up,
+    grad_down, gate_up, down, plane, partial, core, outer, values, grads, taken, send, arrive,
+    local,
 ):
     links = Transfers(send, arrive)
+    late = Late(down_hbm, down, local.at[4]), Late(gate_up_hbm, gate_up, local.at[3])
     fetch = pltpu.make_async_copy(values_in, values, local.at[2])
     fetch.start()
     meet(plane_partners(count))
@@ -389,6 +409,8 @@
         if not fetched:
             fetch.wait()
             fetched.append(True)
+            for copy in late:
+                copy.get()
 
         def one(place):
             for start in range(0, units, wide_block):
@@ -445,19 +467,6 @@
     links.finish()
 
 
-class Late:
-    def __init__(self, source, target, semaphore):
-        self.copy = pltpu.make_async_copy(source, target, semaphore)
-        self.target, self.there = target, False
-        self.copy.start()
-
-    def get(self):
-        if not self.there:
-            self.copy.wait()
-            self.there = True
-        return self.target
-
-
 class GradientRing:
     def __init__(self, ring, own, held):
         self.ring, self.own, self.held = ring, own, held
@@ -508,21 +517,22 @@
     vmem, anywhere = pl.BlockSpec(memory_space=pltpu.VMEM), pl.BlockSpec(memory_space=pl.ANY)
     return pl.pallas_call(
         partial(ffn_back_kernel, count),
-        in_specs=[vmem] * 3 + [anywhere] * 3,
+        in_specs=[vmem] + [anywhere] * 5,
         out_specs=[vmem] * 3,
         out_shape=[
             jax.ShapeDtypeStruct((rows, width), wide),
             jax.ShapeDtypeStruct((width, 2 * units), narrow),
             jax.ShapeDtypeStruct((units, width), narrow),
         ],
-        scratch_shapes=plane_scratch(count, rows, width)
+        scratch_shapes=[pltpu.VMEM(gate_up.shape, narrow), pltpu.VMEM(down.shape, narrow)]
+        + plane_scratch(count, rows, width)
         + [
             pltpu.VMEM((count, rows, 2 * units), wide),
             pltpu.VMEM((count, rows, 2 * units), narrow),
             pltpu.VMEM((2, count, rows, 256), narrow),
             pltpu.SemaphoreType.DMA((copies,)),
             pltpu.SemaphoreType.DMA((copies,)),
-            pltpu.SemaphoreType.DMA((3,)),
+            pltpu.SemaphoreType.DMA((5,)),
         ],
         compiler_params=pltpu.CompilerParams(
             collective_id=2, has_side_effects=True, vmem_limit_bytes=62 * 2**20
@@ -547,11 +557,12 @@
 
 
 def start_kernel(
-    count, depth, clip, pieces, columns, shard, words, text, x, gain, text_gain,
+    count, depth, clip, pieces, columns, shard, words, text_hbm, x, gain, text_gain,
     got, mods, projection, spread, pairs, text_own, normed, q, k, v, rates,
-    product, back, stat, stat_in, partial, core, outer, send, arrive,
+    text, local, product, back, stat, stat_in, partial, core, outer, send, arrive,
 ):
     links = Transfers(send, arrive)
+    late = Late(text_hbm, text, local.at[0])
     ring = Ring(depth, links)
     b, s = lax.axis_index("bucket"), lax.axis_index("seq")
     others = [partner(k) for k in range(1, count)]
@@ -577,13 +588,13 @@
         links.start(product.at[block], back.at[block - 1], others[block - 1])
         for block in range(1, count)
     ]
+    shards = PlaneExchange(count, links, projection, natural=True).gather()
+    next(shards)
     far = {}
     for block in sorted(range(1, count), key=lambda block: (bin(block >> 1).count("1"), block & 1)):
         far[block] = links.start(
             features(jnp.bitwise_xor(b, block)), spread.at[b], others[block - 1]
         )
-    shards = PlaneExchange(count, links, projection, natural=True).gather()
-    next(shards)
 
     total = product[0]
     for i, copy in enumerate(second):
@@ -605,6 +616,7 @@
     rate = lax.rsqrt(jnp.mean(value * value, axis=1, keepdims=True) + EPSILON)
     normed[s] = (value * rate * gain[...] * (1.0 + scale)).astype(narrow)
     moving = [links.start(normed.at[s], normed.at[s], ring.right)]
+    next(shards)
 
     exchange = PlaneExchange(count, links, None, partial, core, outer)
 
@@ -634,6 +646,7 @@
                         rows, target * part : (target + 1) * part
                     ]
 
+    late.get()
     sums = exchange.scatter(finish)
     order = sorted(exchange.outer, key=lambda block: (bin(block).count("1"), block))
     order = order[1:] + order[:1]
@@ -641,11 +654,6 @@
     for block in order[:levels]:
         pair(block | 1)
         pair(block)
-    next(sums)
-    for block in order[levels:]:
-        pair(block | 1)
-        pair(block)
-    next(sums)
     own = q.shape[2]
 
     def project(step):
@@ -661,16 +669,22 @@
         if step < depth - 1:
             moving.append(links.start(normed.at[place], normed.at[place], ring.right))
 
+    next(sums)
     onward(1)
+    for block in order[levels:]:
+        pair(block | 1)
+        pair(block)
+    next(sums)
     for _ in shards:
         pass
     project(0)
     project(1)
-    for step in range(2, depth):
-        if step == depth - 1:
-            next(sums)
+    for step in range(2, depth - 1):
         onward(step)
         project(step)
+    next(sums)
+    onward(depth - 1)
+    project(depth - 1)
     for i, raw in enumerate((q, k)):
         for block in range(depth):
             place = i * depth + block
@@ -698,7 +712,7 @@
     raw = jax.ShapeDtypeStruct((depth, rows, own), wide)
     return pl.pallas_call(
         partial(start_kernel, count, depth),
-        in_specs=[scalar_spec()] + [vmem] * 8,
+        in_specs=[scalar_spec()] + [vmem] * 4 + [pl.BlockSpec(memory_space=pl.ANY)] + [vmem] * 3,
         out_specs=[vmem] * 11,
         out_shape=[
             jax.ShapeDtypeStruct(pieces.shape, wide),
@@ -714,6 +728,8 @@
             jax.ShapeDtypeStruct((2 * depth, rows), wide),
         ],
         scratch_shapes=[
+            pltpu.VMEM(text.shape, narrow),
+            pltpu.SemaphoreType.DMA((1,)),
             pltpu.VMEM((count, places, mod_width), wide),
             pltpu.VMEM((count - 1, places, mod_width), wide),
             pltpu.VMEM((2 * depth, rows), wide),
@@ -861,10 +877,10 @@
 
 def sum_kernel(
     count, depth, flags, text, combined, upstream, normed_hbm, grads_hbm, grad_gate, grad_down,
-    gate_held, down_held, words_hbm, row, small, down_share, text_share, output_share, proj_share, gate_share, null_share, rows_out, small_out,
+    gate_held, down_held, words_hbm, row, small, early, conditions, mod_share, down_share, text_share, output_share, proj_share, gate_share, null_share, rows_out, small_out,
     normed, grads, words, gate_piece, down_piece, local, out_part, out_core, out_outer, proj_part, proj_core, proj_outer, send_low, low_in, out_go,
     out_come, proj_go, proj_come, gate, gate_come, null, null_come, small_come, small_go,
-    small_land, gate_go, down_go, gate_land, down_land, send, arrive,
+    small_land, gate_go, down_go, gate_land, down_land, cond_rows, all_rows, send, arrive,
 ):
     links = Transfers(send, arrive)
     ring = Ring(depth, links)
@@ -1017,6 +1033,27 @@
     for i in range(count - 1):
         sums = sums + small_land[i]
     small_out[...] = sums
+
+    width = row.shape[1]
+    for block in range(count):
+        for source in range(depth):
+            at = slice(block * depth + source, block * depth + source + 1)
+            value = jnp.zeros((1, share), wide)
+            for place in range(places):
+                mark = rows_out[block, source, 1:2, 128 + place : 129 + place]
+                value = value + mark * conditions[block, place : place + 1]
+            cond_rows[at] = value
+            all_rows[at, :width] = rows_out[block, source, 0:1]
+            all_rows[at, width:] = early[block, source]
+    for first in range(0, 4 * width, 1536):
+        columns = slice(first, first + 1536)
+        mod_share[:, columns] = lax.dot_general(
+            cond_rows[...],
+            all_rows[:, columns],
+            (((0,), (0,)), ((), ())),
+            precision=HIGHEST,
+            preferred_element_type=wide,
+        )
     for copy in far:
         copy.wait_recv()
     units = gate.shape[2] // 2
@@ -1044,7 +1081,8 @@
 
 
 def final_sums(
-    count, depth, flags, text, combined, upstream, normed, grads, ffn_grads, held, words, row, small
+    count, depth, flags, text, combined, upstream, normed, grads, ffn_grads, held, words, row, small,
+    early, conditions,
 ):
     vmem = pl.BlockSpec(memory_space=pltpu.VMEM)
     feature, pair_width = text.shape
@@ -1076,9 +1114,10 @@
         + [anywhere] * 4
         + [vmem] * 2
         + [anywhere]
-        + [vmem] * 2,
-        out_specs=[vmem] * 8,
+        + [vmem] * 4,
+        out_specs=[vmem] * 9,
         out_shape=[
+            jax.ShapeDtypeStruct((share, 4 * width), wide),
             jax.ShapeDtypeStruct(down.shape, wide),
             jax.ShapeDtypeStruct((feature // depth, pair_width), wide),
             jax.ShapeDtypeStruct((share, width), wide),
@@ -1116,6 +1155,8 @@
             pltpu.VMEM((depth - 3,) + down.shape, narrow),
             pltpu.VMEM((depth - 3,) + gate.shape, narrow),
             pltpu.VMEM((depth - 3,) + down.shape, narrow),
+            pltpu.VMEM((count * depth, share), wide),
+            pltpu.VMEM((count * depth, 4 * width), wide),
             pltpu.SemaphoreType.DMA((copies,)),
             pltpu.SemaphoreType.DMA((copies,)),
         ],
@@ -1123,7 +1164,7 @@
             collective_id=10, has_side_effects=True, vmem_limit_bytes=60 * 2**20
         ),
         name="final_sums",
-    )(flags, text, combined, upstream, normed, grads, *ffn_grads, *held, words, row, small)
+    )(flags, text, combined, upstream, normed, grads, *ffn_grads, *held, words, row, small, early, conditions)
 
 
 def head_lanes(values, head, size):
@@ -1185,11 +1226,21 @@
 
 
 def forward_kernel(
-    count, depth, size, lanes, spans, lengths, gates, raw_q, raw_k, raw_v, rates, gain_q, gain_k,
-    cosine, sine, text_own, gate_up, combined, q, k, v, qc, total, cross_total, text, gathered,
-    self_out, staged, send, arrive, local,
+    count, depth, size, lanes, spans, lengths, gates, raw_q_hbm, raw_k_hbm, raw_v_hbm, rates, gain_q,
+    gain_k, cosine_hbm, sine_hbm, text_own, gate_up, combined, q, k, v, qc, total, cross_total, text, gathered,
+    raw_q, raw_k, raw_v, cosine, sine, self_out, staged, send, arrive, local,
 ):
     links = Transfers(send, arrive)
+    late = [
+        Late(source, target, local.at[2 + i])
+        for i, (source, target) in enumerate(
+            zip(
+                (raw_v_hbm, raw_q_hbm, raw_k_hbm, cosine_hbm, sine_hbm),
+                (raw_v, raw_q, raw_k, cosine, sine),
+                strict=True,
+            )
+        )
+    ]
     b, s = lax.axis_index("bucket"), lax.axis_index("seq")
     others = [partner(k) for k in range(1, count)]
     turns = [lax.rem(s + step, depth) for step in range(1, depth)]
@@ -1222,6 +1273,8 @@
                 copy = pltpu.make_async_copy(source, landing, local.at[half])
                 copy.start()
                 kept.append(copy)
+    for copy in late:
+        copy.get()
     for block in range(depth):
         v[block_rows_of(block, block_rows)] = raw_v[block].astype(narrow)
     columns = rates[...].T
@@ -1316,7 +1369,11 @@
     totals = jax.ShapeDtypeStruct((grid, heads, rows), wide)
     return pl.pallas_call(
         partial(forward_kernel, count, depth, size, lanes),
-        in_specs=[scalar_spec()] * 3 + [vmem] * 9 + [anywhere],
+        in_specs=[scalar_spec()] * 3
+        + [anywhere] * 3
+        + [vmem] * 3
+        + [anywhere] * 2
+        + [vmem, anywhere],
         out_specs=[vmem] * 9,
         out_shape=[
             jax.ShapeDtypeStruct((depth, block_rows, own), narrow),
@@ -1330,11 +1387,16 @@
             jax.ShapeDtypeStruct((count * gate_up.shape[0], 2 * units), narrow),
         ],
         scratch_shapes=[
+            pltpu.VMEM(raws[0].shape, wide),
+            pltpu.VMEM(raws[0].shape, wide),
+            pltpu.VMEM(raws[0].shape, wide),
+            pltpu.VMEM(angles[0].shape, wide),
+            pltpu.VMEM(angles[0].shape, wide),
             pltpu.VMEM((rows, own), wide),
             pltpu.VMEM((depth, block_rows, own), narrow),
             pltpu.SemaphoreType.DMA((copies,)),
             pltpu.SemaphoreType.DMA((copies,)),
-            pltpu.SemaphoreType.DMA((2,)),
+            pltpu.SemaphoreType.DMA((7,)),
         ],
         compiler_params=pltpu.CompilerParams(
             collective_id=8, has_side_effects=True, vmem_limit_bytes=60 * 2**20
@@ -1825,6 +1887,7 @@
     )
     row = jnp.stack([grad_modulated_pre[0, :width], row], axis=0)
     (
+        mod_share,
         down_share,
         text_share,
         output_share,
@@ -1847,6 +1910,8 @@
         grad_words,
         row,
         small.reshape(8, count_b, count_s, share).transpose(2, 1, 0, 3),
+        early,
+        lax.dynamic_slice_in_dim(cond_columns, s * share, share, 2),
     )
     null_share = lax.ppermute(
         null_share,
@@ -1856,15 +1921,6 @@
     grad_words = grad_words.reshape(places, cap_local, text_width).astype(wide)
     grad_captions = jnp.where(is_null, 0.0, grad_words)
 
-    cond_own = lax.dynamic_slice_in_dim(cond_columns, s * share, share, 2)
-    at_clip = grad_rows[:, :, 1, 128 : 128 + places]
-    cond_rows = jnp.sum(at_clip[:, :, :, None] * cond_own[:, None], axis=2)
-    mod_share = lax.dot_general(
-        flat(cond_rows),
-        jnp.concatenate([flat(grad_rows[:, :, 0]), flat(early)], axis=1),
-        (((0,), (0,)), ((), ())),
-        precision=HIGHEST,
-    )
     return (
         mixed.astype(narrow),
         grad_tokens,

time: 716 us -> 694 us (0.969)
  Pallas kernels: 612 us -> 598 us
    pallas_call x1, Pallas kernels: 122 us -> 111 us  [start_exchange(): pl.pallas_call(partial(start_kernel, count, depth), in_specs=[scalar_spec...]
where the time goes in v5:
time: 694 us; the launch traced here: 684 us
  Pallas kernels  598 us (86%)
  other arithmetic  28.7 us (4%)
  local copies, waits for them, and re-layouts  24.4 us (4%)
  between operations  15.5 us (2%)
  waiting for transfers between devices  11.6 us (2%)
    pallas_call x1, Pallas kernels, start_exchange(): pl.pallas_call(partial(start_kernel, count, depth), in_specs=[scalar_spec...  111 us
    pallas_call x1, Pallas kernels, final_sums(): pl.pallas_call(partial(sum_kernel, count, depth), in_specs=[scalar_spec()...  111 us
    pallas_call x1, Pallas kernels, end_exchange(): pl.pallas_call(partial(end_kernel, count, depth), in_specs=[vmem] + [pl.B...  94.7 us
    pallas_call x1, Pallas kernels, attention_backward(): pl.pallas_call(partial(backward_kernel, count, depth, size, lanes), in_sp...  91.5 us
    pallas_call x1, Pallas kernels, ffn_backward(): pl.pallas_call(partial(ffn_back_kernel, count), in_specs=[vmem] + [anywhe...  67.2 us
    pallas_call x1, Pallas kernels, ffn_forward(): pl.pallas_call(partial(ffn_kernel, count), in_specs=[vmem] + [anywhere] *...  61.5 us
    pallas_call x1, Pallas kernels, attention_forward(): pl.pallas_call(partial(forward_kernel, count, depth, size, lanes), in_spe...  60.1 us
  transfers between devices with their start and end apart: 2, of which 1 were waited for; matrix products, arithmetic and copies ran while one was open for 2% of the time, Pallas kernels for 9%

profile of v5, /device:TPU:4, one launch (start us, length us, event | category | flops | bytes accessed | tf_op | source)
XLA Modules:
  0.0 683.9 jit_solution(13152038944386544555)
XLA Ops:
  7.9 1.5 slice_reduce_fusion.4
  11.5 1.5 fusion.28
  13.0 1.9 constant_dynamic-slice_fusion.8.columns
  14.9 1.2 constant_dynamic-slice_fusion.4
  18.1 1.6 broadcast_select_fusion
  19.7 111.5 %start_exchange.1 = (f32[8,4,192]{2,1,0:T(4,128)}, f32[4,4,1536]{2,1,0:T(4,128)}, bf16[8,192,1152]{2,1,0:T(8,128)(2,1)}, bf16[8,256,512]{2,1,0:T(8,128)(2,1)}, f...) custom-call(s32[1]{0:T(128)} %bitcast.1.clip, ...), custom_call_target="tpu_custom_call" | custom-call | tf_op jit(solution)/shard_map/start_exchange/pallas_call | solution.py:713
  136.1 60.1 %attention_forward.1 = (bf16[4,256,384]{2,1,0:T(8,128)(2,1)}, bf16[1024,384]{1,0:T(8,128)(2,1)}, bf16[1024,384]{1,0:T(8,128)(2,1)}, bf16[1024,384]{1,0:T(8,128)(...) custom-call(s32[3,4]{1,0:T(4,128)} %pad_add_fusion.3.spans, ...), custom_call_target="tpu_custom_call" | custom-call | tf_op jit(solution)/shard_map/attention_forward/pallas_call | solution.py:1370
  199.4 3.9 multiply_reduce_fusion.8
  205.5 61.5 %ffn_forward.1 = (f32[256,1536]{1,0:T(8,128)}, bf16[8,256,1536]{2,1,0:T(8,128)(2,1)}, f32[8,256,1024]{2,1,0:T(8,128)}, bf16[8,256,512]{2,1,0:T(8,128)(2,1)}) custom-call(bf16[256,1536]{1,0:T(8,128)(2,1)} %multiply_convert_fusion.x, bf16[1536,1024]{1,0:T(8,128)(2,1)} %get-tuple-element.73.gate_up_hbm, bf16[512,1536]{1,0:T(8,128)(2,1)} %down_hbm.3), custom_call_target="tpu_custom_call" | custom-call | tf_op jit(solution)/shard_map/ffn_forward/pallas_call | solution.py:368
  267.1 1.7 multiply_reduce_fusion.6
  270.1 1.9 fusion.12
  272.0 67.2 %ffn_backward.1 = (f32[256,1536]{1,0:T(8,128)}, bf16[1536,1024]{1,0:T(8,128)(2,1)}, bf16[512,1536]{1,0:T(8,128)(2,1)}) custom-call(bf16[256,1536]{1,0:T(8,128)(2,1)} %get-tuple-element.141.g, bf16[1536,1024]{1,0:T(8,128)(2,1)} %get-tuple-element.73.gate_up_hbm, bf16[512,1536]{1,0:T(8,128)(2,1)} %down_hbm.3, f32[8,256,1024]{2,1,0:T(8,128)} %get-tuple-element.75.values_in, ...), custom_call_target="tpu_custom_call" | custom-call | tf_op jit(solution)/shard_map/ffn_backward/pallas_call | solution.py:518
  339.2 2.7 multiply_reduce_fusion.1
  341.9 2.8 multiply_reduce_fusion
  344.8 1.3 fusion.13.upstream
  346.8 91.5 %attention_backward.1 = (bf16[4,256,1152]{2,1,0:T(8,128)(2,1)}, f32[2,384]{1,0:T(2,128)}, f32[3,2,256]{2,1,0:T(2,128)}, bf16[256,3072]{1,0:T(8,128)(2,1)}, f32[1...) custom-call(s32[3,4]{1,0:T(4,128)} %pad_add_fusion.3.spans, ...), custom_call_target="tpu_custom_call" | custom-call | tf_op jit(solution)/shard_map/attention_backward/pallas_call | solution.py:1633
  438.3 94.7 %end_exchange.1 = (f32[256,1536]{1,0:T(8,128)}, bf16[256,4096]{1,0:T(8,128)(2,1)}, bf16[512,3072]{1,0:T(8,128)(2,1)}, bf16[8,48,1024]{2,1,0:T(8,128)(2,1)}, bf16[128,1536]{1,0:T(8,128)(2,1)}) custom-call(bf16[256,3072]{1,0:T(8,128)(2,1)} %get-tuple-element.89.pairs, bf16[512,3072]{1,0:T(8,128)(2,1)} %text_hbm.3, ...), custom_call_target="tpu_custom_call" | custom-call | tf_op jit(solution)/shard_map/end_exchange/pallas_call | solution.py:842
  533.0 2.6 fusion.9
  535.7 2.6 convert_select_fusion
  540.6 111.2 %final_sums.1 = (f32[48,6144]{1,0:T(8,128)}, f32[128,1536]{1,0:T(8,128)}, f32[128,3072]{1,0:T(8,128)}, f32[48,1536]{1,0:T(8,128)}, f32[48,4608]{1,0:T(8,128)}, /...) custom-call(s32[4]{0:T(128)} %flags.1, ...), custom_call_target="tpu_custom_call" | custom-call | tf_op jit(solution)/shard_map/final_sums/pallas_call | solution.py:1110
  651.9 2.1 collective-permute-start
  654.0 1.6 fusion.14
  656.7 1.3 slice_reduce_fusion
  658.0 11.6 %collective-permute-done = f32[8,4096]{1,0:T(8,128)S(1)} collective-permute-done((f32[8,4096]{1,0:T(8,128)}, f32[8,4096]{1,0:T(8,128)S(1)}, u32[]{:S(2)}, u32[]{:S(2)}) %collective-permute-start) | collective-permute-done | bytes 131104 | tf_op jit(solution)/shard_map/ppermute | solution.py:1916
  (123 shorter events, 26.9 us)
Async XLA Ops:
  7.2 192.2 %all-gather.2.cloned.1.call-start = ((), (), s32[]{:S(2)}) async-start(), calls=%async_computation | async-start | bytes 5308416 | tf_op jit(solution)/shard_map/all_gather | solution.py:1778
  14.9 3.2 copy-start.12
  19.7 111.5 %copy-start.24 = (f32[24]{0:T(128)S(1)}, f32[24]{0:T(128)}, u32[]{:S(2)}) copy-start(f32[24]{0:T(128)} %param.32) | copy-start | bytes 292
  197.5 5.8 copy-start.11
  199.4 3.9 copy-start.5
  205.5 63.3 %copy-start.8 = (bf16[256,1536]{1,0:T(8,128)(2,1)S(1)}, bf16[256,1536]{1,0:T(8,128)(2,1)}, u32[]{:S(2)}) copy-start(bf16[256,1536]{1,0:T(8,128)(2,1)} %param.33) | copy-start | bytes 2359300
  267.1 1.9 copy-start.4
  339.2 2.7 copy-start.3
  339.2 2.7 copy-start.9
  344.8 1.4 copy-start
  438.3 94.7 %copy-start.6 = (bf16[256,1536]{1,0:T(8,128)(2,1)S(1)}, bf16[256,1536]{1,0:T(8,128)(2,1)}, u32[]{:S(2)}) copy-start(bf16[256,1536]{1,0:T(8,128)(2,1)} %x.19) | copy-start | bytes 2359300
  533.0 2.6 copy-start.7
  535.6 2.6 copy-start.21
  535.7 3.3 copy-start.23
  535.7 3.4 copy-start.20
  540.6 113.3 %copy-start.1 = (f32[256,1536]{1,0:T(8,128)S(1)}, f32[256,1536]{1,0:T(8,128)}, u32[]{:S(2)}) copy-start(f32[256,1536]{1,0:T(8,128)} %copy-done) | copy-start | bytes 4718596
  540.6 113.3 %copy-start.10 = (f32[256,1536]{1,0:T(8,128)S(1)}, f32[256,1536]{1,0:T(8,128)}, u32[]{:S(2)}) copy-start(f32[256,1536]{1,0:T(8,128)} %get-tuple-element.95) | copy-start | bytes 4718596
  651.9 3.7 copy-start.22
  651.9 18.4 %copy-start.15 = (f32[48,6144]{1,0:T(8,128)S(1)}, f32[48,6144]{1,0:T(8,128)}, u32[]{:S(2)}) copy-start(f32[48,6144]{1,0:T(8,128)} %get-tuple-element.176) | copy-start | bytes 3538948
  651.9 17.7 %collective-permute-start = (f32[8,4096]{1,0:T(8,128)}, f32[8,4096]{1,0:T(8,128)S(1)}, u32[]{:S(2)}, u32[]{:S(2)}) collective-permute-start(f32[8,4096]{1,0:T(8,128)} %get-tuple-element.106), channel_id=1, source_target_pairs={{0,0},{1,8},{2,16},{3,24},{4,1},{5,9},{6,17},{7,25},{8,2},{9,10},{... | collective-permute-start | bytes 393224 | tf_op jit(solution)/shard_map/ppermute | solution.py:1916
  655.6 15.7 %copy-start.16 = (f32[48,4608]{1,0:T(8,128)S(1)}, f32[48,4608]{1,0:T(8,128)}, u32[]{:S(2)}) copy-start(f32[48,4608]{1,0:T(8,128)} %get-tuple-element.177) | copy-start | bytes 2654212
  670.3 1.9 copy-start.14
  672.2 2.1 copy-start.13
  674.3 1.7 copy-start.17
  (3 other events, 3.6 us)
Sparse Core Ops, SparseCore 0:
  131.4 56.0 all-gather.1

commit v6 on v5

--- a/solution.py
+++ b/solution.py
@@ -557,12 +557,15 @@
 
 
 def start_kernel(
-    count, depth, clip, pieces, columns, shard, words, text_hbm, x, gain, text_gain,
+    count, depth, clip, pieces, modulation, shard, words, text_hbm, x, gain, text_gain,
     got, mods, projection, spread, pairs, text_own, normed, q, k, v, rates,
-    text, local, product, back, stat, stat_in, partial, core, outer, send, arrive,
+    text, columns, local, product, back, stat, stat_in, partial, core, outer, send, arrive,
 ):
     links = Transfers(send, arrive)
     late = Late(text_hbm, text, local.at[0])
+    mod_width = columns.shape[1]
+    at = pl.multiple_of(lax.axis_index("seq") * mod_width, 128)
+    own_columns = Late(modulation.at[:, pl.ds(at, mod_width)], columns, local.at[1])
     ring = Ring(depth, links)
     b, s = lax.axis_index("bucket"), lax.axis_index("seq")
     others = [partner(k) for k in range(1, count)]
@@ -582,6 +585,7 @@
     spread[b] = words[:, pl.ds(pl.multiple_of(b * feature, 128), feature)]
     for copy in first:
         copy.wait_recv()
+    own_columns.get()
     for block in range(count):
         product[block] = dense(got[block].astype(narrow), columns[...])
     second = [
@@ -614,7 +618,7 @@
     scale = parts[0] if len(parts) == 1 else jnp.concatenate(parts, axis=1)
     value = x[...].astype(wide)
     rate = lax.rsqrt(jnp.mean(value * value, axis=1, keepdims=True) + EPSILON)
-    normed[s] = (value * rate * gain[...] * (1.0 + scale)).astype(narrow)
+    normed[s] = (value * rate * gain[0:1] * (1.0 + scale)).astype(narrow)
     moving = [links.start(normed.at[s], normed.at[s], ring.right)]
     next(shards)
 
@@ -635,7 +639,7 @@
         pairs[pl.ds(half * exchange.rows, exchange.rows)] = total
         keys = total[:, : width // 2]
         rate = lax.rsqrt(jnp.mean(keys * keys, axis=1, keepdims=True) + EPSILON)
-        kinds = (keys * rate * text_gain[...]).astype(narrow), total[:, width // 2 :].astype(narrow)
+        kinds = (keys * rate * text_gain[2:3]).astype(narrow), total[:, width // 2 :].astype(narrow)
         cap_local, part = text_own.shape[3:]
         for kind, value in enumerate(kinds):
             for i in range(exchange.rows // cap_local):
@@ -701,18 +705,18 @@
 
 
 def start_exchange(
-    count, depth, clip, pieces, columns, shard, words, text, x, gain, text_gain
+    count, depth, clip, pieces, modulation, shard, words, text, x, gain, text_gain
 ):
-    vmem = pl.BlockSpec(memory_space=pltpu.VMEM)
+    vmem, anywhere = pl.BlockSpec(memory_space=pltpu.VMEM), pl.BlockSpec(memory_space=pl.ANY)
     rows, width = x.shape
     own = shard.shape[1] // 3
     cap_rows, pair_width = words.shape[0], text.shape[1]
-    places, mod_width = pieces.shape[1], columns.shape[1]
+    places, mod_width = pieces.shape[1], modulation.shape[1] // depth
     copies = sum(plane_copies(count)) + 3 * (count - 1) + 3 * (depth - 1)
     raw = jax.ShapeDtypeStruct((depth, rows, own), wide)
     return pl.pallas_call(
         partial(start_kernel, count, depth),
-        in_specs=[scalar_spec()] + [vmem] * 4 + [pl.BlockSpec(memory_space=pl.ANY)] + [vmem] * 3,
+        in_specs=[scalar_spec(), vmem, anywhere, vmem, vmem, anywhere] + [vmem] * 3,
         out_specs=[vmem] * 11,
         out_shape=[
             jax.ShapeDtypeStruct(pieces.shape, wide),
@@ -729,7 +733,8 @@
         ],
         scratch_shapes=[
             pltpu.VMEM(text.shape, narrow),
-            pltpu.SemaphoreType.DMA((1,)),
+            pltpu.VMEM((modulation.shape[0], mod_width), narrow),
+            pltpu.SemaphoreType.DMA((2,)),
             pltpu.VMEM((count, places, mod_width), wide),
             pltpu.VMEM((count - 1, places, mod_width), wide),
             pltpu.VMEM((2 * depth, rows), wide),
@@ -741,7 +746,7 @@
             collective_id=4, has_side_effects=True, vmem_limit_bytes=60 * 2**20
         ),
         name="start_exchange",
-    )(clip, pieces, columns, shard, words, text, x, gain, text_gain)
+    )(clip, pieces, modulation, shard, words, text, x, gain, text_gain)
 
 
 def end_kernel(
@@ -967,13 +972,14 @@
     places = flags.shape[0]
     cap_local = words.shape[0] // places
     null_rows = null.shape[1]
-    for k in range(count):
-        value = jnp.zeros((null_rows, words.shape[1]), wide)
+    for first in range(0, words.shape[1], 512):
+        columns = slice(first, first + 512)
+        value = jnp.zeros((cap_local, 512), wide)
         for place in range(places):
-            first = place * cap_local + k * null_rows
-            part = words[first : first + null_rows].astype(wide)
+            part = words[place * cap_local : (place + 1) * cap_local, columns].astype(wide)
             value = value + jnp.where(flags[place] == 1, part, 0.0)
-        null[k] = value
+        for k in range(count):
+            null[k, :, columns] = value[k * null_rows : (k + 1) * null_rows]
     next(out_sums)
     next(proj_sums)
     nulls = [
@@ -1725,7 +1731,6 @@
     )
 
     silu_cond = jax.nn.silu(condition).astype(narrow)
-    mod_width = modulation.shape[1] // count_s
     pieces = silu_cond.astype(wide).reshape(places, count_b, -1).transpose(1, 0, 2)
     my_clip = (s * local) // clip_length
     (
@@ -1745,13 +1750,13 @@
         count_s,
         my_clip.astype(jnp.int32)[None],
         pieces,
-        lax.dynamic_slice_in_dim(modulation, s * mod_width, mod_width, 1),
+        modulation,
         own_projection,
         words_own,
         text_weight,
         tokens,
-        norm_gains[:1],
-        head_gains[2:],
+        norm_gains,
+        head_gains,
     )
     own_projection = own_projection.reshape(width, 3 * own)
     modulated = lax.dynamic_index_in_dim(mods, my_clip, 1, keepdims=False).reshape(1, 4 * width)

time: 694 us -> 689 us (level)
  no operation moved by 1% of the time
where the time goes in v6:
time: 689 us; the launch traced here: 680 us
  Pallas kernels  598 us (87%)
  other arithmetic  28.9 us (4%)
  local copies, waits for them, and re-layouts  20 us (3%)
  between operations  15.7 us (2%)
  waiting for transfers between devices  11.4 us (2%)
    pallas_call x1, Pallas kernels, start_exchange(): pl.pallas_call(partial(start_kernel, count, depth), in_specs=[scalar_spec...  111 us
    pallas_call x1, Pallas kernels, final_sums(): pl.pallas_call(partial(sum_kernel, count, depth), in_specs=[scalar_spec()...  111 us
    pallas_call x1, Pallas kernels, end_exchange(): pl.pallas_call(partial(end_kernel, count, depth), in_specs=[vmem] + [pl.B...  95.1 us
    pallas_call x1, Pallas kernels, attention_backward(): pl.pallas_call(partial(backward_kernel, count, depth, size, lanes), in_sp...  91.5 us
    pallas_call x1, Pallas kernels, ffn_backward(): pl.pallas_call(partial(ffn_back_kernel, count), in_specs=[vmem] + [anywhe...  67.2 us
    pallas_call x1, Pallas kernels, ffn_forward(): pl.pallas_call(partial(ffn_kernel, count), in_specs=[vmem] + [anywhere] *...  61.6 us
    pallas_call x1, Pallas kernels, attention_forward(): pl.pallas_call(partial(forward_kernel, count, depth, size, lanes), in_spe...  59.5 us
  transfers between devices with their start and end apart: 2, of which 1 were waited for; matrix products, arithmetic and copies ran while one was open for 2% of the time, Pallas kernels for 9%

profile of v6, /device:TPU:4, one launch (start us, length us, event | category | flops | bytes accessed | tf_op | source)
XLA Modules:
  0.0 679.5 jit_solution(1319416676613504985)
XLA Ops:
  13.2 1.6 broadcast_select_fusion
  14.8 111.4 %start_exchange.1 = (f32[8,4,192]{2,1,0:T(4,128)}, f32[4,4,1536]{2,1,0:T(4,128)}, bf16[8,192,1152]{2,1,0:T(8,128)(2,1)}, bf16[8,256,512]{2,1,0:T(8,128)(2,1)}, f...) custom-call(s32[1]{0:T(128)} %bitcast.1.clip, ...), custom_call_target="tpu_custom_call" | custom-call | tf_op jit(solution)/shard_map/start_exchange/pallas_call | solution.py:717
  131.8 59.5 %attention_forward.1 = (bf16[4,256,384]{2,1,0:T(8,128)(2,1)}, bf16[1024,384]{1,0:T(8,128)(2,1)}, bf16[1024,384]{1,0:T(8,128)(2,1)}, bf16[1024,384]{1,0:T(8,128)(...) custom-call(s32[3,4]{1,0:T(4,128)} %pad_add_fusion.3.spans, ...), custom_call_target="tpu_custom_call" | custom-call | tf_op jit(solution)/shard_map/attention_forward/pallas_call | solution.py:1376
  191.3 1.2 copy.38
  194.5 3.9 multiply_reduce_fusion.8
  199.5 1.1 multiply_convert_fusion.x
  200.7 61.6 %ffn_forward.1 = (f32[256,1536]{1,0:T(8,128)}, bf16[8,256,1536]{2,1,0:T(8,128)(2,1)}, f32[8,256,1024]{2,1,0:T(8,128)}, bf16[8,256,512]{2,1,0:T(8,128)(2,1)}) custom-call(bf16[256,1536]{1,0:T(8,128)(2,1)} %multiply_convert_fusion.x, bf16[1536,1024]{1,0:T(8,128)(2,1)} %get-tuple-element.73.gate_up_hbm, bf16[512,1536]{1,0:T(8,128)(2,1)} %down_hbm.3), custom_call_target="tpu_custom_call" | custom-call | tf_op jit(solution)/shard_map/ffn_forward/pallas_call | solution.py:368
  262.2 1.7 multiply_reduce_fusion.6
  265.2 1.9 fusion.12
  267.1 67.2 %ffn_backward.1 = (f32[256,1536]{1,0:T(8,128)}, bf16[1536,1024]{1,0:T(8,128)(2,1)}, bf16[512,1536]{1,0:T(8,128)(2,1)}) custom-call(bf16[256,1536]{1,0:T(8,128)(2,1)} %get-tuple-element.141.g, bf16[1536,1024]{1,0:T(8,128)(2,1)} %get-tuple-element.73.gate_up_hbm, bf16[512,1536]{1,0:T(8,128)(2,1)} %down_hbm.3, f32[8,256,1024]{2,1,0:T(8,128)} %get-tuple-element.75.values_in, ...), custom_call_target="tpu_custom_call" | custom-call | tf_op jit(solution)/shard_map/ffn_backward/pallas_call | solution.py:518
  334.4 2.8 multiply_reduce_fusion.1
  337.2 2.8 multiply_reduce_fusion
  340.1 1.3 fusion.13.upstream
  342.1 91.5 %attention_backward.1 = (bf16[4,256,1152]{2,1,0:T(8,128)(2,1)}, f32[2,384]{1,0:T(2,128)}, f32[3,2,256]{2,1,0:T(2,128)}, bf16[256,3072]{1,0:T(8,128)(2,1)}, f32[1...) custom-call(s32[3,4]{1,0:T(4,128)} %pad_add_fusion.3.spans, ...), custom_call_target="tpu_custom_call" | custom-call | tf_op jit(solution)/shard_map/attention_backward/pallas_call | solution.py:1639
  433.6 95.1 %end_exchange.1 = (f32[256,1536]{1,0:T(8,128)}, bf16[256,4096]{1,0:T(8,128)(2,1)}, bf16[512,3072]{1,0:T(8,128)(2,1)}, bf16[8,48,1024]{2,1,0:T(8,128)(2,1)}, bf16[128,1536]{1,0:T(8,128)(2,1)}) custom-call(bf16[256,3072]{1,0:T(8,128)(2,1)} %get-tuple-element.89.pairs, bf16[512,3072]{1,0:T(8,128)(2,1)} %text_hbm.3, ...), custom_call_target="tpu_custom_call" | custom-call | tf_op jit(solution)/shard_map/end_exchange/pallas_call | solution.py:847
  528.8 2.6 fusion.9
  531.4 2.6 convert_select_fusion
  536.4 111.3 %final_sums.1 = (f32[48,6144]{1,0:T(8,128)}, f32[128,1536]{1,0:T(8,128)}, f32[128,3072]{1,0:T(8,128)}, f32[48,1536]{1,0:T(8,128)}, f32[48,4608]{1,0:T(8,128)}, /...) custom-call(s32[4]{0:T(128)} %flags.1, ...), custom_call_target="tpu_custom_call" | custom-call | tf_op jit(solution)/shard_map/final_sums/pallas_call | solution.py:1116
  647.7 2.1 collective-permute-start
  649.7 1.6 fusion.14
  652.5 1.3 slice_reduce_fusion
  653.8 11.4 %collective-permute-done = f32[8,4096]{1,0:T(8,128)S(1)} collective-permute-done((f32[8,4096]{1,0:T(8,128)}, f32[8,4096]{1,0:T(8,128)S(1)}, u32[]{:S(2)}, u32[]{:S(2)}) %collective-permute-start) | collective-permute-done | bytes 131104 | tf_op jit(solution)/shard_map/ppermute | solution.py:1921
  667.8 1.1 copy.58
  669.9 1.1 copy.60
  (125 shorter events, 24.0 us)
Async XLA Ops:
  7.2 6.0 copy-start.12
  7.2 187.3 %all-gather.2.cloned.1.call-start = ((), (), s32[]{:S(2)}) async-start(), calls=%async_computation | async-start | bytes 5308416 | tf_op jit(solution)/shard_map/all_gather | solution.py:1783
  14.8 111.4 %copy-start.26 = (f32[24]{0:T(128)S(1)}, f32[24]{0:T(128)}, u32[]{:S(2)}) copy-start(f32[24]{0:T(128)} %param.32) | copy-start | bytes 292
  127.0 3.6 copy-start.20
  191.3 3.0 copy-start.19
  192.5 5.9 copy-start.11
  194.5 3.9 copy-start.5
  200.7 63.3 %copy-start.8 = (bf16[256,1536]{1,0:T(8,128)(2,1)S(1)}, bf16[256,1536]{1,0:T(8,128)(2,1)}, u32[]{:S(2)}) copy-start(bf16[256,1536]{1,0:T(8,128)(2,1)} %param.33) | copy-start | bytes 2359300
  262.2 1.9 copy-start.4
  334.4 2.8 copy-start.3
  334.4 2.8 copy-start.9
  433.6 95.2 %copy-start.6 = (bf16[256,1536]{1,0:T(8,128)(2,1)S(1)}, bf16[256,1536]{1,0:T(8,128)(2,1)}, u32[]{:S(2)}) copy-start(bf16[256,1536]{1,0:T(8,128)(2,1)} %x.19) | copy-start | bytes 2359300
  528.8 2.6 copy-start.7
  531.4 2.6 copy-start.23
  531.4 3.3 copy-start.25
  531.4 3.4 copy-start.22
  536.4 113.4 %copy-start.1 = (f32[256,1536]{1,0:T(8,128)S(1)}, f32[256,1536]{1,0:T(8,128)}, u32[]{:S(2)}) copy-start(f32[256,1536]{1,0:T(8,128)} %copy-done) | copy-start | bytes 4718596
  536.4 113.4 %copy-start.10 = (f32[256,1536]{1,0:T(8,128)S(1)}, f32[256,1536]{1,0:T(8,128)}, u32[]{:S(2)}) copy-start(f32[256,1536]{1,0:T(8,128)} %get-tuple-element.95) | copy-start | bytes 4718596
  647.6 3.7 copy-start.24
  647.7 18.2 %copy-start.15 = (f32[48,6144]{1,0:T(8,128)S(1)}, f32[48,6144]{1,0:T(8,128)}, u32[]{:S(2)}) copy-start(f32[48,6144]{1,0:T(8,128)} %get-tuple-element.179) | copy-start | bytes 3538948
  647.7 17.5 %collective-permute-start = (f32[8,4096]{1,0:T(8,128)}, f32[8,4096]{1,0:T(8,128)S(1)}, u32[]{:S(2)}, u32[]{:S(2)}) collective-permute-start(f32[8,4096]{1,0:T(8,128)} %get-tuple-element.106), channel_id=1, source_target_pairs={{0,0},{1,8},{2,16},{3,24},{4,1},{5,9},{6,17},{7,25},{8,2},{9,10},{... | collective-permute-start | bytes 393224 | tf_op jit(solution)/shard_map/ppermute | solution.py:1921
  651.4 15.5 %copy-start.16 = (f32[48,4608]{1,0:T(8,128)S(1)}, f32[48,4608]{1,0:T(8,128)}, u32[]{:S(2)}) copy-start(f32[48,4608]{1,0:T(8,128)} %get-tuple-element.180) | copy-start | bytes 2654212
  665.9 1.9 copy-start.14
  667.8 2.1 copy-start.13
  (5 other events, 6.7 us)
Sparse Core Ops, SparseCore 0:
  126.4 56.0 all-gather.1

commit v7 on v6

--- a/solution.py
+++ b/solution.py
@@ -459,7 +459,7 @@
     take(0).start()
     done = 0
     for _ in sums:
-        for number in range(done, min(done + 3, len(jobs))):
+        for number in range(done, 3 if done == 0 else len(jobs)):
             work(number)
             done += 1
     for number in range(done, len(jobs)):
@@ -1071,7 +1071,6 @@
             ].astype(wide)
     for copy in out_far + proj_far:
         copy.wait_recv()
-    text_step(depth - 1)
     total = out_come[0].astype(wide)
     for i in range(1, depth):
         total = total + out_come[i].astype(wide)
@@ -1083,6 +1082,7 @@
             proj_share[:, first : first + own] = proj_come[
                 source, :, i * own : (i + 1) * own
             ].astype(wide)
+    text_step(depth - 1)
     links.finish()
 
 

time: 689 us -> 685 us (level)
  no operation moved by 1% of the time
where the time goes in v7:
time: 685 us; the launch traced here: 676 us
  Pallas kernels  594 us (87%)
  other arithmetic  28.9 us (4%)
  local copies, waits for them, and re-layouts  20 us (3%)
  between operations  15.7 us (2%)
  waiting for transfers between devices  11.2 us (2%)
    pallas_call x1, Pallas kernels, start_exchange(): pl.pallas_call(partial(start_kernel, count, depth), in_specs=[scalar_spec...  111 us
    pallas_call x1, Pallas kernels, final_sums(): pl.pallas_call(partial(sum_kernel, count, depth), in_specs=[scalar_spec()...  111 us
    pallas_call x1, Pallas kernels, end_exchange(): pl.pallas_call(partial(end_kernel, count, depth), in_specs=[vmem] + [pl.B...  95.1 us
    pallas_call x1, Pallas kernels, attention_backward(): pl.pallas_call(partial(backward_kernel, count, depth, size, lanes), in_sp...  91.5 us
    pallas_call x1, Pallas kernels, ffn_backward(): pl.pallas_call(partial(ffn_back_kernel, count), in_specs=[vmem] + [anywhe...  63.6 us
    pallas_call x1, Pallas kernels, ffn_forward(): pl.pallas_call(partial(ffn_kernel, count), in_specs=[vmem] + [anywhere] *...  61.6 us
    pallas_call x1, Pallas kernels, attention_forward(): pl.pallas_call(partial(forward_kernel, count, depth, size, lanes), in_spe...  59.5 us
  transfers between devices with their start and end apart: 2, of which 1 were waited for; matrix products, arithmetic and copies ran while one was open for 2% of the time, Pallas kernels for 9%

profile of v7, /device:TPU:4, one launch (start us, length us, event | category | flops | bytes accessed | tf_op | source)
XLA Modules:
  0.0 675.6 jit_solution(7821831208449620022)
XLA Ops:
  13.2 1.6 broadcast_select_fusion
  14.8 111.4 %start_exchange.1 = (f32[8,4,192]{2,1,0:T(4,128)}, f32[4,4,1536]{2,1,0:T(4,128)}, bf16[8,192,1152]{2,1,0:T(8,128)(2,1)}, bf16[8,256,512]{2,1,0:T(8,128)(2,1)}, f...) custom-call(s32[1]{0:T(128)} %bitcast.1.clip, ...), custom_call_target="tpu_custom_call" | custom-call | tf_op jit(solution)/shard_map/start_exchange/pallas_call | solution.py:717
  131.8 59.5 %attention_forward.1 = (bf16[4,256,384]{2,1,0:T(8,128)(2,1)}, bf16[1024,384]{1,0:T(8,128)(2,1)}, bf16[1024,384]{1,0:T(8,128)(2,1)}, bf16[1024,384]{1,0:T(8,128)(...) custom-call(s32[3,4]{1,0:T(4,128)} %pad_add_fusion.3.spans, ...), custom_call_target="tpu_custom_call" | custom-call | tf_op jit(solution)/shard_map/attention_forward/pallas_call | solution.py:1376
  191.3 1.2 copy.38
  194.5 3.9 multiply_reduce_fusion.8
  199.5 1.1 multiply_convert_fusion.x
  200.7 61.6 %ffn_forward.1 = (f32[256,1536]{1,0:T(8,128)}, bf16[8,256,1536]{2,1,0:T(8,128)(2,1)}, f32[8,256,1024]{2,1,0:T(8,128)}, bf16[8,256,512]{2,1,0:T(8,128)(2,1)}) custom-call(bf16[256,1536]{1,0:T(8,128)(2,1)} %multiply_convert_fusion.x, bf16[1536,1024]{1,0:T(8,128)(2,1)} %get-tuple-element.73.gate_up_hbm, bf16[512,1536]{1,0:T(8,128)(2,1)} %down_hbm.3), custom_call_target="tpu_custom_call" | custom-call | tf_op jit(solution)/shard_map/ffn_forward/pallas_call | solution.py:368
  262.2 1.7 multiply_reduce_fusion.6
  265.2 1.9 fusion.12
  267.1 63.6 %ffn_backward.1 = (f32[256,1536]{1,0:T(8,128)}, bf16[1536,1024]{1,0:T(8,128)(2,1)}, bf16[512,1536]{1,0:T(8,128)(2,1)}) custom-call(bf16[256,1536]{1,0:T(8,128)(2,1)} %get-tuple-element.141.g, bf16[1536,1024]{1,0:T(8,128)(2,1)} %get-tuple-element.73.gate_up_hbm, bf16[512,1536]{1,0:T(8,128)(2,1)} %down_hbm.3, f32[8,256,1024]{2,1,0:T(8,128)} %get-tuple-element.75.values_in, ...), custom_call_target="tpu_custom_call" | custom-call | tf_op jit(solution)/shard_map/ffn_backward/pallas_call | solution.py:518
  330.8 2.8 multiply_reduce_fusion.1
  333.6 2.8 multiply_reduce_fusion
  336.5 1.3 fusion.13.upstream
  338.5 91.5 %attention_backward.1 = (bf16[4,256,1152]{2,1,0:T(8,128)(2,1)}, f32[2,384]{1,0:T(2,128)}, f32[3,2,256]{2,1,0:T(2,128)}, bf16[256,3072]{1,0:T(8,128)(2,1)}, f32[1...) custom-call(s32[3,4]{1,0:T(4,128)} %pad_add_fusion.3.spans, ...), custom_call_target="tpu_custom_call" | custom-call | tf_op jit(solution)/shard_map/attention_backward/pallas_call | solution.py:1639
  430.0 95.1 %end_exchange.1 = (f32[256,1536]{1,0:T(8,128)}, bf16[256,4096]{1,0:T(8,128)(2,1)}, bf16[512,3072]{1,0:T(8,128)(2,1)}, bf16[8,48,1024]{2,1,0:T(8,128)(2,1)}, bf16[128,1536]{1,0:T(8,128)(2,1)}) custom-call(bf16[256,3072]{1,0:T(8,128)(2,1)} %get-tuple-element.89.pairs, bf16[512,3072]{1,0:T(8,128)(2,1)} %text_hbm.3, ...), custom_call_target="tpu_custom_call" | custom-call | tf_op jit(solution)/shard_map/end_exchange/pallas_call | solution.py:847
  525.2 2.6 fusion.9
  527.8 2.6 convert_select_fusion
  532.7 111.3 %final_sums.1 = (f32[48,6144]{1,0:T(8,128)}, f32[128,1536]{1,0:T(8,128)}, f32[128,3072]{1,0:T(8,128)}, f32[48,1536]{1,0:T(8,128)}, f32[48,4608]{1,0:T(8,128)}, /...) custom-call(s32[4]{0:T(128)} %flags.1, ...), custom_call_target="tpu_custom_call" | custom-call | tf_op jit(solution)/shard_map/final_sums/pallas_call | solution.py:1116
  644.0 2.1 collective-permute-start
  646.1 1.6 fusion.14
  648.9 1.3 slice_reduce_fusion
  650.2 11.1 %collective-permute-done = f32[8,4096]{1,0:T(8,128)S(1)} collective-permute-done((f32[8,4096]{1,0:T(8,128)}, f32[8,4096]{1,0:T(8,128)S(1)}, u32[]{:S(2)}, u32[]{:S(2)}) %collective-permute-start) | collective-permute-done | bytes 131104 | tf_op jit(solution)/shard_map/ppermute | solution.py:1921
  663.9 1.1 copy.58
  666.0 1.1 copy.60
  (125 shorter events, 24.0 us)
Async XLA Ops:
  7.2 6.0 copy-start.12
  7.2 187.3 %all-gather.2.cloned.1.call-start = ((), (), s32[]{:S(2)}) async-start(), calls=%async_computation | async-start | bytes 5308416 | tf_op jit(solution)/shard_map/all_gather | solution.py:1783
  14.8 111.4 %copy-start.26 = (f32[24]{0:T(128)S(1)}, f32[24]{0:T(128)}, u32[]{:S(2)}) copy-start(f32[24]{0:T(128)} %param.32) | copy-start | bytes 292
  127.0 3.6 copy-start.20
  191.3 3.0 copy-start.19
  192.5 5.9 copy-start.11
  194.5 3.9 copy-start.5
  200.7 63.3 %copy-start.8 = (bf16[256,1536]{1,0:T(8,128)(2,1)S(1)}, bf16[256,1536]{1,0:T(8,128)(2,1)}, u32[]{:S(2)}) copy-start(bf16[256,1536]{1,0:T(8,128)(2,1)} %param.33) | copy-start | bytes 2359300
  262.2 1.9 copy-start.4
  330.8 2.8 copy-start.3
  330.8 2.8 copy-start.9
  430.0 95.2 %copy-start.6 = (bf16[256,1536]{1,0:T(8,128)(2,1)S(1)}, bf16[256,1536]{1,0:T(8,128)(2,1)}, u32[]{:S(2)}) copy-start(bf16[256,1536]{1,0:T(8,128)(2,1)} %x.19) | copy-start | bytes 2359300
  525.1 2.6 copy-start.7
  527.8 2.6 copy-start.23
  527.8 3.3 copy-start.25
  527.8 3.4 copy-start.22
  532.7 113.4 %copy-start.1 = (f32[256,1536]{1,0:T(8,128)S(1)}, f32[256,1536]{1,0:T(8,128)}, u32[]{:S(2)}) copy-start(f32[256,1536]{1,0:T(8,128)} %copy-done) | copy-start | bytes 4718596
  532.7 113.4 %copy-start.10 = (f32[256,1536]{1,0:T(8,128)S(1)}, f32[256,1536]{1,0:T(8,128)}, u32[]{:S(2)}) copy-start(f32[256,1536]{1,0:T(8,128)} %get-tuple-element.95) | copy-start | bytes 4718596
  644.0 3.7 copy-start.24
  644.0 17.9 %copy-start.15 = (f32[48,6144]{1,0:T(8,128)S(1)}, f32[48,6144]{1,0:T(8,128)}, u32[]{:S(2)}) copy-start(f32[48,6144]{1,0:T(8,128)} %get-tuple-element.179) | copy-start | bytes 3538948
  644.0 17.3 %collective-permute-start = (f32[8,4096]{1,0:T(8,128)}, f32[8,4096]{1,0:T(8,128)S(1)}, u32[]{:S(2)}, u32[]{:S(2)}) collective-permute-start(f32[8,4096]{1,0:T(8,128)} %get-tuple-element.106), channel_id=1, source_target_pairs={{0,0},{1,8},{2,16},{3,24},{4,1},{5,9},{6,17},{7,25},{8,2},{9,10},{... | collective-permute-start | bytes 393224 | tf_op jit(solution)/shard_map/ppermute | solution.py:1921
  647.7 15.3 %copy-start.16 = (f32[48,4608]{1,0:T(8,128)S(1)}, f32[48,4608]{1,0:T(8,128)}, u32[]{:S(2)}) copy-start(f32[48,4608]{1,0:T(8,128)} %get-tuple-element.180) | copy-start | bytes 2654212
  662.0 1.9 copy-start.14
  663.9 2.1 copy-start.13
  (5 other events, 6.7 us)
Sparse Core Ops, SparseCore 0:
  126.4 56.0 all-gather.1
